TPU v7x, 32 devices: a whole 2x2x4 slice. The times are simulated.
32 devices in a mesh: chan: 8 (over z, x), win: 4 (over y, core).
Axes of the slice: x: 2, y: 2, z: 4, core: 2. Of those that a mesh axis runs over, the one named last changes fastest.
Arguments:
- spectra: bfloat16 [64, 1024, 1024], P('win', 'chan'), may hold values from -400 to 400
- valid: int32 [64], P('win'), may hold values 0 or 1
- sources: int32 [32], replicated, may hold values from 0 to 1023, as said below
Outputs:
- correlations: bfloat16 [1024, 32, 512], P(('chan', 'win'))
Inputs may be any that keep to these rules, and one draw needn't show every extreme that they name: `sources`: each entry is a receiver channel; entries may repeat.
All inputs are finite; a program needn't handle non-finite values. No bound on the sum of `valid` on one device may be relied on, other than what follows from the above.
Results may differ from a plain program's by a relative error of at most 0.023.
Values may be sent and summed in bfloat16 or wider, within the bound.
No kernel may reach another device: no remote copies, remote signals or barrier semaphores. Data moves between devices by JAX's collectives and lax.ppermute only.
A program may use at most 128 MiB of HBM per device.

v0:
```python
import math

import jax
import jax.numpy as jnp
from jax import lax
from jax.sharding import PartitionSpec as P

LAGS = 512
SMOOTH = 21


EPSILON = 1e-06


def with_halo(block, sides, width):
    for axis, dim in sides:
        count = lax.axis_size(axis)
        forward = [(i, i + 1) for i in range(count - 1)]
        forward.append((count - 1, 0))
        backward = [(target, source) for source, target in forward]
        low = lax.ppermute(
            lax.slice_in_dim(block, block.shape[dim] - width, None, axis=dim), axis, forward
        )
        high = lax.ppermute(lax.slice_in_dim(block, 0, width, axis=dim), axis, backward)
        block = jnp.concatenate([low, block, high], axis=dim)
    return block


def cross_spectra(src_rows, received, freqs):
    src_both = jnp.concatenate([src_rows[..., :freqs], src_rows[..., freqs:]], axis=1)
    recv_real = received[..., :freqs]
    recv_imag = received[..., freqs:]
    real_rhs = jnp.concatenate([recv_real, recv_imag], axis=0)
    imag_rhs = jnp.concatenate([recv_imag, -recv_real], axis=0)
    real_part = jnp.einsum("swf,wcf->csf", src_both, real_rhs, preferred_element_type=jnp.float32)
    imag_part = jnp.einsum("swf,wcf->csf", src_both, imag_rhs, preferred_element_type=jnp.float32)
    return jnp.concatenate([real_part, imag_part], axis=-1)


def on_device(spectra, valid, sources):
    win_local, chan_local, width = spectra.shape
    freqs = width // 2
    values = spectra.astype(jnp.float32)
    magnitude = jnp.sqrt(
        values[..., :freqs] * values[..., :freqs] + values[..., freqs:] * values[..., freqs:]
    )
    positions = jnp.arange(freqs)
    band_matrix = (jnp.abs(positions[:, None] - positions[None, :]) <= SMOOTH).astype(jnp.float32)
    flat_mag = magnitude.reshape(-1, freqs)
    mag_head = flat_mag.astype(jnp.bfloat16)
    mag_rest = (flat_mag - mag_head.astype(jnp.float32)).astype(jnp.bfloat16)
    both_parts = jnp.concatenate([mag_head, mag_rest], axis=0)
    band_sums = jnp.dot(
        both_parts, band_matrix.astype(jnp.bfloat16), preferred_element_type=jnp.float32
    )
    row_count = flat_mag.shape[0]
    smoothed = (band_sums[:row_count] + band_sums[row_count:]).reshape(win_local, chan_local, freqs)
    padded = with_halo(smoothed.astype(jnp.bfloat16), (("chan", 1),), 1).astype(smoothed.dtype)
    spatial = padded[:, :-2] + padded[:, 1:-1] + padded[:, 2:]
    entries = 3.0 * jnp.sum(band_matrix, axis=0)
    divisor = spatial / entries[None, None, :] + EPSILON
    whitened = (values / jnp.concatenate([divisor, divisor], axis=-1)).astype(jnp.bfloat16)
    offset = lax.axis_index("chan") * chan_local
    source_count = sources.shape[0]
    selector = (sources[:, None] - offset == jnp.arange(chan_local)[None, :]).astype(jnp.bfloat16)
    picked = jnp.einsum("sc,wcf->swf", selector, whitened, preferred_element_type=jnp.float32)
    source_rows = lax.psum(picked, "chan").astype(jnp.bfloat16)
    masked_rows = source_rows * valid.astype(jnp.bfloat16)[None, :, None]
    stacked = lax.psum_scatter(
        cross_spectra(masked_rows, whitened, freqs).astype(jnp.bfloat16),
        "win",
        scatter_dimension=0,
        tiled=True,
    )
    freq_index = jnp.arange(freqs).astype(jnp.float32)[:, None]
    lag_shift = (jnp.arange(LAGS) - LAGS // 2).astype(jnp.float32)[None, :]
    phase_angle = math.pi * freq_index * lag_shift / freqs
    weights = jnp.where(freq_index == 0.0, 1.0, 2.0)
    lag_scale = 0.25 / math.sqrt(freqs * win_local)
    lag_table = jnp.concatenate(
        [weights * jnp.cos(phase_angle) * lag_scale, -weights * jnp.sin(phase_angle) * lag_scale],
        axis=0,
    ).astype(jnp.bfloat16)
    out_rows = stacked.shape[0]
    lagged = jnp.dot(stacked.reshape(-1, width), lag_table, preferred_element_type=jnp.float32)
    return lagged.reshape(out_rows, source_count, LAGS).astype(jnp.bfloat16)


def solution(mesh):
    return jax.shard_map(
        on_device,
        mesh=mesh,
        in_specs=(P("win", "chan", None), P("win"), P()),
        out_specs=P(("chan", "win"), None, None),
        check_vma=False,
    )
```

profile of v0, /device:TPU:0, one launch (start us, length us, event | category | flops | bytes accessed | tf_op | source)
XLA Modules:
  0.0 273.2 jit_solution(16487910897249023415)
XLA Ops:
  6.5 0.0 reduce-scatter.2.cloned.1.call-start
  6.5 3.2 %convert_element_type.68 = f32[16,128,1024]{2,1,0:T(8,128)S(1)} convert(bf16[16,128,1024]{2,1,0:T(8,128)(2,1)} %param.3) | non-fusion elementwise | flops 2097152 | bytes 12582912 | tf_op jit(solution)/shard_map/convert_element_type | solution.py:43
  9.8 1.4 fusion.5
  11.1 0.7 fusion.10
  11.8 2.3 fusion.6
  14.2 0.0 copy-start.3
  14.2 0.0 copy-start.4
  14.2 0.8 fusion.3
  15.0 0.1 fusion.24
  15.0 3.0 %collective-permute-start = (bf16[16,1,512]{2,1,0:T(2,128)(2,1)S(1)}, bf16[16,1,512]{2,1,0:T(2,128)(2,1)S(1)}, u32[]{:S(2)}, u32[]{:S(2)}) collective-permute-start(bf16[16,1,512]{2,1,0:T(2,128)(2,1)S(1)} %get-tuple-element.12), channel_id=1, source_target_pairs={{0,4},{4,8},{8,12},{12,16},{16,20},{20,24},{24,28},{28,0},{1,5},{5... | collective-permute-start | bytes 49160 | tf_op jit(solution)/shard_map/ppermute | solution.py:21
  18.0 3.1 %collective-permute-start.1 = (bf16[16,1,512]{2,1,0:T(2,128)(2,1)S(1)}, bf16[16,1,512]{2,1,0:T(2,128)(2,1)S(1)}, u32[]{:S(2)}, u32[]{:S(2)}) collective-permute-start(bf16[16,1,512]{2,1,0:T(2,128)(2,1)S(1)} %get-tuple-element.13), channel_id=1, source_target_pairs={{4,0},{8,4},{12,8},{16,12},{20,16},{24,20},{28,24},{0,28},{5,1},{9... | collective-permute-start | bytes 49160 | tf_op jit(solution)/shard_map/ppermute | solution.py:24
  21.1 0.1 convert_reduce_fusion
  21.2 0.0 copy-done.3
  21.2 0.0 copy-done.4
  21.3 1.7 collective-permute-done
  22.9 0.0 collective-permute-done.1
  22.9 0.7 maximum_convert_fusion
  23.7 0.0 copy-start
  23.7 1.1 fusion.2
  24.8 1.1 copy-done
  25.8 2.3 fusion
  28.2 2.4 fusion.23
  30.6 2.1 fusion.15
  32.6 92.1 %all-reduce.1 = bf16[32,16,1024]{2,0,1:T(8,128)(2,1)S(1)} all-reduce(f32[32,16,1024]{2,0,1:T(8,128)} %fusion.15), channel_id=1, replica_groups=mesh['chan'=8,'win'=4] {'chan'}, use_global_device_ids=true, to_apply=%region_1.0 | all-reduce | flops 524288 | bytes 3145728 | tf_op jit(solution)/shard_map/psum | solution.py:67
  124.7 0.0 copy-start.1
  124.7 0.0 copy-start.2
  124.7 0.1 convert_multiply_fusion
  124.8 0.1 fusion.25
  125.0 1.3 copy-done.1
  126.3 0.6 copy-done.2
  126.9 3.6 %pad_maximum_fusion.1 = (bf16[32,128,512]{2,1,0:T(8,128)(2,1)}, bf16[32,128,512]{2,1,0:T(8,128)(2,1)}) fusion(bf16[16,128,512]{2,1,0:T(8,128)(2,1)S(1)} %copy-done.2, bf16[16,128,512]{2,1,0:T(8,128)(2,1)S(1)} %get-tuple-element.7, bf16[16,128,512]{2,1,0:T(8,128)(2,1)S(1)} %copy-done.1), kind=kLoop, calls=%fused_computation.17 | loop fusion | flops 4194304 | bytes 14680064 | tf_op jit(solution)/shard_map/concatenate | solution.py:33
  130.5 8.0 %copy.4 = bf16[32,128,512]{1,0,2:T(8,128)(2,1)} copy(bf16[32,128,512]{2,1,0:T(8,128)(2,1)} %get-tuple-element.10) | data formatting | bytes 8388608 | tf_op jit(solution)/shard_map/concatenate | solution.py:33
  138.5 0.1 pad_maximum_fusion.3
  138.6 6.5 %copy.5 = bf16[32,32,512]{0,1,2:T(8,128)(2,1)} copy(bf16[32,32,512]{2,0,1:T(8,128)(2,1)S(1)} %pad_maximum_fusion.3) | data formatting | bytes 2097152 | tf_op jit(solution)/shard_map/concatenate | solution.py:30
  145.1 6.9 %fusion.26 = bf16[512,128,32]{1,2,0:T(8,128)(2,1)} fusion(bf16[32,128,512]{1,0,2:T(8,128)(2,1)} %copy.4, bf16[32,32,512]{0,1,2:T(8,128)(2,1)} %copy.5), kind=kOutput, calls=%fused_computation.56 | convolution fusion | flops 134217728 | bytes 9437184 | tf_op jit(solution)/shard_map/swf,wcf->csf/dot_general | solution.py:35
  152.0 8.6 %copy.6 = bf16[512,128,32]{0,2,1:T(8,128)(2,1)} copy(bf16[512,128,32]{1,2,0:T(8,128)(2,1)} %fusion.26) | data formatting | bytes 8388608 | tf_op jit(solution)/shard_map/swf,wcf->csf/dot_general | solution.py:35
  160.6 7.9 %copy.7 = bf16[32,128,512]{1,0,2:T(8,128)(2,1)} copy(bf16[32,128,512]{2,1,0:T(8,128)(2,1)} %get-tuple-element.11) | data formatting | bytes 8388608 | tf_op jit(solution)/shard_map/concatenate | solution.py:34
  168.5 6.9 %fusion.27 = bf16[512,128,32]{1,2,0:T(8,128)(2,1)} fusion(bf16[32,128,512]{1,0,2:T(8,128)(2,1)} %copy.7, bf16[32,32,512]{0,1,2:T(8,128)(2,1)} %copy.5), kind=kOutput, calls=%fused_computation.57 | convolution fusion | flops 134217728 | bytes 9437184 | tf_op jit(solution)/shard_map/swf,wcf->csf/dot_general | solution.py:36
  175.4 8.6 %copy.8 = bf16[512,128,32]{0,2,1:T(8,128)(2,1)} copy(bf16[512,128,32]{1,2,0:T(8,128)(2,1)} %fusion.27) | data formatting | bytes 8388608 | tf_op jit(solution)/shard_map/swf,wcf->csf/dot_general | solution.py:36
  184.1 8.2 %pad_maximum_fusion = bf16[128,32,1024]{2,1,0:T(8,128)(2,1)} fusion(bf16[128,32,512]{2,1,0:T(8,128)(2,1)} %bitcast.26, bf16[128,32,512]{2,1,0:T(8,128)(2,1)} %bitcast.25), kind=kLoop, calls=%fused_computation.2 | loop fusion | flops 16777216 | bytes 16777216 | tf_op jit(solution)/shard_map/concatenate | solution.py:37
  192.3 0.0 reduce-scatter.2.cloned.1.call-update
  192.3 4.5 %multiply_convert_fusion.1 = (bf16[512,512]{1,0:T(8,128)(2,1)S(1)}, bf16[512,512]{1,0:T(8,128)(2,1)S(1)}) fusion(f32[512]{0:T(512)S(1)} %add_convert_fusion, f32[512]{0:T(512)S(1)} %get-tuple-element.18, f32[512]{0:T(512)S(1)} %get-tuple-element.19, f32[512]{0:T(512)S(1)} %fusion.19), kind=kLoop, calls=%fused_computation.33 | loop fusion | flops 2097152 | bytes 1056768 | tf_op jit(solution)/shard_map/convert
  196.8 65.7 %reduce-scatter.2.cloned.1.call-done = bf16[32,32,1024]{2,1,0:T(8,128)(2,1)} async-done(((bf16[128,32,1024]{2,1,0:T(8,128)(2,1)}), bf16[32,32,1024]{2,1,0:T(8,128)(2,1)}) %reduce-scatter.2.cloned.1.call-update) | async-done | bytes 2097168 | tf_op jit(solution)/shard_map/reduce_scatter | solution.py:69
  262.5 3.8 %convolution_convert_fusion = bf16[32,32,512]{2,1,0:T(8,128)(2,1)} fusion(bf16[32,32,1024]{2,1,0:T(8,128)(2,1)} %reduce-scatter.2.cloned.1.call-done, bf16[512,512]{1,0:T(8,128)(2,1)S(1)} %get-tuple-element.17, bf16[512,512]{1,0:T(8,128)(2,1)S(1)} %get-tuple-element.16), kind=kOutput, calls=%fused_computation.25 | convolution fusion | flops 1076363264 | bytes 4194304 | tf_op jit(solution)/shard_map/dot_general | solution.py:85
  (6 shorter events, 0.0 us)
Async XLA Ops:
  6.5 256.0 %reduce-scatter.2.cloned.1.call-start = ((), (), s32[]{:S(2)}) async-start(), calls=%async_computation.1 | async-start | bytes 10485760 | tf_op jit(solution)/shard_map/reduce_scatter | solution.py:69
  14.2 7.1 %copy-start.3 = (s32[32]{0:T(128)S(1)}, s32[32]{0:T(128)}, u32[]{:S(2)}) copy-start(s32[32]{0:T(128)} %param.5) | copy-start | bytes 388
  14.2 7.1 %copy-start.4 = (s32[16]{0:T(128)S(1)}, s32[16]{0:T(128)}, u32[]{:S(2)}) copy-start(s32[16]{0:T(128)} %param.4) | copy-start | bytes 196
  15.0 7.9 %collective-permute-start = (bf16[16,1,512]{2,1,0:T(2,128)(2,1)S(1)}, bf16[16,1,512]{2,1,0:T(2,128)(2,1)S(1)}, u32[]{:S(2)}, u32[]{:S(2)}) collective-permute-start(bf16[16,1,512]{2,1,0:T(2,128)(2,1)S(1)} %get-tuple-element.12), channel_id=1, source_target_pairs={{0,4},{4,8},{8,12},{12,16},{16,20},{20,24},{24,28},{28,0},{1,5},{5... | collective-permute-start | bytes 49160 | tf_op jit(solution)/shard_map/ppermute | solution.py:21
  18.0 4.9 %collective-permute-start.1 = (bf16[16,1,512]{2,1,0:T(2,128)(2,1)S(1)}, bf16[16,1,512]{2,1,0:T(2,128)(2,1)S(1)}, u32[]{:S(2)}, u32[]{:S(2)}) collective-permute-start(bf16[16,1,512]{2,1,0:T(2,128)(2,1)S(1)} %get-tuple-element.13), channel_id=1, source_target_pairs={{4,0},{8,4},{12,8},{16,12},{20,16},{24,20},{28,24},{0,28},{5,1},{9... | collective-permute-start | bytes 49160 | tf_op jit(solution)/shard_map/ppermute | solution.py:24
  23.7 2.2 copy-start
  124.7 1.6 copy-start.1
  124.7 2.2 copy-start.2
Sparse Core Ops, SparseCore 0:
  192.4 70.0 reduce-scatter.1
where the time goes:
time: 274 us; the launch traced here: 273 us
  blocking collectives  92.1 us (34%)
  waiting for transfers between devices  67.4 us (25%)
  local copies, waits for them, and re-layouts  42.8 us (16%)
  other arithmetic  29.1 us (11%)
  matrix products  22.1 us (8%)
  between operations  13.6 us (5%)
  starting transfers between devices  6.1 us (2%)
    psum x1, blocking collectives, on_device(): source_rows = lax.psum(picked, 'chan').astype(jnp.bfloat16)  92.1 us
    reduce_scatter x1, waiting for transfers between devices, on_device(): lax.psum_scatter(cross_spectra(masked_rows, whitened, freqs).astype(jnp.b...  65.7 us
    dot_general x1, local copies, waits for them, and re-layouts, cross_spectra(): jnp.einsum('swf,wcf->csf', src_both, imag_rhs, preferred_element_type=jnp...  8.62 us
    dot_general x1, local copies, waits for them, and re-layouts, cross_spectra(): jnp.einsum('swf,wcf->csf', src_both, real_rhs, preferred_element_type=jnp...  8.6 us
    concatenate x1, other arithmetic, cross_spectra(): return jnp.concatenate([real_part, imag_part], axis=-1)  8.21 us
    concatenate x1, local copies, waits for them, and re-layouts, cross_spectra(): real_rhs = jnp.concatenate([recv_real, recv_imag], axis=0)  7.97 us
    concatenate x1, local copies, waits for them, and re-layouts, cross_spectra(): imag_rhs = jnp.concatenate([recv_imag, -recv_real], axis=0)  7.9 us
    dot_general x1, matrix products, cross_spectra(): jnp.einsum('swf,wcf->csf', src_both, real_rhs, preferred_element_type=jnp...  6.94 us
  transfers between devices with their start and end apart: 3, of which 2 were waited for; matrix products, arithmetic and copies ran while one was open for 2% of the time, Pallas kernels for 0%

commit v1 on v0

v1 whole, which is shorter than its diff:
```python
import functools
import math

import jax
import jax.numpy as jnp
from jax import lax
from jax.experimental import pallas as pl
from jax.experimental.pallas import tpu as pltpu
from jax.sharding import PartitionSpec as P

LAGS = 512
SMOOTH = 21
EPSILON = 1e-06
CHUNKS = 2
F32 = jnp.float32
BF16 = jnp.bfloat16
MIB = 1024 * 1024
LANES = 128


def xor_pairs(count, mask):
    return [(i, i ^ mask) for i in range(count)]


def place(blocks):
    if blocks != 8:
        return 0, 0
    at = lax.axis_index("chan")
    return at % 2, at // 2


def whiten_kernel(blocks, src_ref, valid_ref, spec_ref, low_ref, high_ref, white_ref, *rest):
    picks, (band, sel, held) = rest[:-3], rest[-3:]
    step = pl.program_id(0)
    chans, width = white_ref.shape[1:]
    freqs = width // 2
    sources = src_ref.shape[0]
    windows = held.shape[1] // sources

    @pl.when(step == 0)
    def _():
        row = lax.broadcasted_iota(jnp.int32, (freqs, freqs), 0)
        col = lax.broadcasted_iota(jnp.int32, (freqs, freqs), 1)
        band[...] = jnp.where(jnp.abs(row - col) <= SMOOTH, 1.0, 0.0).astype(BF16)
        x, z = place(blocks)
        offset = lax.axis_index("chan") * chans
        lane = lax.broadcasted_iota(jnp.int32, (1, chans), 1)
        per_chunk = sources // CHUNKS
        quarter = per_chunk // 8
        for r in range(sources):
            chunk, rest_r = divmod(r, per_chunk)
            half, rest_r = divmod(rest_r, 4 * quarter)
            part, i = divmod(rest_r, quarter)
            at = chunk * per_chunk + (x ^ half) * 4 * quarter + (z ^ part) * quarter + i
            sel[r : r + 1, :] = jnp.where(lane == src_ref[at] - offset, 1.0, 0.0)

    values = spec_ref[0].astype(F32)
    real, imag = values[:, :freqs], values[:, freqs:]
    magnitude = jnp.sqrt(real * real + imag * imag)

    def edge(ref):
        v = ref[0].astype(F32)
        return jnp.sqrt(v[:, :freqs] * v[:, :freqs] + v[:, freqs:] * v[:, freqs:])

    row = lax.broadcasted_iota(jnp.int32, (chans, freqs), 0)
    before = jnp.where(row == 0, edge(low_ref), pltpu.roll(magnitude, 1, 0))
    after = jnp.where(row == chans - 1, edge(high_ref), pltpu.roll(magnitude, chans - 1, 0))
    triple = (before + magnitude + after).astype(BF16)
    spatial = jnp.dot(triple, band[...], preferred_element_type=F32)
    f = lax.broadcasted_iota(jnp.int32, (1, freqs), 1)
    entries = jnp.minimum(f, SMOOTH) + jnp.minimum(freqs - 1 - f, SMOOTH) + 1
    inverse = 1.0 / (spatial * (1.0 / (3.0 * entries.astype(F32))) + EPSILON)
    white = jnp.concatenate([real * inverse, imag * inverse], axis=1).astype(BF16)
    white_ref[0] = white
    keep = (sel[...] * valid_ref[step].astype(F32)).astype(BF16)
    picked = jnp.dot(keep, white, preferred_element_type=F32)
    for j in range(width // LANES):
        held[j, pl.ds(step, sources, stride=windows), :] = picked[:, j * LANES : (j + 1) * LANES]

    @pl.when(step == windows - 1)
    def _():
        rows = picks[0].shape[0]
        for i, pick in enumerate(picks):
            for s in range(rows):
                at = (i * rows + s) * windows
                for j in range(width // LANES):
                    pick[s, :, j * LANES : (j + 1) * LANES] = held[j, at : at + windows, :].astype(BF16)


def whiten(blocks, spectra, valid, sources, low, high):
    windows, chans, width = spectra.shape
    count = sources.shape[0]
    rows = count // CHUNKS // 2
    smem = pl.BlockSpec(memory_space=pltpu.SMEM)
    edge = pl.BlockSpec((1, 1, width), lambda w: (w, 0, 0))
    block = pl.BlockSpec((1, chans, width), lambda w: (w, 0, 0))
    pick = pl.BlockSpec((rows, windows, width), lambda w: (0, 0, 0))
    return pl.pallas_call(
        functools.partial(whiten_kernel, blocks),
        grid=(windows,),
        in_specs=[smem, smem, block, edge, edge],
        out_specs=[block] + [pick] * (2 * CHUNKS),
        out_shape=[jax.ShapeDtypeStruct(spectra.shape, BF16)]
        + [jax.ShapeDtypeStruct((rows, windows, width), BF16)] * (2 * CHUNKS),
        scratch_shapes=[
            pltpu.VMEM((width // 2, width // 2), BF16),
            pltpu.VMEM((count, chans), F32),
            pltpu.VMEM((width // LANES, count * windows, LANES), F32),
        ],
        compiler_params=pltpu.CompilerParams(vmem_limit_bytes=24 * MIB),
        name="whiten",
    )(sources, valid, spectra, low, high)


def turn_kernel(real_ref, imag_ref, out_ref, held):
    windows, chans, tile = real_ref.shape
    rows = 2 * windows
    for w in range(windows):
        re = real_ref[w].astype(F32).T
        im = imag_ref[w].astype(F32).T
        held[0, pl.ds(w, tile, stride=rows), :] = re
        held[0, pl.ds(windows + w, tile, stride=rows), :] = im
        held[1, pl.ds(w, tile, stride=rows), :] = im
        held[1, pl.ds(windows + w, tile, stride=rows), :] = -re
    out_ref[:, :, :chans] = held[0].astype(BF16).reshape(tile, rows, chans)
    out_ref[:, :, chans:] = held[1].astype(BF16).reshape(tile, rows, chans)


def turn(white):
    windows, chans, width = white.shape
    freqs = width // 2
    tile = 128
    tiles = freqs // tile
    return pl.pallas_call(
        turn_kernel,
        grid=(tiles,),
        in_specs=[
            pl.BlockSpec((windows, chans, tile), lambda j: (0, 0, j)),
            pl.BlockSpec((windows, chans, tile), lambda j: (0, 0, j + tiles)),
        ],
        out_specs=pl.BlockSpec((tile, 2 * windows, 2 * chans), lambda j: (j, 0, 0)),
        out_shape=jax.ShapeDtypeStruct((freqs, 2 * windows, 2 * chans), BF16),
        scratch_shapes=[pltpu.VMEM((2, tile * 2 * windows, chans), F32)],
        compiler_params=pltpu.CompilerParams(vmem_limit_bytes=32 * MIB),
        cost_estimate=pl.CostEstimate(flops=0, bytes_accessed=24 * MIB, transcendentals=0),
        name="turn",
    )(white, white)


def cross_kernel(parts, mine_ref, theirs_ref, turned_ref, table_ref, keep_ref, send_ref, vt, st):
    half, windows, width = mine_ref.shape
    freqs, depth, both = turned_ref.shape
    chans = both // 2
    rows = 2 * half
    tile = 128
    group = tile // depth
    for g in range(rows // group):
        pieces = []
        for s in range(g * group, (g + 1) * group):
            ref = mine_ref if s < half else theirs_ref
            v = ref[s % half].astype(F32)
            pieces += [v[:, :freqs], v[:, freqs:]]
        stack = jnp.concatenate(pieces, axis=0)
        for j in range(freqs // tile):
            t = stack[:, j * tile : (j + 1) * tile].T
            for i in range(group):
                turned_here = t if i == 0 else pltpu.roll(t, tile - i * depth, 1)
                vt[pl.ds(j * tile * rows + g * group + i, tile, stride=rows), :] = turned_here

    unroll = 16

    def step(i, carry):
        for k in range(unroll):
            f = i * unroll + k
            at = pl.multiple_of(f * rows, rows)
            lhs = vt[pl.ds(at, rows), 0:depth].astype(BF16)
            sums = jnp.dot(lhs, turned_ref[f], preferred_element_type=F32)
            st[0, pl.ds(at, rows), :] = sums[:, :chans]
            st[1, pl.ds(at, rows), :] = sums[:, chans:]
        return carry

    lax.fori_loop(0, freqs // unroll, step, 0)

    me = lax.axis_index("win")
    share = chans // parts

    def lags(p, carry):
        cols = []
        for s in (2 * p, 2 * p + 1):
            parts_of_s = [st[i, pl.ds(s, freqs, stride=rows), :].astype(BF16) for i in (0, 1)]
            cols.append(jnp.concatenate(parts_of_s, axis=0))
        out = jnp.dot(table_ref[...], jnp.concatenate(cols, axis=1), preferred_element_type=F32)
        for k in range(2):
            flat = out[:, k * chans : (k + 1) * chans].T.astype(BF16)
            for b in range(parts):
                slot = b ^ me
                value = flat[b * share : (b + 1) * share, :]

                @pl.when(slot % 2 == 0)
                def _():
                    keep_ref[slot // 2, 2 * p + k] = value

                @pl.when(slot % 2 == 1)
                def _():
                    send_ref[slot // 2, 2 * p + k] = value

        return carry

    lax.fori_loop(0, rows // 2, lags, 0)


def cross(parts, mine, theirs, turned, table):
    half, windows, width = mine.shape
    freqs, depth, both = turned.shape
    rows = 2 * half
    chans = both // 2
    lags = table.shape[0]
    shape = jax.ShapeDtypeStruct((parts // 2, rows, chans // parts, lags), BF16)
    whole = pl.BlockSpec(memory_space=pltpu.VMEM)
    return pl.pallas_call(
        functools.partial(cross_kernel, parts),
        in_specs=[whole] * 4,
        out_specs=[whole] * 2,
        out_shape=[shape] * 2,
        scratch_shapes=[
            pltpu.VMEM((freqs * rows, 128), F32),
            pltpu.VMEM((2, freqs * rows, chans), F32),
        ],
        compiler_params=pltpu.CompilerParams(vmem_limit_bytes=48 * MIB),
        cost_estimate=pl.CostEstimate(flops=8 * 10**9, bytes_accessed=16 * MIB, transcendentals=0),
        name="cross",
    )(mine, theirs, turned, table)


def finish_kernel(blocks, *refs):
    ins, (out_ref, held) = refs[:-2], refs[-2:]
    chans, sources, lags = out_ref.shape
    x, z = place(blocks)
    per_chunk = sources // CHUNKS
    quarter = per_chunk // 8
    for chunk in range(CHUNKS):
        own, came = ins[2 * chunk], ins[2 * chunk + 1]
        for r in range(per_chunk):
            half, rest_r = divmod(r, 4 * quarter)
            part, i = divmod(rest_r, quarter)
            at = chunk * per_chunk + (x ^ half) * 4 * quarter + (z ^ part) * quarter + i
            total = own[0, r].astype(F32) + came[0, r].astype(F32)
            for j in range(lags // LANES):
                held[j, pl.ds(at, chans, stride=sources), :] = total[:, j * LANES : (j + 1) * LANES]
    for c in range(chans):
        for j in range(lags // LANES):
            rows = held[j, c * sources : (c + 1) * sources, :]
            out_ref[c, :, j * LANES : (j + 1) * LANES] = rows.astype(BF16)


def finish(blocks, ins, sources):
    _, _, chans, lags = ins[0].shape
    whole = pl.BlockSpec(memory_space=pltpu.VMEM)
    return pl.pallas_call(
        functools.partial(finish_kernel, blocks),
        in_specs=[whole] * len(ins),
        out_specs=whole,
        out_shape=jax.ShapeDtypeStruct((chans, sources, lags), BF16),
        scratch_shapes=[pltpu.VMEM((lags // LANES, chans * sources, LANES), F32)],
        compiler_params=pltpu.CompilerParams(vmem_limit_bytes=24 * MIB),
        name="finish",
    )(*ins)


def spread(blocks, keep, send):
    if blocks != 8:
        return lax.psum(keep, "chan"), lax.psum(send, "chan")
    quarter = keep.shape[0] // 4
    across = xor_pairs(8, 1)
    total = keep + lax.ppermute(send, "chan", across)
    pieces = [total[p * quarter : (p + 1) * quarter] for p in range(4)]
    own = pieces[0]
    came = [lax.ppermute(pieces[p], "chan", xor_pairs(8, 2 * p)) for p in (1, 2, 3)]
    own = own + came[0] + came[1] + came[2]
    others = [lax.ppermute(own, "chan", xor_pairs(8, 2 * p)) for p in (1, 2, 3)]
    mine = jnp.concatenate([own] + others, axis=0)
    return mine, lax.ppermute(mine, "chan", across)


def lag_table(freqs, windows):
    freq_index = jnp.arange(freqs).astype(F32)[None, :]
    lag_shift = (jnp.arange(LAGS) - LAGS // 2).astype(F32)[:, None]
    phase_angle = math.pi * freq_index * lag_shift / freqs
    weights = jnp.where(freq_index == 0.0, 1.0, 2.0)
    lag_scale = 0.25 / math.sqrt(freqs * windows)
    return jnp.concatenate(
        [weights * jnp.cos(phase_angle) * lag_scale, -weights * jnp.sin(phase_angle) * lag_scale], axis=1
    ).astype(BF16)


def on_device(blocks, parts, spectra, valid, sources):
    windows, chans, width = spectra.shape
    freqs = width // 2
    forward = [(i, (i + 1) % blocks) for i in range(blocks)]
    backward = [(b, a) for a, b in forward]
    low = lax.ppermute(spectra[:, chans - 1 :, :], "chan", forward)
    high = lax.ppermute(spectra[:, :1, :], "chan", backward)
    white, *picks = whiten(blocks, spectra, valid, sources, low, high)
    table = lag_table(freqs, windows)
    turned = turn(white)
    ins = []
    for chunk in range(CHUNKS):
        mine, theirs = spread(blocks, picks[2 * chunk], picks[2 * chunk + 1])
        keep, send = cross(parts, mine, theirs, turned, table)
        total = keep + lax.ppermute(send, "win", xor_pairs(parts, 1))
        ins += [total[:1], lax.ppermute(total[1:], "win", xor_pairs(parts, 2))]
    return finish(blocks, ins, sources.shape[0])


def solution(mesh):
    return jax.shard_map(
        functools.partial(on_device, mesh.shape["chan"], mesh.shape["win"]),
        mesh=mesh,
        in_specs=(P("win", "chan", None), P("win"), P()),
        out_specs=P(("chan", "win"), None, None),
        check_vma=False,
    )
```

time: 274 us -> 144 us (0.53)
  blocking collectives: 92.1 us -> 0 us
  Pallas kernels: 0 us -> 61.2 us
  local copies, waits for them, and re-layouts: 42.8 us -> 8.06 us
  waiting for transfers between devices: 67.4 us -> 35 us
  starting transfers between devices: 6.1 us -> 33.7 us
  other arithmetic: 29.1 us -> 5.47 us
  matrix products: 22.1 us -> 0 us
  between operations: 13.6 us -> 0.21 us
    psum x1 -> x0, blocking collectives: 92.1 us -> none  [on_device(): source_rows = lax.psum(picked, 'chan').astype(jnp.bfloat16)]
    reduce_scatter x1 -> x0, waiting for transfers between devices: 65.7 us -> none  [on_device(): lax.psum_scatter(cross_spectra(masked_rows, whitened, freqs).astype(jnp.b...]
    pallas_call x0 -> x5, Pallas kernels: none -> 61.2 us  [the longest x2 34.2 us: cross(): pl.pallas_call(functools.partial(cross_kernel, parts), in_specs=[whole] *...]
    ppermute x2 -> x22, waiting for transfers between devices: 1.67 us -> 35 us  [the longest x2 21.3 us: on_device(): ins += [total[:1], lax.ppermute(total[1:], 'win', xor_pairs(parts, 2))]]
    ppermute x2 -> x22, starting transfers between devices: 6.09 us -> 33.7 us  [the longest x6 8.9 us: spread(): lax.ppermute(pieces[p], 'chan', xor_pairs(8, 2 * p))]
    concatenate x3 -> x0, local copies, waits for them, and re-layouts: 22.4 us -> none  [the longest x1 7.97 us: cross_spectra(): real_rhs = jnp.concatenate([recv_real, recv_imag], axis=0)]
    dot_general x5 -> x0, matrix products: 22.1 us -> none  [the longest x1 6.94 us: cross_spectra(): jnp.einsum('swf,wcf->csf', src_both, real_rhs, preferred_element_type=jnp...]
    dot_general x2 -> x0, local copies, waits for them, and re-layouts: 17.2 us -> none  [the longest x1 8.62 us: cross_spectra(): jnp.einsum('swf,wcf->csf', src_both, imag_rhs, preferred_element_type=jnp...]
  transfers between devices with their start and end apart: 3 -> 22, of which waited for: 2 -> 8; matrix products, arithmetic and copies ran while one was open for 2% -> 4% of each run, Pallas kernels for 0% -> 34%
where the time goes in v1:
time: 144 us
  Pallas kernels  61.2 us (42%)
  waiting for transfers between devices  35 us (24%)
  starting transfers between devices  33.7 us (23%)
  local copies, waits for them, and re-layouts  8.06 us (6%)
  other arithmetic  5.47 us (4%)
    pallas_call x2, Pallas kernels, cross(): pl.pallas_call(functools.partial(cross_kernel, parts), in_specs=[whole] *...  34.2 us
    ppermute x2, waiting for transfers between devices, on_device(): ins += [total[:1], lax.ppermute(total[1:], 'win', xor_pairs(parts, 2))]  21.3 us
    pallas_call x1, Pallas kernels, turn(): pl.pallas_call(turn_kernel, grid=(tiles,), in_specs=[pl.BlockSpec((window...  14.4 us
    pallas_call x1, Pallas kernels, whiten(): pl.pallas_call(functools.partial(whiten_kernel, blocks), grid=(windows,),...  9.3 us
    ppermute x6, starting transfers between devices, spread(): lax.ppermute(pieces[p], 'chan', xor_pairs(8, 2 * p))  8.9 us
    ppermute x6, starting transfers between devices, spread(): others = [lax.ppermute(own, 'chan', xor_pairs(8, 2 * p)) for p in (1, 2, 3)]  8.9 us
    ppermute x2, waiting for transfers between devices, spread(): total = keep + lax.ppermute(send, 'chan', across)  7.14 us
    unnamed x8, local copies, waits for them, and re-layouts  6.76 us
  transfers between devices with their start and end apart: 22, of which 8 were waited for; matrix products, arithmetic and copies ran while one was open for 4% of the time, Pallas kernels for 34%

profile of v1, /device:TPU:0, one launch (start us, length us, event | category | flops | bytes accessed | tf_op | source)
XLA Modules:
  0.0 143.6 jit_solution(16595016005563703753)
XLA Ops:
  0.0 1.1 fusion.6
  1.1 3.0 %collective-permute-start = (bf16[16,1,1024]{2,1,0:T(2,128)(2,1)S(1)}, bf16[16,1,1024]{2,1,0:T(2,128)(2,1)S(1)}, u32[]{:S(2)}, u32[]{:S(2)}) collective-permute-start(bf16[16,1,1024]{2,1,0:T(2,128)(2,1)S(1)} %get-tuple-element.24), channel_id=1, source_target_pairs={{0,4},{4,8},{8,12},{12,16},{16,20},{20,24},{24,28},{28,0},{1,5},{5... | collective-permute-start | bytes 98312 | tf_op jit(solution)/shard_map/ppermute | solution.py:301
  4.1 3.1 %collective-permute-start.1 = (bf16[16,1,1024]{2,1,0:T(2,128)(2,1)S(1)}, bf16[16,1,1024]{2,1,0:T(2,128)(2,1)S(1)}, u32[]{:S(2)}, u32[]{:S(2)}) collective-permute-start(bf16[16,1,1024]{2,1,0:T(2,128)(2,1)S(1)} %get-tuple-element.23), channel_id=1, source_target_pairs={{4,0},{8,4},{12,8},{16,12},{20,16},{24,20},{28,24},{0,28},{5,1},{9... | collective-permute-start | bytes 98312 | tf_op jit(solution)/shard_map/ppermute | solution.py:302
  7.2 2.2 %collective-permute-done.low_ref = bf16[16,1,1024]{2,1,0:T(2,128)(2,1)S(1)} collective-permute-done((bf16[16,1,1024]{2,1,0:T(2,128)(2,1)S(1)}, bf16[16,1,1024]{2,1,0:T(2,128)(2,1)S(1)}, u32[]{:S(2)}, u32[]{:S(2)}) %collective-permute-start) | collective-permute-done | bytes 32800 | tf_op jit(solution)/shard_map/ppermute | solution.py:301
  9.5 0.3 collective-permute-done.1.high_ref
  9.8 0.0 copy-start.1
  9.8 2.2 %copy-done.1 = bf16[16,128,1024]{2,1,0:T(8,128)(2,1)S(1)} copy-done((bf16[16,128,1024]{2,1,0:T(8,128)(2,1)S(1)}, bf16[16,128,1024]{2,1,0:T(8,128)(2,1)}, u32[]{:S(2)}) %copy-start.1) | copy-done | bytes 4194328
  12.0 0.7 copy-done.2
  12.6 0.7 copy-done.3
  13.3 9.3 %whiten.1 = (bf16[16,128,1024]{2,1,0:T(8,128)(2,1)S(1)}, bf16[8,16,1024]{2,1,0:T(8,128)(2,1)S(1)}, bf16[8,16,1024]{2,1,0:T(8,128)(2,1)S(1)}, bf16[8,16,1024]{2,1,0:T(8,128)(2,1)S(1)}, bf16[8,16,1024]{2,1,0:T(8,128)(2,1)S(1)}) custom-call(s32[32]{0:T(128)S(1)} %copy-done.2, s32[16]{0:T(128)S(1)} %copy-done.3, bf16[16,128,1024]{2,1,0:T(8,128)(2,1)S(1)} %copy-done.1, ...), custom_call_target="tpu_custom_call" | custom-call | tf_op jit(solution)/shard_map/whiten/pallas_call | solution.py:98
  22.6 1.1 collective-permute-start.12
  23.7 1.0 collective-permute-start.2
  24.8 7.1 %collective-permute-done.12 = bf16[8,16,1024]{2,1,0:T(8,128)(2,1)S(1)} collective-permute-done((bf16[8,16,1024]{2,1,0:T(8,128)(2,1)S(1)}, bf16[8,16,1024]{2,1,0:T(8,128)(2,1)S(1)}, u32[]{:S(2)}, u32[]{:S(2)}) %collective-permute-start.12) | collective-permute-done | bytes 262176 | tf_op jit(solution)/shard_map/ppermute | solution.py:275
  31.9 0.1 add.40
  32.0 0.7 collective-permute-start.13
  32.7 2.9 %collective-permute-start.14 = (bf16[2,16,1024]{2,1,0:T(8,128)(2,1)S(1)}, bf16[2,16,1024]{2,1,0:T(8,128)(2,1)S(1)}, u32[]{:S(2)}, u32[]{:S(2)}) collective-permute-start(bf16[2,16,1024]{2,1,0:T(8,128)(2,1)S(1)} %get-tuple-element.31), channel_id=1, source_target_pairs={{0,16},{4,20},{8,24},{12,28},{16,0},{20,4},{24,8},{28,12},{1,17},{... | collective-permute-start | bytes 196616 | tf_op jit(solution)/shard_map/ppermute | solution.py:278
  35.6 0.9 collective-permute-start.15
  36.5 4.3 %multiply_convert_fusion.1 = (bf16[512,512]{1,0:T(8,128)(2,1)S(1)}, bf16[512,512]{1,0:T(8,128)(2,1)S(1)}) fusion(f32[512]{0:T(512)S(1)} %add_convert_fusion, f32[512]{0:T(512)S(1)} %get-tuple-element.37, f32[512]{0:T(512)S(1)} %get-tuple-element.38, f32[512]{0:T(512)S(1)} %fusion.5), kind=kLoop, calls=%fused_computation.2 | loop fusion | flops 2097152 | bytes 1056768 | tf_op jit(solution)/shard_map/convert
  40.8 0.0 collective-permute-done.2
  40.8 0.1 add.35
  40.9 0.0 collective-permute-done.13
  40.9 0.0 collective-permute-done.14
  40.9 1.4 collective-permute-done.15
  42.3 0.1 collective-permute-start.16
  42.4 2.1 %collective-permute-start.17 = (bf16[2,16,1024]{2,1,0:T(8,128)(2,1)S(1)}, bf16[2,16,1024]{2,1,0:T(8,128)(2,1)S(1)}, u32[]{:S(2)}, u32[]{:S(2)}) collective-permute-start(bf16[2,16,1024]{2,1,0:T(8,128)(2,1)S(1)} %fusion.1), channel_id=1, source_target_pairs={{0,16},{4,20},{8,24},{12,28},{16,0},{20,4},{24,8},{28,12},{1,17},{... | collective-permute-start | bytes 196616 | tf_op jit(solution)/shard_map/ppermute | solution.py:280
  44.5 2.3 %collective-permute-start.18 = (bf16[2,16,1024]{2,1,0:T(8,128)(2,1)S(1)}, bf16[2,16,1024]{2,1,0:T(8,128)(2,1)S(1)}, u32[]{:S(2)}, u32[]{:S(2)}) collective-permute-start(bf16[2,16,1024]{2,1,0:T(8,128)(2,1)S(1)} %fusion.1), channel_id=1, source_target_pairs={{0,24},{4,28},{8,16},{12,20},{16,8},{20,12},{24,0},{28,4},{1,25},{... | collective-permute-start | bytes 196616 | tf_op jit(solution)/shard_map/ppermute | solution.py:280
  46.8 0.1 collective-permute-start.3
  46.9 2.1 %collective-permute-start.4 = (bf16[2,16,1024]{2,1,0:T(8,128)(2,1)S(1)}, bf16[2,16,1024]{2,1,0:T(8,128)(2,1)S(1)}, u32[]{:S(2)}, u32[]{:S(2)}) collective-permute-start(bf16[2,16,1024]{2,1,0:T(8,128)(2,1)S(1)} %get-tuple-element.34), channel_id=1, source_target_pairs={{0,16},{4,20},{8,24},{12,28},{16,0},{20,4},{24,8},{28,12},{1,17},{... | collective-permute-start | bytes 196616 | tf_op jit(solution)/shard_map/ppermute | solution.py:278
  49.0 0.0 collective-permute-done.16
  49.0 2.3 %collective-permute-start.5 = (bf16[2,16,1024]{2,1,0:T(8,128)(2,1)S(1)}, bf16[2,16,1024]{2,1,0:T(8,128)(2,1)S(1)}, u32[]{:S(2)}, u32[]{:S(2)}) collective-permute-start(bf16[2,16,1024]{2,1,0:T(8,128)(2,1)S(1)} %get-tuple-element.33), channel_id=1, source_target_pairs={{0,24},{4,28},{8,16},{12,20},{16,8},{20,12},{24,0},{28,4},{1,25},{... | collective-permute-start | bytes 196616 | tf_op jit(solution)/shard_map/ppermute | solution.py:278
  51.2 0.0 collective-permute-done.17
  51.2 0.0 collective-permute-done.18
  51.3 2.1 %collective-permute-start.19 = (bf16[8,16,1024]{2,1,0:T(8,128)(2,1)S(1)}, bf16[8,16,1024]{2,1,0:T(8,128)(2,1)S(1)}, u32[]{:S(2)}, u32[]{:S(2)}) collective-permute-start(bf16[8,16,1024]{2,1,0:T(8,128)(2,1)S(1)} %pad_maximum_fusion.2.mine_ref), channel_id=1, source_target_pairs={{0,4},{4,0},{8,12},{12,8},{16,20},{20,16},{24,28},{28,24},{1,5},{5... | collective-permute-start | bytes 786440 | tf_op jit(solution)/shard_map/ppermute | solution.py:282
  53.4 0.0 collective-permute-done.3
  53.4 0.0 collective-permute-done.4
  53.4 2.3 %collective-permute-done.5 = bf16[2,16,1024]{2,1,0:T(8,128)(2,1)S(1)} collective-permute-done((bf16[2,16,1024]{2,1,0:T(8,128)(2,1)S(1)}, bf16[2,16,1024]{2,1,0:T(8,128)(2,1)S(1)}, u32[]{:S(2)}, u32[]{:S(2)}) %collective-permute-start.5) | collective-permute-done | bytes 65568 | tf_op jit(solution)/shard_map/ppermute | solution.py:278
  55.7 1.6 %collective-permute-start.6 = (bf16[2,16,1024]{2,1,0:T(8,128)(2,1)S(1)}, bf16[2,16,1024]{2,1,0:T(8,128)(2,1)S(1)}, u32[]{:S(2)}, u32[]{:S(2)}) collective-permute-start(bf16[2,16,1024]{2,1,0:T(8,128)(2,1)S(1)} %fusion.3), channel_id=1, source_target_pairs={{0,8},{4,12},{8,0},{12,4},{16,24},{20,28},{24,16},{28,20},{1,9},{5... | collective-permute-start | bytes 196616 | tf_op jit(solution)/shard_map/ppermute | solution.py:280
  57.3 1.4 collective-permute-start.7
  58.7 1.5 %collective-permute-start.8 = (bf16[2,16,1024]{2,1,0:T(8,128)(2,1)S(1)}, bf16[2,16,1024]{2,1,0:T(8,128)(2,1)S(1)}, u32[]{:S(2)}, u32[]{:S(2)}) collective-permute-start(bf16[2,16,1024]{2,1,0:T(8,128)(2,1)S(1)} %fusion.3), channel_id=1, source_target_pairs={{0,24},{4,28},{8,16},{12,20},{16,8},{20,12},{24,0},{28,4},{1,25},{... | collective-permute-start | bytes 196616 | tf_op jit(solution)/shard_map/ppermute | solution.py:280
  60.1 0.1 pad_maximum_fusion.table_ref
  60.3 14.4 %turn.1.turned_ref = bf16[512,32,256]{2,1,0:T(8,128)(2,1)S(1)} custom-call(bf16[16,128,1024]{2,1,0:T(8,128)(2,1)S(1)} %get-tuple-element.16.real_ref.imag_ref, bf16[16,128,1024]{2,1,0:T(8,128)(2,1)S(1)} %get-tuple-element.16.real_ref.imag_ref), custom_call_target="tpu_custom_call" | custom-call | bytes 25165824 | tf_op jit(solution)/shard_map/turn/pallas_call | solution.py:134
  74.7 0.0 copy-start
  74.7 3.3 %copy-done = bf16[512,32,256]{2,1,0:T(8,128)(2,1)} copy-done((bf16[512,32,256]{2,1,0:T(8,128)(2,1)}, bf16[512,32,256]{2,1,0:T(8,128)(2,1)S(1)}, u32[]{:S(2)}) %copy-start) | copy-done | bytes 8388632
  78.0 0.0 collective-permute-done.6
  78.0 0.0 collective-permute-done.7
  78.0 0.0 collective-permute-done.8
  78.0 1.7 %collective-permute-start.9 = (bf16[8,16,1024]{2,1,0:T(8,128)(2,1)S(1)}, bf16[8,16,1024]{2,1,0:T(8,128)(2,1)S(1)}, u32[]{:S(2)}, u32[]{:S(2)}) collective-permute-start(bf16[8,16,1024]{2,1,0:T(8,128)(2,1)S(1)} %pad_maximum_fusion.1.mine_ref), channel_id=1, source_target_pairs={{0,4},{4,0},{8,12},{12,8},{16,20},{20,16},{24,28},{28,24},{1,5},{5... | collective-permute-start | bytes 786440 | tf_op jit(solution)/shard_map/ppermute | solution.py:282
  79.8 0.0 collective-permute-done.19.theirs_ref
  79.8 17.0 %cross.3 = (bf16[2,16,32,512]{3,2,1,0:T(8,128)(2,1)S(1)}, bf16[2,16,32,512]{3,2,1,0:T(8,128)(2,1)S(1)}) custom-call(bf16[8,16,1024]{2,1,0:T(8,128)(2,1)S(1)} %pad_maximum_fusion.2.mine_ref, bf16[8,16,1024]{2,1,0:T(8,128)(2,1)S(1)} %collective-permute-done.19.theirs_ref, bf16[512,32,256]{2,1,0:T(8,128)(2,1)} %copy-done, ...), custom_call_target="tpu_custom_call" | custom-call | flops 8000000000 | bytes 16777216 | tf_op jit(solution)/shard_map/cross/pallas_call | solution.py:220
  96.8 0.1 collective-permute-start.20
  96.9 0.0 collective-permute-done.9.theirs_ref
  96.9 17.2 %cross.2 = (bf16[2,16,32,512]{3,2,1,0:T(8,128)(2,1)S(1)}, bf16[2,16,32,512]{3,2,1,0:T(8,128)(2,1)S(1)}) custom-call(bf16[8,16,1024]{2,1,0:T(8,128)(2,1)S(1)} %pad_maximum_fusion.1.mine_ref, bf16[8,16,1024]{2,1,0:T(8,128)(2,1)S(1)} %collective-permute-done.9.theirs_ref, bf16[512,32,256]{2,1,0:T(8,128)(2,1)} %copy-done, ...), custom_call_target="tpu_custom_call" | custom-call | flops 8000000000 | bytes 16777216 | tf_op jit(solution)/shard_map/cross/pallas_call | solution.py:220
  114.1 0.6 collective-permute-start.10
  114.6 0.0 collective-permute-done.20
  114.7 0.4 add.44
  115.0 0.1 fusion.7
  115.1 1.5 %collective-permute-start.21 = (bf16[1,16,32,512]{3,2,1,0:T(8,128)(2,1)S(1)}, bf16[1,16,32,512]{3,2,1,0:T(8,128)(2,1)S(1)}, u32[]{:S(2)}, u32[]{:S(2)}) collective-permute-start(bf16[1,16,32,512]{3,2,1,0:T(8,128)(2,1)S(1)} %get-tuple-element.25), channel_id=1, source_target_pairs={{0,2},{1,3},{2,0},{3,1},{4,6},{5,7},{6,4},{7,5},{8,10},{9,11},{10,... | collective-permute-start | bytes 1572872 | tf_op jit(solution)/shard_map/ppermute | solution.py:311
  116.7 0.3 collective-permute-done.10
  116.9 0.4 add.39
  117.3 0.1 fusion.8
  117.4 1.6 %collective-permute-start.11 = (bf16[1,16,32,512]{3,2,1,0:T(8,128)(2,1)S(1)}, bf16[1,16,32,512]{3,2,1,0:T(8,128)(2,1)S(1)}, u32[]{:S(2)}, u32[]{:S(2)}) collective-permute-start(bf16[1,16,32,512]{3,2,1,0:T(8,128)(2,1)S(1)} %get-tuple-element.27), channel_id=1, source_target_pairs={{0,2},{1,3},{2,0},{3,1},{4,6},{5,7},{6,4},{7,5},{8,10},{9,11},{10,... | collective-permute-start | bytes 1572872 | tf_op jit(solution)/shard_map/ppermute | solution.py:311
  119.0 11.0 %collective-permute-done.21.refs_3_ = bf16[1,16,32,512]{3,2,1,0:T(8,128)(2,1)S(1)} collective-permute-done((bf16[1,16,32,512]{3,2,1,0:T(8,128)(2,1)S(1)}, bf16[1,16,32,512]{3,2,1,0:T(8,128)(2,1)S(1)}, u32[]{:S(2)}, u32[]{:S(2)}) %collective-permute-start.21) | collective-permute-done | bytes 524320 | tf_op jit(solution)/shard_map/ppermute | solution.py:311
  130.0 10.3 %collective-permute-done.11.refs_1_ = bf16[1,16,32,512]{3,2,1,0:T(8,128)(2,1)S(1)} collective-permute-done((bf16[1,16,32,512]{3,2,1,0:T(8,128)(2,1)S(1)}, bf16[1,16,32,512]{3,2,1,0:T(8,128)(2,1)S(1)}, u32[]{:S(2)}, u32[]{:S(2)}) %collective-permute-start.11) | collective-permute-done | bytes 524320 | tf_op jit(solution)/shard_map/ppermute | solution.py:311
  140.3 3.3 %finish.1 = bf16[32,32,512]{2,1,0:T(8,128)(2,1)} custom-call(bf16[1,16,32,512]{3,2,1,0:T(8,128)(2,1)S(1)} %get-tuple-element.28.refs_0_, bf16[1,16,32,512]{3,2,1,0:T(8,128)(2,1)S(1)} %collective-permute-done.11.refs_1_, bf16[1,16,32,512]{3,2,1,0:T(8,128)(2,1)S(1)} %get-tuple-element.26.refs_2_, bf16[1,16,32,512]{3,2,1,0:T(8,128)(2,1)S(1)} %collective-permute-done.21.refs_3_), custom_call_target="tpu_custom_call" | custom-call | tf_op jit(solution)/shard_map/finish/pallas_call | solution.py:259
  (11 shorter events, 0.2 us)
Async XLA Ops:
  1.1 8.3 %collective-permute-start = (bf16[16,1,1024]{2,1,0:T(2,128)(2,1)S(1)}, bf16[16,1,1024]{2,1,0:T(2,128)(2,1)S(1)}, u32[]{:S(2)}, u32[]{:S(2)}) collective-permute-start(bf16[16,1,1024]{2,1,0:T(2,128)(2,1)S(1)} %get-tuple-element.24), channel_id=1, source_target_pairs={{0,4},{4,8},{8,12},{12,16},{16,20},{20,24},{24,28},{28,0},{1,5},{5... | collective-permute-start | bytes 98312 | tf_op jit(solution)/shard_map/ppermute | solution.py:301
  4.1 5.7 %collective-permute-start.1 = (bf16[16,1,1024]{2,1,0:T(2,128)(2,1)S(1)}, bf16[16,1,1024]{2,1,0:T(2,128)(2,1)S(1)}, u32[]{:S(2)}, u32[]{:S(2)}) collective-permute-start(bf16[16,1,1024]{2,1,0:T(2,128)(2,1)S(1)} %get-tuple-element.23), channel_id=1, source_target_pairs={{4,0},{8,4},{12,8},{16,12},{20,16},{24,20},{28,24},{0,28},{5,1},{9... | collective-permute-start | bytes 98312 | tf_op jit(solution)/shard_map/ppermute | solution.py:302
  9.8 2.2 %copy-start.1 = (bf16[16,128,1024]{2,1,0:T(8,128)(2,1)S(1)}, bf16[16,128,1024]{2,1,0:T(8,128)(2,1)}, u32[]{:S(2)}) copy-start(bf16[16,128,1024]{2,1,0:T(8,128)(2,1)} %spec_ref.1) | copy-start | bytes 12582916
  12.0 0.7 copy-start.2
  12.6 0.7 copy-start.3
  22.6 9.3 %collective-permute-start.12 = (bf16[8,16,1024]{2,1,0:T(8,128)(2,1)S(1)}, bf16[8,16,1024]{2,1,0:T(8,128)(2,1)S(1)}, u32[]{:S(2)}, u32[]{:S(2)}) collective-permute-start(bf16[8,16,1024]{2,1,0:T(8,128)(2,1)S(1)} %get-tuple-element.20), channel_id=1, source_target_pairs={{0,4},{4,0},{8,12},{12,8},{16,20},{20,16},{24,28},{28,24},{1,5},{5... | collective-permute-start | bytes 786440 | tf_op jit(solution)/shard_map/ppermute | solution.py:275
  23.7 17.1 %collective-permute-start.2 = (bf16[8,16,1024]{2,1,0:T(8,128)(2,1)S(1)}, bf16[8,16,1024]{2,1,0:T(8,128)(2,1)S(1)}, u32[]{:S(2)}, u32[]{:S(2)}) collective-permute-start(bf16[8,16,1024]{2,1,0:T(8,128)(2,1)S(1)} %get-tuple-element.15), channel_id=1, source_target_pairs={{0,4},{4,0},{8,12},{12,8},{16,20},{20,16},{24,28},{28,24},{1,5},{5... | collective-permute-start | bytes 786440 | tf_op jit(solution)/shard_map/ppermute | solution.py:275
  32.0 8.9 %collective-permute-start.13 = (bf16[2,16,1024]{2,1,0:T(8,128)(2,1)S(1)}, bf16[2,16,1024]{2,1,0:T(8,128)(2,1)S(1)}, u32[]{:S(2)}, u32[]{:S(2)}) collective-permute-start(bf16[2,16,1024]{2,1,0:T(8,128)(2,1)S(1)} %get-tuple-element.29), channel_id=1, source_target_pairs={{0,8},{4,12},{8,0},{12,4},{16,24},{20,28},{24,16},{28,20},{1,9},{5... | collective-permute-start | bytes 196616 | tf_op jit(solution)/shard_map/ppermute | solution.py:278
  32.7 8.2 %collective-permute-start.14 = (bf16[2,16,1024]{2,1,0:T(8,128)(2,1)S(1)}, bf16[2,16,1024]{2,1,0:T(8,128)(2,1)S(1)}, u32[]{:S(2)}, u32[]{:S(2)}) collective-permute-start(bf16[2,16,1024]{2,1,0:T(8,128)(2,1)S(1)} %get-tuple-element.31), channel_id=1, source_target_pairs={{0,16},{4,20},{8,24},{12,28},{16,0},{20,4},{24,8},{28,12},{1,17},{... | collective-permute-start | bytes 196616 | tf_op jit(solution)/shard_map/ppermute | solution.py:278
  35.6 6.7 %collective-permute-start.15 = (bf16[2,16,1024]{2,1,0:T(8,128)(2,1)S(1)}, bf16[2,16,1024]{2,1,0:T(8,128)(2,1)S(1)}, u32[]{:S(2)}, u32[]{:S(2)}) collective-permute-start(bf16[2,16,1024]{2,1,0:T(8,128)(2,1)S(1)} %get-tuple-element.30), channel_id=1, source_target_pairs={{0,24},{4,28},{8,16},{12,20},{16,8},{20,12},{24,0},{28,4},{1,25},{... | collective-permute-start | bytes 196616 | tf_op jit(solution)/shard_map/ppermute | solution.py:278
  42.3 6.7 %collective-permute-start.16 = (bf16[2,16,1024]{2,1,0:T(8,128)(2,1)S(1)}, bf16[2,16,1024]{2,1,0:T(8,128)(2,1)S(1)}, u32[]{:S(2)}, u32[]{:S(2)}) collective-permute-start(bf16[2,16,1024]{2,1,0:T(8,128)(2,1)S(1)} %fusion.1), channel_id=1, source_target_pairs={{0,8},{4,12},{8,0},{12,4},{16,24},{20,28},{24,16},{28,20},{1,9},{5... | collective-permute-start | bytes 196616 | tf_op jit(solution)/shard_map/ppermute | solution.py:280
  42.4 8.9 %collective-permute-start.17 = (bf16[2,16,1024]{2,1,0:T(8,128)(2,1)S(1)}, bf16[2,16,1024]{2,1,0:T(8,128)(2,1)S(1)}, u32[]{:S(2)}, u32[]{:S(2)}) collective-permute-start(bf16[2,16,1024]{2,1,0:T(8,128)(2,1)S(1)} %fusion.1), channel_id=1, source_target_pairs={{0,16},{4,20},{8,24},{12,28},{16,0},{20,4},{24,8},{28,12},{1,17},{... | collective-permute-start | bytes 196616 | tf_op jit(solution)/shard_map/ppermute | solution.py:280
  44.5 6.7 %collective-permute-start.18 = (bf16[2,16,1024]{2,1,0:T(8,128)(2,1)S(1)}, bf16[2,16,1024]{2,1,0:T(8,128)(2,1)S(1)}, u32[]{:S(2)}, u32[]{:S(2)}) collective-permute-start(bf16[2,16,1024]{2,1,0:T(8,128)(2,1)S(1)} %fusion.1), channel_id=1, source_target_pairs={{0,24},{4,28},{8,16},{12,20},{16,8},{20,12},{24,0},{28,4},{1,25},{... | collective-permute-start | bytes 196616 | tf_op jit(solution)/shard_map/ppermute | solution.py:280
  46.8 6.6 %collective-permute-start.3 = (bf16[2,16,1024]{2,1,0:T(8,128)(2,1)S(1)}, bf16[2,16,1024]{2,1,0:T(8,128)(2,1)S(1)}, u32[]{:S(2)}, u32[]{:S(2)}) collective-permute-start(bf16[2,16,1024]{2,1,0:T(8,128)(2,1)S(1)} %get-tuple-element.32), channel_id=1, source_target_pairs={{0,8},{4,12},{8,0},{12,4},{16,24},{20,28},{24,16},{28,20},{1,9},{5... | collective-permute-start | bytes 196616 | tf_op jit(solution)/shard_map/ppermute | solution.py:278
  46.9 6.6 %collective-permute-start.4 = (bf16[2,16,1024]{2,1,0:T(8,128)(2,1)S(1)}, bf16[2,16,1024]{2,1,0:T(8,128)(2,1)S(1)}, u32[]{:S(2)}, u32[]{:S(2)}) collective-permute-start(bf16[2,16,1024]{2,1,0:T(8,128)(2,1)S(1)} %get-tuple-element.34), channel_id=1, source_target_pairs={{0,16},{4,20},{8,24},{12,28},{16,0},{20,4},{24,8},{28,12},{1,17},{... | collective-permute-start | bytes 196616 | tf_op jit(solution)/shard_map/ppermute | solution.py:278
  49.0 6.7 %collective-permute-start.5 = (bf16[2,16,1024]{2,1,0:T(8,128)(2,1)S(1)}, bf16[2,16,1024]{2,1,0:T(8,128)(2,1)S(1)}, u32[]{:S(2)}, u32[]{:S(2)}) collective-permute-start(bf16[2,16,1024]{2,1,0:T(8,128)(2,1)S(1)} %get-tuple-element.33), channel_id=1, source_target_pairs={{0,24},{4,28},{8,16},{12,20},{16,8},{20,12},{24,0},{28,4},{1,25},{... | collective-permute-start | bytes 196616 | tf_op jit(solution)/shard_map/ppermute | solution.py:278
  51.3 28.5 %collective-permute-start.19 = (bf16[8,16,1024]{2,1,0:T(8,128)(2,1)S(1)}, bf16[8,16,1024]{2,1,0:T(8,128)(2,1)S(1)}, u32[]{:S(2)}, u32[]{:S(2)}) collective-permute-start(bf16[8,16,1024]{2,1,0:T(8,128)(2,1)S(1)} %pad_maximum_fusion.2.mine_ref), channel_id=1, source_target_pairs={{0,4},{4,0},{8,12},{12,8},{16,20},{20,16},{24,28},{28,24},{1,5},{5... | collective-permute-start | bytes 786440 | tf_op jit(solution)/shard_map/ppermute | solution.py:282
  55.7 22.3 %collective-permute-start.6 = (bf16[2,16,1024]{2,1,0:T(8,128)(2,1)S(1)}, bf16[2,16,1024]{2,1,0:T(8,128)(2,1)S(1)}, u32[]{:S(2)}, u32[]{:S(2)}) collective-permute-start(bf16[2,16,1024]{2,1,0:T(8,128)(2,1)S(1)} %fusion.3), channel_id=1, source_target_pairs={{0,8},{4,12},{8,0},{12,4},{16,24},{20,28},{24,16},{28,20},{1,9},{5... | collective-permute-start | bytes 196616 | tf_op jit(solution)/shard_map/ppermute | solution.py:280
  57.3 20.7 %collective-permute-start.7 = (bf16[2,16,1024]{2,1,0:T(8,128)(2,1)S(1)}, bf16[2,16,1024]{2,1,0:T(8,128)(2,1)S(1)}, u32[]{:S(2)}, u32[]{:S(2)}) collective-permute-start(bf16[2,16,1024]{2,1,0:T(8,128)(2,1)S(1)} %fusion.3), channel_id=1, source_target_pairs={{0,16},{4,20},{8,24},{12,28},{16,0},{20,4},{24,8},{28,12},{1,17},{... | collective-permute-start | bytes 196616 | tf_op jit(solution)/shard_map/ppermute | solution.py:280
  58.7 19.3 %collective-permute-start.8 = (bf16[2,16,1024]{2,1,0:T(8,128)(2,1)S(1)}, bf16[2,16,1024]{2,1,0:T(8,128)(2,1)S(1)}, u32[]{:S(2)}, u32[]{:S(2)}) collective-permute-start(bf16[2,16,1024]{2,1,0:T(8,128)(2,1)S(1)} %fusion.3), channel_id=1, source_target_pairs={{0,24},{4,28},{8,16},{12,20},{16,8},{20,12},{24,0},{28,4},{1,25},{... | collective-permute-start | bytes 196616 | tf_op jit(solution)/shard_map/ppermute | solution.py:280
  74.7 3.3 %copy-start = (bf16[512,32,256]{2,1,0:T(8,128)(2,1)}, bf16[512,32,256]{2,1,0:T(8,128)(2,1)S(1)}, u32[]{:S(2)}) copy-start(bf16[512,32,256]{2,1,0:T(8,128)(2,1)S(1)} %turn.1.turned_ref) | copy-start | bytes 25165828
  78.0 18.8 %collective-permute-start.9 = (bf16[8,16,1024]{2,1,0:T(8,128)(2,1)S(1)}, bf16[8,16,1024]{2,1,0:T(8,128)(2,1)S(1)}, u32[]{:S(2)}, u32[]{:S(2)}) collective-permute-start(bf16[8,16,1024]{2,1,0:T(8,128)(2,1)S(1)} %pad_maximum_fusion.1.mine_ref), channel_id=1, source_target_pairs={{0,4},{4,0},{8,12},{12,8},{16,20},{20,16},{24,28},{28,24},{1,5},{5... | collective-permute-start | bytes 786440 | tf_op jit(solution)/shard_map/ppermute | solution.py:282
  96.8 17.9 %collective-permute-start.20 = (bf16[2,16,32,512]{3,2,1,0:T(8,128)(2,1)S(1)}, bf16[2,16,32,512]{3,2,1,0:T(8,128)(2,1)S(1)}, u32[]{:S(2)}, u32[]{:S(2)}) collective-permute-start(bf16[2,16,32,512]{3,2,1,0:T(8,128)(2,1)S(1)} %get-tuple-element.22), channel_id=1, source_target_pairs={{0,1},{1,0},{2,3},{3,2},{4,5},{5,4},{6,7},{7,6},{8,9},{9,8},{10,11... | collective-permute-start | bytes 3145736 | tf_op jit(solution)/shard_map/ppermute | solution.py:310
  114.1 2.9 %collective-permute-start.10 = (bf16[2,16,32,512]{3,2,1,0:T(8,128)(2,1)S(1)}, bf16[2,16,32,512]{3,2,1,0:T(8,128)(2,1)S(1)}, u32[]{:S(2)}, u32[]{:S(2)}) collective-permute-start(bf16[2,16,32,512]{3,2,1,0:T(8,128)(2,1)S(1)} %get-tuple-element.18), channel_id=1, source_target_pairs={{0,1},{1,0},{2,3},{3,2},{4,5},{5,4},{6,7},{7,6},{8,9},{9,8},{10,11... | collective-permute-start | bytes 3145736 | tf_op jit(solution)/shard_map/ppermute | solution.py:310
  115.1 14.8 %collective-permute-start.21 = (bf16[1,16,32,512]{3,2,1,0:T(8,128)(2,1)S(1)}, bf16[1,16,32,512]{3,2,1,0:T(8,128)(2,1)S(1)}, u32[]{:S(2)}, u32[]{:S(2)}) collective-permute-start(bf16[1,16,32,512]{3,2,1,0:T(8,128)(2,1)S(1)} %get-tuple-element.25), channel_id=1, source_target_pairs={{0,2},{1,3},{2,0},{3,1},{4,6},{5,7},{6,4},{7,5},{8,10},{9,11},{10,... | collective-permute-start | bytes 1572872 | tf_op jit(solution)/shard_map/ppermute | solution.py:311
  117.4 22.9 %collective-permute-start.11 = (bf16[1,16,32,512]{3,2,1,0:T(8,128)(2,1)S(1)}, bf16[1,16,32,512]{3,2,1,0:T(8,128)(2,1)S(1)}, u32[]{:S(2)}, u32[]{:S(2)}) collective-permute-start(bf16[1,16,32,512]{3,2,1,0:T(8,128)(2,1)S(1)} %get-tuple-element.27), channel_id=1, source_target_pairs={{0,2},{1,3},{2,0},{3,1},{4,6},{5,7},{6,4},{7,5},{8,10},{9,11},{10,... | collective-permute-start | bytes 1572872 | tf_op jit(solution)/shard_map/ppermute | solution.py:311

commit v2 on v0

v2 whole, which is shorter than its diff:
```python
import functools
import math

import jax
import jax.numpy as jnp
import ml_dtypes
import numpy as np
from jax import lax
from jax.experimental import pallas as pl
from jax.experimental.pallas import tpu as pltpu
from jax.sharding import PartitionSpec as P

LAGS = 512
SMOOTH = 21
EPSILON = 1e-06
CHUNKS = 2
LANES = 128
F32 = jnp.float32
BF16 = jnp.bfloat16
MIB = 1024 * 1024
SMEM = pl.BlockSpec(memory_space=pltpu.SMEM)
VMEM = pl.BlockSpec(memory_space=pltpu.VMEM)
ANY = pl.BlockSpec(memory_space=pl.ANY)


def cost(us):
    return pl.CostEstimate(flops=0, bytes_accessed=int(us * 3 * 10**6), transcendentals=0)


def call(kernel, ins, in_specs, outs, scratch, limit, us, name):
    return pl.pallas_call(
        kernel,
        in_specs=in_specs,
        out_specs=[VMEM] * len(outs),
        out_shape=[jax.ShapeDtypeStruct(shape, dtype) for shape, dtype in outs],
        scratch_shapes=scratch,
        compiler_params=pltpu.CompilerParams(vmem_limit_bytes=limit * MIB),
        cost_estimate=cost(us),
        name=name,
    )(*ins)


def xor_pairs(count, mask):
    return [(i, i ^ mask) for i in range(count)]


def place(blocks):
    if blocks != 8:
        return 0, 0
    at = lax.axis_index("chan")
    return at % 2, at // 2


def source_at(blocks, r, per_chunk):
    x, z = place(blocks)
    quarter = per_chunk // 8
    chunk, r = divmod(r, per_chunk)
    half, r = divmod(r, 4 * quarter)
    part, i = divmod(r, quarter)
    return chunk * per_chunk + (x ^ half) * 4 * quarter + (z ^ part) * quarter + i


def amplitude(values):
    freqs = values.shape[-1] // 2
    real, imag = values[:, :freqs], values[:, freqs:]
    return jnp.sqrt(real * real + imag * imag)


def bin_share(freqs):
    f = lax.broadcasted_iota(jnp.int32, (1, freqs), 1)
    entries = jnp.minimum(f, SMOOTH) + jnp.minimum(freqs - 1 - f, SMOOTH) + 1
    return 1.0 / (3.0 * entries.astype(F32))


def whitened_rows(values, triple, band, share):
    freqs = triple.shape[-1]
    spatial = jnp.dot(triple.astype(BF16), band, preferred_element_type=F32)
    inverse = 1.0 / (spatial * share + EPSILON)
    return jnp.concatenate([values[:, :freqs] * inverse, values[:, freqs:] * inverse], axis=1).astype(BF16)


def whiten_kernel(blocks, src_ref, valid_ref, spec_ref, white_ref, held, band, part_ref, raw_ref, buf, sel, sems):
    windows, chans, width = white_ref.shape
    freqs = width // 2
    sources = src_ref.shape[0]
    pitch = windows + 8

    def fetch(w):
        return pltpu.make_async_copy(spec_ref.at[w], buf.at[w], sems.at[w])

    for w in range(windows):
        fetch(w).start()
    row = lax.broadcasted_iota(jnp.int32, (freqs, freqs), 0)
    col = lax.broadcasted_iota(jnp.int32, (freqs, freqs), 1)
    band[...] = jnp.where(jnp.abs(row - col) <= SMOOTH, 1.0, 0.0).astype(BF16)
    offset = lax.axis_index("chan") * chans
    lane = lax.broadcasted_iota(jnp.int32, (1, chans), 1)
    inner = jnp.where((lane > 0) & (lane < chans - 1), 1.0, 0.0)
    for r in range(sources):
        at = src_ref[source_at(blocks, r, sources // CHUNKS)] - offset
        sel[r : r + 1, :] = jnp.where(lane == at, inner, 0.0)
    share = bin_share(freqs)

    def one(w, carry):
        fetch(w).wait()
        values = buf[w].astype(F32)
        magnitude = amplitude(values)
        triple = pltpu.roll(magnitude, 1, 0) + magnitude + pltpu.roll(magnitude, chans - 1, 0)
        white = whitened_rows(values, triple, band[...], share)
        white_ref[w] = white
        part_ref[0, pl.ds(w, 1), :] = magnitude[0:1] + magnitude[1:2]
        part_ref[1, pl.ds(w, 1), :] = magnitude[chans - 2 : chans - 1] + magnitude[chans - 1 :]
        raw_ref[0, pl.ds(w, 1), :] = values[0:1]
        raw_ref[1, pl.ds(w, 1), :] = values[chans - 1 :]
        keep = (sel[...] * valid_ref[w].astype(F32)).astype(BF16)
        picked = jnp.dot(keep, white, preferred_element_type=F32)
        for j in range(width // LANES):
            held[j, pl.ds(w, sources, stride=pitch), :] = picked[:, j * LANES : (j + 1) * LANES]
        return carry

    lax.fori_loop(0, windows, one, 0, unroll=2)


def whiten(blocks, spectra, valid, sources):
    windows, chans, width = spectra.shape
    count = sources.shape[0]
    return call(
        functools.partial(whiten_kernel, blocks),
        (sources, valid, spectra),
        [SMEM, SMEM, ANY],
        [
            (spectra.shape, BF16),
            ((width // LANES, count * (windows + 8), LANES), F32),
            ((width // 2, width // 2), BF16),
            ((2, windows, width // 2), F32),
            ((2, windows, width), F32),
        ],
        [
            pltpu.VMEM(spectra.shape, BF16),
            pltpu.VMEM((count, chans), F32),
            pltpu.SemaphoreType.DMA((windows,)),
        ],
        24,
        6,
        "whiten",
    )


def edges_kernel(blocks, chans, src_ref, valid_ref, low_ref, high_ref, held, band, part_ref, raw_ref, *outs):
    picks, edge_ref = outs[:-1], outs[-1]
    windows, width = raw_ref.shape[1:]
    freqs = width // 2
    sources = src_ref.shape[0]
    pitch = windows + 8
    share = bin_share(freqs)
    row = lax.broadcasted_iota(jnp.int32, (windows, 1), 0)
    valid = jnp.zeros((windows, 1), F32)
    for w in range(windows):
        valid = valid + jnp.where(row == w, valid_ref[w].astype(F32), 0.0)
    entering = []
    for k, ref in enumerate((low_ref, high_ref)):
        beside = jnp.concatenate([ref[w] for w in range(windows)], axis=0).astype(F32)
        white = whitened_rows(raw_ref[k], part_ref[k] + amplitude(beside), band[...], share).astype(F32)
        edge_ref[k] = white
        entering.append(white * valid)
    offset = lax.axis_index("chan") * chans
    rows = picks[0].shape[0]
    for r in range(sources):
        at = src_ref[source_at(blocks, r, sources // CHUNKS)] - offset
        first = (at == 0).astype(F32)
        last = (at == chans - 1).astype(F32)
        for j in range(width // LANES):
            lanes = slice(j * LANES, (j + 1) * LANES)
            value = held[j, r * pitch : r * pitch + windows, :]
            value = value + first * entering[0][:, lanes] + last * entering[1][:, lanes]
            picks[r // rows][r % rows, :, lanes] = value.astype(BF16)


def edges(blocks, chans, valid, sources, low, high, held, band, part, raw):
    _, windows, width = raw.shape
    rows = sources.shape[0] // CHUNKS // 2
    return call(
        functools.partial(edges_kernel, blocks, chans),
        (sources, valid, low, high, held, band, part, raw),
        [SMEM, SMEM] + [VMEM] * 6,
        [((rows, windows, width), BF16)] * (2 * CHUNKS) + [(raw.shape, F32)],
        [],
        16,
        1,
        "edges",
    )


def turn_kernel(first, white_ref, edge_ref, out_ref, held):
    windows, chans, width = white_ref.shape
    tile = LANES
    pitch = 2 * windows + 8
    for block in range(out_ref.shape[0] // tile):
        for w in range(windows):
            for half in range(2):
                at = half * (width // 2) + (first + block) * tile
                lanes = slice(at, at + tile)
                body = white_ref[w, :, lanes].astype(F32)
                row = lax.broadcasted_iota(jnp.int32, (8, tile), 0)
                top = jnp.where(row == 0, edge_ref[0, w : w + 1, lanes], body[:8])
                bottom = jnp.where(row == 7, edge_ref[1, w : w + 1, lanes], body[chans - 8 :])
                body = jnp.concatenate([top, body[8 : chans - 8], bottom], axis=0)
                held[pl.ds(half * windows + w, tile, stride=pitch), :] = body.T
        for f in range(tile):
            out_ref[block * tile + f] = held[f * pitch : f * pitch + 2 * windows, :].astype(BF16)


def turn(white, edge, first, tiles):
    windows, chans, width = white.shape
    return call(
        functools.partial(turn_kernel, first),
        (white, edge),
        [VMEM, VMEM],
        [((tiles * LANES, 2 * windows, chans), BF16)],
        [pltpu.VMEM((LANES * (2 * windows + 8), chans), F32)],
        16,
        4,
        "turn",
    )[0]


def add_parts_kernel(keep_ref, came_ref, after_ref, *outs):
    rows = outs[0].shape[0]
    for p, out in enumerate(outs):
        out[...] = keep_ref[p * rows : (p + 1) * rows] + came_ref[p * rows : (p + 1) * rows]


def add_parts(keep, came, after):
    rows, windows, width = keep.shape
    return call(
        add_parts_kernel,
        (keep, came, after),
        [VMEM, VMEM, ANY],
        [((rows // 4, windows, width), BF16)] * 4,
        [],
        8,
        0.2,
        "add_parts",
    )


def add_four_kernel(a_ref, b_ref, c_ref, d_ref, after_ref, out_ref):
    out_ref[...] = a_ref[...] + b_ref[...] + c_ref[...] + d_ref[...]


def add_four(pieces, after):
    return call(
        add_four_kernel,
        (*pieces, after),
        [VMEM] * 4 + [ANY],
        [(pieces[0].shape, BF16)],
        [],
        8,
        0.2,
        "add_four",
    )[0]


def cross_kernel(parts, mine_ref, theirs_ref, low_ref, high_ref, cos_ref, sin_ref, after_ref, keep_ref, send_ref, vt, st):
    half, windows, width = mine_ref.shape
    held_freqs, depth, chans = low_ref.shape
    freqs = width // 2
    rows = 2 * half
    pitch = rows + 8
    tile = LANES
    group = tile // depth
    for g in range(rows // group):
        pieces = []
        for s in range(g * group, (g + 1) * group):
            ref = mine_ref if s < half else theirs_ref
            v = ref[s % half].astype(F32)
            pieces += [v[:, :freqs], v[:, freqs:]]
        stack = jnp.concatenate(pieces, axis=0)
        for j in range(freqs // tile):
            t = stack[:, j * tile : (j + 1) * tile].T
            for i in range(group):
                moved = t if i == 0 else pltpu.roll(t, tile - i * depth, 1)
                vt[pl.ds(j * tile * pitch + g * group + i, tile, stride=pitch), :] = moved

    unroll = 64
    for which, ref in enumerate((low_ref, high_ref)):

        def step(i, carry):
            for k in range(unroll):
                f = i * unroll + k
                at = pl.multiple_of((which * held_freqs + f) * pitch, 8)
                lhs = vt[pl.ds(at, rows), 0:depth].astype(BF16)
                x = ref[f]
                crossed = jnp.concatenate([x[windows:], -x[:windows]], axis=0)
                sums = jnp.dot(lhs, jnp.concatenate([x, crossed], axis=1), preferred_element_type=F32)
                st[0, pl.ds(at, rows), :] = sums[:, :chans]
                st[1, pl.ds(at, rows), :] = sums[:, chans:]
            return carry

        lax.fori_loop(0, held_freqs // unroll, step, 0)

    me = lax.axis_index("win")
    share = chans // parts
    lags = keep_ref.shape[-1]
    last_row = lax.broadcasted_iota(jnp.int32, (8, 1), 0) == 7

    def transform(p, carry):
        real, imag = [
            jnp.concatenate([st[i, pl.ds(2 * p + k, freqs, stride=pitch), :].astype(BF16) for k in (0, 1)], axis=1)
            for i in (0, 1)
        ]
        even = jnp.dot(cos_ref[...], real, preferred_element_type=F32)
        odd = jnp.dot(sin_ref[...], imag, preferred_element_type=F32)
        tail = odd[lags // 2 - 8 :] + jnp.where(last_row, even[lags // 2 : lags // 2 + 1], 0.0)
        out = jnp.concatenate([even[: lags // 2], odd[: lags // 2 - 8], tail], axis=0)
        for k in range(2):
            flat = out[:, k * chans : (k + 1) * chans].T.astype(BF16)
            for b in range(parts):
                slot = b ^ me
                value = flat[b * share : (b + 1) * share, :]

                @pl.when(slot % 2 == 0)
                def _():
                    keep_ref[slot // 2, 2 * p + k] = value

                @pl.when(slot % 2 == 1)
                def _():
                    send_ref[slot // 2, 2 * p + k] = value

        return carry

    lax.fori_loop(0, rows // 2, transform, 0)


def cross(parts, mine, theirs, turned, tables, after):
    half, windows, width = mine.shape
    chans = turned[0].shape[-1]
    rows = 2 * half
    held = width // 2 * (rows + 8)
    return call(
        functools.partial(cross_kernel, parts),
        (mine, theirs, *turned, *tables, after),
        [VMEM] * 6 + [ANY],
        [((parts // 2, rows, chans // parts, LAGS), BF16)] * 2,
        [pltpu.VMEM((held, LANES), F32), pltpu.VMEM((2, held, chans), F32)],
        32,
        7,
        "cross",
    )


def unfold_kernel(blocks, chunk, own_ref, came_ref, mix_ref, *rest):
    earlier, (out_ref, held) = rest[:-2], rest[-2:]
    rows, chans, lags = own_ref.shape[1:]
    pitch = rows + 8
    total = jnp.zeros((rows * chans, lags), F32)
    for ref in (own_ref, came_ref):
        flat = ref[...].reshape(rows * chans, lags)
        total = total + jnp.dot(flat, mix_ref[...], preferred_element_type=F32)
    for r in range(rows):
        at = source_at(blocks, r, rows)
        for j in range(lags // LANES):
            held[j, pl.ds(at, chans, stride=pitch), :] = total[r * chans : (r + 1) * chans, j * LANES : (j + 1) * LANES]
    first = out_ref.shape[1] - rows
    for c in range(chans):
        if earlier:
            out_ref[c, :first, :] = earlier[0][c]
        for j in range(lags // LANES):
            lanes = slice(j * LANES, (j + 1) * LANES)
            out_ref[c, first:, lanes] = held[j, c * pitch : c * pitch + rows, :].astype(BF16)


def unfold(blocks, own, came, mix, earlier):
    _, rows, chans, lags = own.shape
    return call(
        functools.partial(unfold_kernel, blocks, len(earlier)),
        (own, came, mix, *earlier),
        [VMEM] * (3 + len(earlier)),
        [((chans, rows * (1 + len(earlier)), lags), BF16)],
        [pltpu.VMEM((lags // LANES, chans * (rows + 8), LANES), F32)],
        16,
        1.5,
        "unfold",
    )[0]


def exchange_x(blocks, keep, send):
    return lax.ppermute(send, "chan", xor_pairs(blocks, 1))


def spread(blocks, keep, send, after):
    if blocks != 8:
        return lax.psum(keep, "chan"), lax.psum(send, "chan")
    across = xor_pairs(8, 1)
    pieces = add_parts(keep, lax.ppermute(send, "chan", across), after[0])
    came = [lax.ppermute(pieces[p], "chan", xor_pairs(8, 2 * p)) for p in (1, 2, 3)]
    own = add_four([pieces[0]] + came, after[1])
    others = [lax.ppermute(own, "chan", xor_pairs(8, 2 * p)) for p in (1, 2, 3)]
    mine = jnp.concatenate([own] + others, axis=0)
    return mine, lax.ppermute(mine, "chan", across)


def lag_tables(freqs, windows):
    half = LAGS // 2
    f = np.arange(freqs)[None, :]
    scale = np.where(f == 0, 1.0, 2.0) * 0.25 / math.sqrt(freqs * windows)
    u = np.arange(half + 16)[:, None]
    cos = np.where(u <= half, scale * np.cos(math.pi * (f * u % (2 * freqs)) / freqs), 0.0)
    u = np.arange(1, half + 1)[:, None]
    sin = -scale * np.sin(math.pi * (f * u % (2 * freqs)) / freqs) * np.where(u == half, -1.0, 1.0)
    return jnp.asarray(cos.astype(ml_dtypes.bfloat16)), jnp.asarray(sin.astype(ml_dtypes.bfloat16))


def lag_mix():
    half = LAGS // 2
    mix = np.zeros((LAGS, LAGS))
    u = np.arange(half)
    mix[u, half + u] = 1
    u = np.arange(1, half)
    mix[u, half - u] = 1
    mix[half - 1 + u, half + u] = 1
    mix[half - 1 + u, half - u] = -1
    mix[LAGS - 1, 0] = 1
    return jnp.asarray(mix.astype(ml_dtypes.bfloat16))


def on_device(blocks, parts, spectra, valid, sources):
    windows, chans, width = spectra.shape
    freqs = width // 2
    forward = [(i, (i + 1) % blocks) for i in range(blocks)]
    backward = [(b, a) for a, b in forward]
    low = lax.ppermute(spectra[:, chans - 1 :, :], "chan", forward)
    high = lax.ppermute(spectra[:, :1, :], "chan", backward)
    white, held, band, part, raw = whiten(blocks, spectra, valid, sources)
    *picks, edge = edges(blocks, chans, valid, sources, low, high, held, band, part, raw)
    tables = lag_tables(freqs, windows)
    mix = lag_mix()
    tiles = freqs // LANES // 2
    turned = [turn(white, edge, i * tiles, tiles) for i in range(2)]
    rows = [spread(blocks, picks[2 * c], picks[2 * c + 1], turned) for c in range(CHUNKS)]
    out, after = [], turned[0]
    for mine, theirs in rows:
        keep, send = cross(parts, mine, theirs, turned, tables, after)
        total = keep + lax.ppermute(send, "win", xor_pairs(parts, 1))
        after = total
        out = [unfold(blocks, total[:1], lax.ppermute(total[1:], "win", xor_pairs(parts, 2)), mix, out)]
    return out[0]


def solution(mesh):
    return jax.shard_map(
        functools.partial(on_device, mesh.shape["chan"], mesh.shape["win"]),
        mesh=mesh,
        in_specs=(P("win", "chan", None), P("win"), P()),
        out_specs=P(("chan", "win"), None, None),
        check_vma=False,
    )
```

time: 274 us -> 130 us (0.47)
  blocking collectives: 92.1 us -> 0 us
  local copies, waits for them, and re-layouts: 42.8 us -> 4.79 us
  Pallas kernels: 0 us -> 32.4 us
  other arithmetic: 29.1 us -> 0.86 us
  matrix products: 22.1 us -> 0 us
  starting transfers between devices: 6.1 us -> 28.2 us
  between operations: 13.6 us -> 0.21 us
  waiting for transfers between devices: 67.4 us -> 63.4 us
    psum x1 -> x0, blocking collectives: 92.1 us -> none  [on_device(): source_rows = lax.psum(picked, 'chan').astype(jnp.bfloat16)]
    reduce_scatter x1 -> x0, waiting for transfers between devices: 65.7 us -> none  [on_device(): lax.psum_scatter(cross_spectra(masked_rows, whitened, freqs).astype(jnp.b...]
    ppermute x2 -> x22, waiting for transfers between devices: 1.67 us -> 63.4 us  [the longest x2 19.9 us: on_device(): lax.ppermute(total[1:], 'win', xor_pairs(parts, 2))]
    pallas_call x0 -> x12, Pallas kernels: none -> 32.4 us  [call(): pl.pallas_call(kernel, in_specs=in_specs, out_specs=[VMEM] * len(outs), o...]
    concatenate x3 -> x0, local copies, waits for them, and re-layouts: 22.4 us -> none  [the longest x1 7.97 us: cross_spectra(): real_rhs = jnp.concatenate([recv_real, recv_imag], axis=0)]
    ppermute x2 -> x22, starting transfers between devices: 6.09 us -> 28.2 us  [the longest x6 8.9 us: spread(): others = [lax.ppermute(own, 'chan', xor_pairs(8, 2 * p)) for p in (1, 2, 3)]]
    dot_general x5 -> x0, matrix products: 22.1 us -> none  [the longest x1 6.94 us: cross_spectra(): jnp.einsum('swf,wcf->csf', src_both, real_rhs, preferred_element_type=jnp...]
    dot_general x2 -> x0, local copies, waits for them, and re-layouts: 17.2 us -> none  [the longest x1 8.62 us: cross_spectra(): jnp.einsum('swf,wcf->csf', src_both, imag_rhs, preferred_element_type=jnp...]
  transfers between devices with their start and end apart: 3 -> 22, of which waited for: 2 -> 15; matrix products, arithmetic and copies ran while one was open for 2% -> 1% of each run, Pallas kernels for 0% -> 10%
where the time goes in v2:
time: 130 us
  waiting for transfers between devices  63.4 us (49%)
  Pallas kernels  32.4 us (25%)
  starting transfers between devices  28.2 us (22%)
  local copies, waits for them, and re-layouts  4.79 us (4%)
    pallas_call x12, Pallas kernels, call(): pl.pallas_call(kernel, in_specs=in_specs, out_specs=[VMEM] * len(outs), o...  32.4 us
    ppermute x2, waiting for transfers between devices, on_device(): lax.ppermute(total[1:], 'win', xor_pairs(parts, 2))  19.9 us
    ppermute x2, waiting for transfers between devices, spread(): pieces = add_parts(keep, lax.ppermute(send, 'chan', across), after[0])  15 us
    ppermute x2, waiting for transfers between devices, spread(): return (mine, lax.ppermute(mine, 'chan', across))  12 us
    ppermute x6, waiting for transfers between devices, spread(): others = [lax.ppermute(own, 'chan', xor_pairs(8, 2 * p)) for p in (1, 2, 3)]  9.46 us
    ppermute x6, starting transfers between devices, spread(): others = [lax.ppermute(own, 'chan', xor_pairs(8, 2 * p)) for p in (1, 2, 3)]  8.9 us
    ppermute x6, starting transfers between devices, spread(): lax.ppermute(pieces[p], 'chan', xor_pairs(8, 2 * p))  8.89 us
    ppermute x6, waiting for transfers between devices, spread(): lax.ppermute(pieces[p], 'chan', xor_pairs(8, 2 * p))  6.28 us
  transfers between devices with their start and end apart: 22, of which 15 were waited for; matrix products, arithmetic and copies ran while one was open for 1% of the time, Pallas kernels for 10%

profile of v2, /device:TPU:0, one launch (start us, length us, event | category | flops | bytes accessed | tf_op | source)
XLA Modules:
  0.0 129.9 jit_solution(13221126659066477906)
XLA Ops:
  0.0 1.1 fusion
  1.1 3.0 %collective-permute-start = (bf16[16,1,1024]{2,1,0:T(2,128)(2,1)S(1)}, bf16[16,1,1024]{2,1,0:T(2,128)(2,1)S(1)}, u32[]{:S(2)}, u32[]{:S(2)}) collective-permute-start(bf16[16,1,1024]{2,1,0:T(2,128)(2,1)S(1)} %get-tuple-element.50), channel_id=1, source_target_pairs={{0,4},{4,8},{8,12},{12,16},{16,20},{20,24},{24,28},{28,0},{1,5},{5... | collective-permute-start | bytes 98312 | tf_op jit(solution)/shard_map/ppermute | solution.py:432
  4.1 3.1 %collective-permute-start.1 = (bf16[16,1,1024]{2,1,0:T(2,128)(2,1)S(1)}, bf16[16,1,1024]{2,1,0:T(2,128)(2,1)S(1)}, u32[]{:S(2)}, u32[]{:S(2)}) collective-permute-start(bf16[16,1,1024]{2,1,0:T(2,128)(2,1)S(1)} %get-tuple-element.49), channel_id=1, source_target_pairs={{4,0},{8,4},{12,8},{16,12},{20,16},{24,20},{28,24},{0,28},{5,1},{9... | collective-permute-start | bytes 98312 | tf_op jit(solution)/shard_map/ppermute | solution.py:433
  7.2 2.2 %copy-done = bf16[16,128,1024]{2,1,0:T(8,128)(2,1)S(1)} copy-done((bf16[16,128,1024]{2,1,0:T(8,128)(2,1)S(1)}, bf16[16,128,1024]{2,1,0:T(8,128)(2,1)}, u32[]{:S(2)}) %copy-start) | copy-done | bytes 4194328
  9.4 0.7 copy-done.4
  10.1 0.7 copy-done.5
  10.7 9.0 %whiten.1 = (bf16[16,128,1024]{2,1,0:T(8,128)(2,1)S(1)}, f32[8,768,128]{2,1,0:T(8,128)S(1)}, bf16[512,512]{1,0:T(8,128)(2,1)S(1)}, f32[2,16,512]{2,1,0:T(8,128)S(1)}, f32[2,16,1024]{2,1,0:T(8,128)S(1)}) custom-call(s32[32]{0:T(128)S(1)} %copy-done.4, s32[16]{0:T(128)S(1)} %copy-done.5, bf16[16,128,1024]{2,1,0:T(8,128)(2,1)S(1)} %copy-done), custom_call_target="tpu_custom_call" | custom-call | bytes 18000000 | tf_op jit(solution)/shard_map/whiten/pallas_call | solution.py:31
  19.7 0.0 collective-permute-done.low_ref
  19.7 0.0 collective-permute-done.1.high_ref
  19.7 1.2 edges.1
  21.0 0.1 collective-permute-start.10
  21.0 1.4 %turn.2.after_ref.low_ref = bf16[256,32,128]{2,1,0:T(8,128)(2,1)S(1)} custom-call(bf16[16,128,1024]{2,1,0:T(8,128)(2,1)S(1)} %get-tuple-element.33.white_ref, f32[2,16,1024]{2,1,0:T(8,128)S(1)} %get-tuple-element.34.edge_ref), custom_call_target="tpu_custom_call" | custom-call | bytes 12000000 | tf_op jit(solution)/shard_map/turn/pallas_call | solution.py:31
  22.5 6.3 %collective-permute-done.10.came_ref = bf16[8,16,1024]{2,1,0:T(8,128)(2,1)S(1)} collective-permute-done((bf16[8,16,1024]{2,1,0:T(8,128)(2,1)S(1)}, bf16[8,16,1024]{2,1,0:T(8,128)(2,1)S(1)}, u32[]{:S(2)}, u32[]{:S(2)}) %collective-permute-start.10) | collective-permute-done | bytes 262176 | tf_op jit(solution)/shard_map/ppermute | solution.py:395
  28.8 0.1 collective-permute-start.11
  28.9 2.2 %collective-permute-start.12 = (bf16[2,16,1024]{2,1,0:T(8,128)(2,1)S(1)}, bf16[2,16,1024]{2,1,0:T(8,128)(2,1)S(1)}, u32[]{:S(2)}, u32[]{:S(2)}) collective-permute-start(bf16[2,16,1024]{2,1,0:T(8,128)(2,1)S(1)} %get-tuple-element.43), channel_id=1, source_target_pairs={{0,16},{4,20},{8,24},{12,28},{16,0},{20,4},{24,8},{28,12},{1,17},{... | collective-permute-start | bytes 196616 | tf_op jit(solution)/shard_map/ppermute | solution.py:396
  31.1 2.2 %collective-permute-start.13 = (bf16[2,16,1024]{2,1,0:T(8,128)(2,1)S(1)}, bf16[2,16,1024]{2,1,0:T(8,128)(2,1)S(1)}, u32[]{:S(2)}, u32[]{:S(2)}) collective-permute-start(bf16[2,16,1024]{2,1,0:T(8,128)(2,1)S(1)} %get-tuple-element.44), channel_id=1, source_target_pairs={{0,24},{4,28},{8,16},{12,20},{16,8},{20,12},{24,0},{28,4},{1,25},{... | collective-permute-start | bytes 196616 | tf_op jit(solution)/shard_map/ppermute | solution.py:396
  33.3 1.4 %turn.3.after_ref.high_ref = bf16[256,32,128]{2,1,0:T(8,128)(2,1)S(1)} custom-call(bf16[16,128,1024]{2,1,0:T(8,128)(2,1)S(1)} %get-tuple-element.33.white_ref, f32[2,16,1024]{2,1,0:T(8,128)S(1)} %get-tuple-element.34.edge_ref), custom_call_target="tpu_custom_call" | custom-call | bytes 12000000 | tf_op jit(solution)/shard_map/turn/pallas_call | solution.py:31
  34.7 0.0 collective-permute-done.11.b_ref
  34.7 0.0 collective-permute-done.12.c_ref
  34.8 2.5 %collective-permute-done.13.d_ref = bf16[2,16,1024]{2,1,0:T(8,128)(2,1)S(1)} collective-permute-done((bf16[2,16,1024]{2,1,0:T(8,128)(2,1)S(1)}, bf16[2,16,1024]{2,1,0:T(8,128)(2,1)S(1)}, u32[]{:S(2)}, u32[]{:S(2)}) %collective-permute-start.13) | collective-permute-done | bytes 65568 | tf_op jit(solution)/shard_map/ppermute | solution.py:396
  37.2 0.1 collective-permute-start.14
  37.3 3.1 %collective-permute-start.15 = (bf16[2,16,1024]{2,1,0:T(8,128)(2,1)S(1)}, bf16[2,16,1024]{2,1,0:T(8,128)(2,1)S(1)}, u32[]{:S(2)}, u32[]{:S(2)}) collective-permute-start(bf16[2,16,1024]{2,1,0:T(8,128)(2,1)S(1)} %add_four.3), channel_id=1, source_target_pairs={{0,16},{4,20},{8,24},{12,28},{16,0},{20,4},{24,8},{28,12},{1,17},{... | collective-permute-start | bytes 196616 | tf_op jit(solution)/shard_map/ppermute | solution.py:398
  40.5 1.2 collective-permute-start.16
  41.7 1.3 collective-permute-done.14
  43.0 0.0 collective-permute-done.15
  43.0 3.5 %collective-permute-done.16 = bf16[2,16,1024]{2,1,0:T(8,128)(2,1)S(1)} collective-permute-done((bf16[2,16,1024]{2,1,0:T(8,128)(2,1)S(1)}, bf16[2,16,1024]{2,1,0:T(8,128)(2,1)S(1)}, u32[]{:S(2)}, u32[]{:S(2)}) %collective-permute-start.16) | collective-permute-done | bytes 65568 | tf_op jit(solution)/shard_map/ppermute | solution.py:398
  46.6 0.1 collective-permute-start.17
  46.6 6.3 %collective-permute-done.17.theirs_ref = bf16[8,16,1024]{2,1,0:T(8,128)(2,1)S(1)} collective-permute-done((bf16[8,16,1024]{2,1,0:T(8,128)(2,1)S(1)}, bf16[8,16,1024]{2,1,0:T(8,128)(2,1)S(1)}, u32[]{:S(2)}, u32[]{:S(2)}) %collective-permute-start.17) | collective-permute-done | bytes 262176 | tf_op jit(solution)/shard_map/ppermute | solution.py:400
  53.0 0.0 copy-done.2
  53.0 0.0 copy-done.3
  53.0 8.3 %cross.2 = (bf16[2,16,32,512]{3,2,1,0:T(8,128)(2,1)S(1)}, bf16[2,16,32,512]{3,2,1,0:T(8,128)(2,1)S(1)}) custom-call(bf16[8,16,1024]{2,1,0:T(8,128)(2,1)S(1)} %pad_maximum_fusion.1.mine_ref, bf16[8,16,1024]{2,1,0:T(8,128)(2,1)S(1)} %collective-permute-done.17.theirs_ref, bf16[256,32,128]{2,1,0:T(8,128)(2,1)S(1)} %turn.2.after_ref.low_ref, ...), custom_call_target="tpu_custom_call" | custom-call | bytes 21000000 | tf_op jit(solution)/shard_map/cross/pallas_call | solution.py:31
  61.3 0.1 collective-permute-start.18
  61.3 0.1 collective-permute-start.2
  61.4 8.6 %collective-permute-done.2.came_ref = bf16[8,16,1024]{2,1,0:T(8,128)(2,1)S(1)} collective-permute-done((bf16[8,16,1024]{2,1,0:T(8,128)(2,1)S(1)}, bf16[8,16,1024]{2,1,0:T(8,128)(2,1)S(1)}, u32[]{:S(2)}, u32[]{:S(2)}) %collective-permute-start.2) | collective-permute-done | bytes 262176 | tf_op jit(solution)/shard_map/ppermute | solution.py:395
  70.1 0.1 collective-permute-start.3
  70.2 1.8 %collective-permute-start.4 = (bf16[2,16,1024]{2,1,0:T(8,128)(2,1)S(1)}, bf16[2,16,1024]{2,1,0:T(8,128)(2,1)S(1)}, u32[]{:S(2)}, u32[]{:S(2)}) collective-permute-start(bf16[2,16,1024]{2,1,0:T(8,128)(2,1)S(1)} %get-tuple-element.37), channel_id=1, source_target_pairs={{0,16},{4,20},{8,24},{12,28},{16,0},{20,4},{24,8},{28,12},{1,17},{... | collective-permute-start | bytes 196616 | tf_op jit(solution)/shard_map/ppermute | solution.py:396
  72.0 2.6 %collective-permute-start.5 = (bf16[2,16,1024]{2,1,0:T(8,128)(2,1)S(1)}, bf16[2,16,1024]{2,1,0:T(8,128)(2,1)S(1)}, u32[]{:S(2)}, u32[]{:S(2)}) collective-permute-start(bf16[2,16,1024]{2,1,0:T(8,128)(2,1)S(1)} %get-tuple-element.38), channel_id=1, source_target_pairs={{0,24},{4,28},{8,16},{12,20},{16,8},{20,12},{24,0},{28,4},{1,25},{... | collective-permute-start | bytes 196616 | tf_op jit(solution)/shard_map/ppermute | solution.py:396
  74.6 0.2 collective-permute-done.3.b_ref
  74.8 3.5 %collective-permute-done.4.c_ref = bf16[2,16,1024]{2,1,0:T(8,128)(2,1)S(1)} collective-permute-done((bf16[2,16,1024]{2,1,0:T(8,128)(2,1)S(1)}, bf16[2,16,1024]{2,1,0:T(8,128)(2,1)S(1)}, u32[]{:S(2)}, u32[]{:S(2)}) %collective-permute-start.4) | collective-permute-done | bytes 65568 | tf_op jit(solution)/shard_map/ppermute | solution.py:396
  78.3 0.0 collective-permute-done.5.d_ref
  78.3 1.3 %collective-permute-start.6 = (bf16[2,16,1024]{2,1,0:T(8,128)(2,1)S(1)}, bf16[2,16,1024]{2,1,0:T(8,128)(2,1)S(1)}, u32[]{:S(2)}, u32[]{:S(2)}) collective-permute-start(bf16[2,16,1024]{2,1,0:T(8,128)(2,1)S(1)} %add_four.2), channel_id=1, source_target_pairs={{0,8},{4,12},{8,0},{12,4},{16,24},{20,28},{24,16},{28,20},{1,9},{5... | collective-permute-start | bytes 196616 | tf_op jit(solution)/shard_map/ppermute | solution.py:398
  79.7 1.7 %collective-permute-start.7 = (bf16[2,16,1024]{2,1,0:T(8,128)(2,1)S(1)}, bf16[2,16,1024]{2,1,0:T(8,128)(2,1)S(1)}, u32[]{:S(2)}, u32[]{:S(2)}) collective-permute-start(bf16[2,16,1024]{2,1,0:T(8,128)(2,1)S(1)} %add_four.2), channel_id=1, source_target_pairs={{0,16},{4,20},{8,24},{12,28},{16,0},{20,4},{24,8},{28,12},{1,17},{... | collective-permute-start | bytes 196616 | tf_op jit(solution)/shard_map/ppermute | solution.py:398
  81.4 1.4 %collective-permute-start.8 = (bf16[2,16,1024]{2,1,0:T(8,128)(2,1)S(1)}, bf16[2,16,1024]{2,1,0:T(8,128)(2,1)S(1)}, u32[]{:S(2)}, u32[]{:S(2)}) collective-permute-start(bf16[2,16,1024]{2,1,0:T(8,128)(2,1)S(1)} %add_four.2), channel_id=1, source_target_pairs={{0,24},{4,28},{8,16},{12,20},{16,8},{20,12},{24,0},{28,4},{1,25},{... | collective-permute-start | bytes 196616 | tf_op jit(solution)/shard_map/ppermute | solution.py:398
  82.8 0.2 collective-permute-done.6
  82.9 2.7 %collective-permute-done.7 = bf16[2,16,1024]{2,1,0:T(8,128)(2,1)S(1)} collective-permute-done((bf16[2,16,1024]{2,1,0:T(8,128)(2,1)S(1)}, bf16[2,16,1024]{2,1,0:T(8,128)(2,1)S(1)}, u32[]{:S(2)}, u32[]{:S(2)}) %collective-permute-start.7) | collective-permute-done | bytes 65568 | tf_op jit(solution)/shard_map/ppermute | solution.py:398
  85.7 1.7 %collective-permute-done.8 = bf16[2,16,1024]{2,1,0:T(8,128)(2,1)S(1)} collective-permute-done((bf16[2,16,1024]{2,1,0:T(8,128)(2,1)S(1)}, bf16[2,16,1024]{2,1,0:T(8,128)(2,1)S(1)}, u32[]{:S(2)}, u32[]{:S(2)}) %collective-permute-start.8) | collective-permute-done | bytes 65568 | tf_op jit(solution)/shard_map/ppermute | solution.py:398
  87.5 0.3 collective-permute-start.9
  87.8 0.0 collective-permute-done.18
  87.8 0.4 add.6.after_ref
  88.2 5.7 %collective-permute-done.9.theirs_ref = bf16[8,16,1024]{2,1,0:T(8,128)(2,1)S(1)} collective-permute-done((bf16[8,16,1024]{2,1,0:T(8,128)(2,1)S(1)}, bf16[8,16,1024]{2,1,0:T(8,128)(2,1)S(1)}, u32[]{:S(2)}, u32[]{:S(2)}) %collective-permute-start.9) | collective-permute-done | bytes 262176 | tf_op jit(solution)/shard_map/ppermute | solution.py:400
  93.9 8.3 %cross.3 = (bf16[2,16,32,512]{3,2,1,0:T(8,128)(2,1)S(1)}, bf16[2,16,32,512]{3,2,1,0:T(8,128)(2,1)S(1)}) custom-call(bf16[8,16,1024]{2,1,0:T(8,128)(2,1)S(1)} %pad_maximum_fusion.mine_ref, bf16[8,16,1024]{2,1,0:T(8,128)(2,1)S(1)} %collective-permute-done.9.theirs_ref, bf16[256,32,128]{2,1,0:T(8,128)(2,1)S(1)} %turn.2.after_ref.low_ref, ...), custom_call_target="tpu_custom_call" | custom-call | bytes 21000000 | tf_op jit(solution)/shard_map/cross/pallas_call | solution.py:31
  102.2 0.0 copy-start.1
  102.2 0.1 collective-permute-start.19
  102.3 0.1 fusion.1
  102.3 1.8 %collective-permute-start.21 = (bf16[1,16,32,512]{3,2,1,0:T(8,128)(2,1)S(1)}, bf16[1,16,32,512]{3,2,1,0:T(8,128)(2,1)S(1)}, u32[]{:S(2)}, u32[]{:S(2)}) collective-permute-start(bf16[1,16,32,512]{3,2,1,0:T(8,128)(2,1)S(1)} %get-tuple-element.51), channel_id=1, source_target_pairs={{0,2},{1,3},{2,0},{3,1},{4,6},{5,7},{6,4},{7,5},{8,10},{9,11},{10,... | collective-permute-start | bytes 1572872 | tf_op jit(solution)/shard_map/ppermute | solution.py:446
  104.1 0.8 collective-permute-done.19
  104.9 0.4 add.7
  105.3 0.1 fusion.2
  105.4 1.8 %collective-permute-start.20 = (bf16[1,16,32,512]{3,2,1,0:T(8,128)(2,1)S(1)}, bf16[1,16,32,512]{3,2,1,0:T(8,128)(2,1)S(1)}, u32[]{:S(2)}, u32[]{:S(2)}) collective-permute-start(bf16[1,16,32,512]{3,2,1,0:T(8,128)(2,1)S(1)} %get-tuple-element.53), channel_id=1, source_target_pairs={{0,2},{1,3},{2,0},{3,1},{4,6},{5,7},{6,4},{7,5},{8,10},{9,11},{10,... | collective-permute-start | bytes 1572872 | tf_op jit(solution)/shard_map/ppermute | solution.py:446
  107.2 10.0 %collective-permute-done.21.came_ref = bf16[1,16,32,512]{3,2,1,0:T(8,128)(2,1)S(1)} collective-permute-done((bf16[1,16,32,512]{3,2,1,0:T(8,128)(2,1)S(1)}, bf16[1,16,32,512]{3,2,1,0:T(8,128)(2,1)S(1)}, u32[]{:S(2)}, u32[]{:S(2)}) %collective-permute-start.21) | collective-permute-done | bytes 524320 | tf_op jit(solution)/shard_map/ppermute | solution.py:446
  117.1 0.0 copy-done.1
  117.1 0.9 unfold.2.rest_0_
  118.0 9.9 %collective-permute-done.20.came_ref = bf16[1,16,32,512]{3,2,1,0:T(8,128)(2,1)S(1)} collective-permute-done((bf16[1,16,32,512]{3,2,1,0:T(8,128)(2,1)S(1)}, bf16[1,16,32,512]{3,2,1,0:T(8,128)(2,1)S(1)}, u32[]{:S(2)}, u32[]{:S(2)}) %collective-permute-start.20) | collective-permute-done | bytes 524320 | tf_op jit(solution)/shard_map/ppermute | solution.py:446
  128.0 1.9 %unfold.3 = bf16[32,32,512]{2,1,0:T(8,128)(2,1)} custom-call(bf16[1,16,32,512]{3,2,1,0:T(8,128)(2,1)S(1)} %get-tuple-element.54.own_ref, bf16[1,16,32,512]{3,2,1,0:T(8,128)(2,1)S(1)} %collective-permute-done.20.came_ref, bf16[512,512]{1,0:T(8,128)(2,1)S(1)} %copy-done.1, bf16[32,16,512]{2,1,0:T(8,128)(2,1)S(1)} %unfold.2.rest_0_), custom_call_target="tpu_custom_call" | custom-call | bytes 4500000 | tf_op jit(solution)/shard_map/unfold/pallas_call | solution.py:31
  (11 shorter events, 0.2 us)
Async XLA Ops:
  1.1 18.6 %collective-permute-start = (bf16[16,1,1024]{2,1,0:T(2,128)(2,1)S(1)}, bf16[16,1,1024]{2,1,0:T(2,128)(2,1)S(1)}, u32[]{:S(2)}, u32[]{:S(2)}) collective-permute-start(bf16[16,1,1024]{2,1,0:T(2,128)(2,1)S(1)} %get-tuple-element.50), channel_id=1, source_target_pairs={{0,4},{4,8},{8,12},{12,16},{16,20},{20,24},{24,28},{28,0},{1,5},{5... | collective-permute-start | bytes 98312 | tf_op jit(solution)/shard_map/ppermute | solution.py:432
  4.1 15.6 %collective-permute-start.1 = (bf16[16,1,1024]{2,1,0:T(2,128)(2,1)S(1)}, bf16[16,1,1024]{2,1,0:T(2,128)(2,1)S(1)}, u32[]{:S(2)}, u32[]{:S(2)}) collective-permute-start(bf16[16,1,1024]{2,1,0:T(2,128)(2,1)S(1)} %get-tuple-element.49), channel_id=1, source_target_pairs={{4,0},{8,4},{12,8},{16,12},{20,16},{24,20},{28,24},{0,28},{5,1},{9... | collective-permute-start | bytes 98312 | tf_op jit(solution)/shard_map/ppermute | solution.py:433
  7.2 2.2 %copy-start = (bf16[16,128,1024]{2,1,0:T(8,128)(2,1)S(1)}, bf16[16,128,1024]{2,1,0:T(8,128)(2,1)}, u32[]{:S(2)}) copy-start(bf16[16,128,1024]{2,1,0:T(8,128)(2,1)} %spec_ref.1) | copy-start | bytes 12582916
  9.4 0.7 copy-start.4
  10.1 0.7 copy-start.5
  21.0 7.8 %collective-permute-start.10 = (bf16[8,16,1024]{2,1,0:T(8,128)(2,1)S(1)}, bf16[8,16,1024]{2,1,0:T(8,128)(2,1)S(1)}, u32[]{:S(2)}, u32[]{:S(2)}) collective-permute-start(bf16[8,16,1024]{2,1,0:T(8,128)(2,1)S(1)} %get-tuple-element.40), channel_id=1, source_target_pairs={{0,4},{4,0},{8,12},{12,8},{16,20},{20,16},{24,28},{28,24},{1,5},{5... | collective-permute-start | bytes 786440 | tf_op jit(solution)/shard_map/ppermute | solution.py:395
  28.8 5.9 %collective-permute-start.11 = (bf16[2,16,1024]{2,1,0:T(8,128)(2,1)S(1)}, bf16[2,16,1024]{2,1,0:T(8,128)(2,1)S(1)}, u32[]{:S(2)}, u32[]{:S(2)}) collective-permute-start(bf16[2,16,1024]{2,1,0:T(8,128)(2,1)S(1)} %get-tuple-element.42), channel_id=1, source_target_pairs={{0,8},{4,12},{8,0},{12,4},{16,24},{20,28},{24,16},{28,20},{1,9},{5... | collective-permute-start | bytes 196616 | tf_op jit(solution)/shard_map/ppermute | solution.py:396
  28.9 5.8 %collective-permute-start.12 = (bf16[2,16,1024]{2,1,0:T(8,128)(2,1)S(1)}, bf16[2,16,1024]{2,1,0:T(8,128)(2,1)S(1)}, u32[]{:S(2)}, u32[]{:S(2)}) collective-permute-start(bf16[2,16,1024]{2,1,0:T(8,128)(2,1)S(1)} %get-tuple-element.43), channel_id=1, source_target_pairs={{0,16},{4,20},{8,24},{12,28},{16,0},{20,4},{24,8},{28,12},{1,17},{... | collective-permute-start | bytes 196616 | tf_op jit(solution)/shard_map/ppermute | solution.py:396
  31.1 21.9 %copy-start.2 = (bf16[272,512]{1,0:T(8,128)(2,1)S(1)}, bf16[272,512]{1,0:T(8,128)(2,1)}, u32[]{:S(2)}) copy-start(bf16[272,512]{1,0:T(8,128)(2,1)} %constant.6.clone.cos_ref) | copy-start | bytes 835588
  31.1 21.9 %copy-start.3 = (bf16[256,512]{1,0:T(8,128)(2,1)S(1)}, bf16[256,512]{1,0:T(8,128)(2,1)}, u32[]{:S(2)}) copy-start(bf16[256,512]{1,0:T(8,128)(2,1)} %constant.7.clone.sin_ref) | copy-start | bytes 786436
  31.1 6.1 %collective-permute-start.13 = (bf16[2,16,1024]{2,1,0:T(8,128)(2,1)S(1)}, bf16[2,16,1024]{2,1,0:T(8,128)(2,1)S(1)}, u32[]{:S(2)}, u32[]{:S(2)}) collective-permute-start(bf16[2,16,1024]{2,1,0:T(8,128)(2,1)S(1)} %get-tuple-element.44), channel_id=1, source_target_pairs={{0,24},{4,28},{8,16},{12,20},{16,8},{20,12},{24,0},{28,4},{1,25},{... | collective-permute-start | bytes 196616 | tf_op jit(solution)/shard_map/ppermute | solution.py:396
  37.2 5.7 %collective-permute-start.14 = (bf16[2,16,1024]{2,1,0:T(8,128)(2,1)S(1)}, bf16[2,16,1024]{2,1,0:T(8,128)(2,1)S(1)}, u32[]{:S(2)}, u32[]{:S(2)}) collective-permute-start(bf16[2,16,1024]{2,1,0:T(8,128)(2,1)S(1)} %add_four.3), channel_id=1, source_target_pairs={{0,8},{4,12},{8,0},{12,4},{16,24},{20,28},{24,16},{28,20},{1,9},{5... | collective-permute-start | bytes 196616 | tf_op jit(solution)/shard_map/ppermute | solution.py:398
  37.3 5.7 %collective-permute-start.15 = (bf16[2,16,1024]{2,1,0:T(8,128)(2,1)S(1)}, bf16[2,16,1024]{2,1,0:T(8,128)(2,1)S(1)}, u32[]{:S(2)}, u32[]{:S(2)}) collective-permute-start(bf16[2,16,1024]{2,1,0:T(8,128)(2,1)S(1)} %add_four.3), channel_id=1, source_target_pairs={{0,16},{4,20},{8,24},{12,28},{16,0},{20,4},{24,8},{28,12},{1,17},{... | collective-permute-start | bytes 196616 | tf_op jit(solution)/shard_map/ppermute | solution.py:398
  40.5 6.1 %collective-permute-start.16 = (bf16[2,16,1024]{2,1,0:T(8,128)(2,1)S(1)}, bf16[2,16,1024]{2,1,0:T(8,128)(2,1)S(1)}, u32[]{:S(2)}, u32[]{:S(2)}) collective-permute-start(bf16[2,16,1024]{2,1,0:T(8,128)(2,1)S(1)} %add_four.3), channel_id=1, source_target_pairs={{0,24},{4,28},{8,16},{12,20},{16,8},{20,12},{24,0},{28,4},{1,25},{... | collective-permute-start | bytes 196616 | tf_op jit(solution)/shard_map/ppermute | solution.py:398
  46.6 6.4 %collective-permute-start.17 = (bf16[8,16,1024]{2,1,0:T(8,128)(2,1)S(1)}, bf16[8,16,1024]{2,1,0:T(8,128)(2,1)S(1)}, u32[]{:S(2)}, u32[]{:S(2)}) collective-permute-start(bf16[8,16,1024]{2,1,0:T(8,128)(2,1)S(1)} %pad_maximum_fusion.1.mine_ref), channel_id=1, source_target_pairs={{0,4},{4,0},{8,12},{12,8},{16,20},{20,16},{24,28},{28,24},{1,5},{5... | collective-permute-start | bytes 786440 | tf_op jit(solution)/shard_map/ppermute | solution.py:400
  61.3 26.5 %collective-permute-start.18 = (bf16[2,16,32,512]{3,2,1,0:T(8,128)(2,1)S(1)}, bf16[2,16,32,512]{3,2,1,0:T(8,128)(2,1)S(1)}, u32[]{:S(2)}, u32[]{:S(2)}) collective-permute-start(bf16[2,16,32,512]{3,2,1,0:T(8,128)(2,1)S(1)} %get-tuple-element.46), channel_id=1, source_target_pairs={{0,1},{1,0},{2,3},{3,2},{4,5},{5,4},{6,7},{7,6},{8,9},{9,8},{10,11... | collective-permute-start | bytes 3145736 | tf_op jit(solution)/shard_map/ppermute | solution.py:444
  61.3 8.7 %collective-permute-start.2 = (bf16[8,16,1024]{2,1,0:T(8,128)(2,1)S(1)}, bf16[8,16,1024]{2,1,0:T(8,128)(2,1)S(1)}, u32[]{:S(2)}, u32[]{:S(2)}) collective-permute-start(bf16[8,16,1024]{2,1,0:T(8,128)(2,1)S(1)} %get-tuple-element.32), channel_id=1, source_target_pairs={{0,4},{4,0},{8,12},{12,8},{16,20},{20,16},{24,28},{28,24},{1,5},{5... | collective-permute-start | bytes 786440 | tf_op jit(solution)/shard_map/ppermute | solution.py:395
  70.1 4.7 %collective-permute-start.3 = (bf16[2,16,1024]{2,1,0:T(8,128)(2,1)S(1)}, bf16[2,16,1024]{2,1,0:T(8,128)(2,1)S(1)}, u32[]{:S(2)}, u32[]{:S(2)}) collective-permute-start(bf16[2,16,1024]{2,1,0:T(8,128)(2,1)S(1)} %get-tuple-element.36), channel_id=1, source_target_pairs={{0,8},{4,12},{8,0},{12,4},{16,24},{20,28},{24,16},{28,20},{1,9},{5... | collective-permute-start | bytes 196616 | tf_op jit(solution)/shard_map/ppermute | solution.py:396
  70.2 8.1 %collective-permute-start.4 = (bf16[2,16,1024]{2,1,0:T(8,128)(2,1)S(1)}, bf16[2,16,1024]{2,1,0:T(8,128)(2,1)S(1)}, u32[]{:S(2)}, u32[]{:S(2)}) collective-permute-start(bf16[2,16,1024]{2,1,0:T(8,128)(2,1)S(1)} %get-tuple-element.37), channel_id=1, source_target_pairs={{0,16},{4,20},{8,24},{12,28},{16,0},{20,4},{24,8},{28,12},{1,17},{... | collective-permute-start | bytes 196616 | tf_op jit(solution)/shard_map/ppermute | solution.py:396
  72.0 6.3 %collective-permute-start.5 = (bf16[2,16,1024]{2,1,0:T(8,128)(2,1)S(1)}, bf16[2,16,1024]{2,1,0:T(8,128)(2,1)S(1)}, u32[]{:S(2)}, u32[]{:S(2)}) collective-permute-start(bf16[2,16,1024]{2,1,0:T(8,128)(2,1)S(1)} %get-tuple-element.38), channel_id=1, source_target_pairs={{0,24},{4,28},{8,16},{12,20},{16,8},{20,12},{24,0},{28,4},{1,25},{... | collective-permute-start | bytes 196616 | tf_op jit(solution)/shard_map/ppermute | solution.py:396
  78.3 4.6 %collective-permute-start.6 = (bf16[2,16,1024]{2,1,0:T(8,128)(2,1)S(1)}, bf16[2,16,1024]{2,1,0:T(8,128)(2,1)S(1)}, u32[]{:S(2)}, u32[]{:S(2)}) collective-permute-start(bf16[2,16,1024]{2,1,0:T(8,128)(2,1)S(1)} %add_four.2), channel_id=1, source_target_pairs={{0,8},{4,12},{8,0},{12,4},{16,24},{20,28},{24,16},{28,20},{1,9},{5... | collective-permute-start | bytes 196616 | tf_op jit(solution)/shard_map/ppermute | solution.py:398
  79.7 6.0 %collective-permute-start.7 = (bf16[2,16,1024]{2,1,0:T(8,128)(2,1)S(1)}, bf16[2,16,1024]{2,1,0:T(8,128)(2,1)S(1)}, u32[]{:S(2)}, u32[]{:S(2)}) collective-permute-start(bf16[2,16,1024]{2,1,0:T(8,128)(2,1)S(1)} %add_four.2), channel_id=1, source_target_pairs={{0,16},{4,20},{8,24},{12,28},{16,0},{20,4},{24,8},{28,12},{1,17},{... | collective-permute-start | bytes 196616 | tf_op jit(solution)/shard_map/ppermute | solution.py:398
  81.4 6.1 %collective-permute-start.8 = (bf16[2,16,1024]{2,1,0:T(8,128)(2,1)S(1)}, bf16[2,16,1024]{2,1,0:T(8,128)(2,1)S(1)}, u32[]{:S(2)}, u32[]{:S(2)}) collective-permute-start(bf16[2,16,1024]{2,1,0:T(8,128)(2,1)S(1)} %add_four.2), channel_id=1, source_target_pairs={{0,24},{4,28},{8,16},{12,20},{16,8},{20,12},{24,0},{28,4},{1,25},{... | collective-permute-start | bytes 196616 | tf_op jit(solution)/shard_map/ppermute | solution.py:398
  87.5 6.4 %collective-permute-start.9 = (bf16[8,16,1024]{2,1,0:T(8,128)(2,1)S(1)}, bf16[8,16,1024]{2,1,0:T(8,128)(2,1)S(1)}, u32[]{:S(2)}, u32[]{:S(2)}) collective-permute-start(bf16[8,16,1024]{2,1,0:T(8,128)(2,1)S(1)} %pad_maximum_fusion.mine_ref), channel_id=1, source_target_pairs={{0,4},{4,0},{8,12},{12,8},{16,20},{20,16},{24,28},{28,24},{1,5},{5... | collective-permute-start | bytes 786440 | tf_op jit(solution)/shard_map/ppermute | solution.py:400
  102.2 15.0 %copy-start.1 = (bf16[512,512]{1,0:T(8,128)(2,1)S(1)}, bf16[512,512]{1,0:T(8,128)(2,1)}, u32[]{:S(2)}) copy-start(bf16[512,512]{1,0:T(8,128)(2,1)} %constant.8.clone.mix_ref) | copy-start | bytes 1572868
  102.2 2.7 %collective-permute-start.19 = (bf16[2,16,32,512]{3,2,1,0:T(8,128)(2,1)S(1)}, bf16[2,16,32,512]{3,2,1,0:T(8,128)(2,1)S(1)}, u32[]{:S(2)}, u32[]{:S(2)}) collective-permute-start(bf16[2,16,32,512]{3,2,1,0:T(8,128)(2,1)S(1)} %get-tuple-element.48), channel_id=1, source_target_pairs={{0,1},{1,0},{2,3},{3,2},{4,5},{5,4},{6,7},{7,6},{8,9},{9,8},{10,11... | collective-permute-start | bytes 3145736 | tf_op jit(solution)/shard_map/ppermute | solution.py:444
  102.3 14.8 %collective-permute-start.21 = (bf16[1,16,32,512]{3,2,1,0:T(8,128)(2,1)S(1)}, bf16[1,16,32,512]{3,2,1,0:T(8,128)(2,1)S(1)}, u32[]{:S(2)}, u32[]{:S(2)}) collective-permute-start(bf16[1,16,32,512]{3,2,1,0:T(8,128)(2,1)S(1)} %get-tuple-element.51), channel_id=1, source_target_pairs={{0,2},{1,3},{2,0},{3,1},{4,6},{5,7},{6,4},{7,5},{8,10},{9,11},{10,... | collective-permute-start | bytes 1572872 | tf_op jit(solution)/shard_map/ppermute | solution.py:446
  105.4 22.6 %collective-permute-start.20 = (bf16[1,16,32,512]{3,2,1,0:T(8,128)(2,1)S(1)}, bf16[1,16,32,512]{3,2,1,0:T(8,128)(2,1)S(1)}, u32[]{:S(2)}, u32[]{:S(2)}) collective-permute-start(bf16[1,16,32,512]{3,2,1,0:T(8,128)(2,1)S(1)} %get-tuple-element.53), channel_id=1, source_target_pairs={{0,2},{1,3},{2,0},{3,1},{4,6},{5,7},{6,4},{7,5},{8,10},{9,11},{10,... | collective-permute-start | bytes 1572872 | tf_op jit(solution)/shard_map/ppermute | solution.py:446

commit v3 on v2

v3 whole, which is shorter than its diff:
```python
import functools
import math

import jax
import jax.numpy as jnp
import ml_dtypes
import numpy as np
from jax import lax
from jax.experimental import pallas as pl
from jax.experimental.pallas import tpu as pltpu
from jax.sharding import PartitionSpec as P

LAGS = 512
SMOOTH = 21
EPSILON = 1e-06
CHUNKS = 2
LANES = 128
F32 = jnp.float32
BF16 = jnp.bfloat16
MIB = 1024 * 1024
SMEM = pl.BlockSpec(memory_space=pltpu.SMEM)
VMEM = pl.BlockSpec(memory_space=pltpu.VMEM)
ANY = pl.BlockSpec(memory_space=pl.ANY)
HBM = pl.BlockSpec(memory_space=pltpu.HBM)


def call(kernel, ins, in_specs, outs, scratch, limit, name, after=()):
    count = len(ins)

    def body(*refs):
        kernel(*refs[:count], *refs[count + len(after) :])

    return pl.pallas_call(
        body,
        in_specs=[*in_specs] + [ANY] * len(after),
        out_specs=[VMEM] * len(outs),
        out_shape=[jax.ShapeDtypeStruct(shape, dtype) for shape, dtype in outs],
        scratch_shapes=scratch,
        compiler_params=pltpu.CompilerParams(vmem_limit_bytes=limit * MIB),
        cost_estimate=pl.CostEstimate(flops=0, bytes_accessed=16, transcendentals=0),
        name=name,
    )(*ins, *after)


def xor_pairs(count, mask):
    return [(i, i ^ mask) for i in range(count)]


def place(blocks):
    if blocks != 8:
        return 0, 0
    at = lax.axis_index("chan")
    return at % 2, at // 2


def source_at(blocks, r, per_chunk):
    x, z = place(blocks)
    quarter = per_chunk // 8
    chunk, r = divmod(r, per_chunk)
    half, r = divmod(r, 4 * quarter)
    part, i = divmod(r, quarter)
    return chunk * per_chunk + (x ^ half) * 4 * quarter + (z ^ part) * quarter + i


def amplitude(values):
    freqs = values.shape[-1] // 2
    real, imag = values[:, :freqs], values[:, freqs:]
    square = real * real + imag * imag
    return square * lax.rsqrt(jnp.maximum(square, 1e-36))


def bin_share(freqs):
    f = lax.broadcasted_iota(jnp.int32, (1, freqs), 1)
    entries = jnp.minimum(f, SMOOTH) + jnp.minimum(freqs - 1 - f, SMOOTH) + 1
    return 1.0 / (3.0 * entries.astype(F32))


def inverse_divisor(triple, band, share):
    divisor = jnp.dot(triple, band, preferred_element_type=F32) * share + EPSILON
    near = pl.reciprocal(divisor, approx=True)
    return near * (2.0 - divisor * near)


def whiten_kernel(spec_ref, white_ref, band, part_ref, raw_ref, buf, tri, inv, sems):
    windows, chans, width = buf.shape
    freqs = width // 2
    pitch = chans + 8
    together = tri.shape[0] // chans

    def fetch(w):
        return pltpu.make_async_copy(spec_ref.at[w], buf.at[w], sems.at[w])

    for w in range(windows):
        fetch(w).start()
    row = lax.broadcasted_iota(jnp.int32, (freqs, freqs), 0)
    col = lax.broadcasted_iota(jnp.int32, (freqs, freqs), 1)
    band[...] = jnp.where(jnp.abs(row - col) <= SMOOTH, 1.0, 0.0).astype(BF16)
    share = bin_share(freqs)

    def some(i, carry):
        for k in range(together):
            w = i * together + k
            fetch(w).wait()
            values = buf[w].astype(F32)
            magnitude = amplitude(values)
            triple = pltpu.roll(magnitude, 1, 0) + magnitude + pltpu.roll(magnitude, chans - 1, 0)
            tri[k * chans : (k + 1) * chans, :] = triple.astype(BF16)
            part_ref[0, pl.ds(w, 1), :] = magnitude[0:1] + magnitude[1:2]
            part_ref[1, pl.ds(w, 1), :] = magnitude[chans - 2 : chans - 1] + magnitude[chans - 1 :]
            raw_ref[0, pl.ds(w, 1), :] = values[0:1]
            raw_ref[1, pl.ds(w, 1), :] = values[chans - 1 :]
        inv[...] = inverse_divisor(tri[...], band[...], share)
        for k in range(together):
            w = i * together + k
            at = pl.multiple_of(w * pitch, 8)
            for j in range(width // LANES):
                values = buf[w, :, j * LANES : (j + 1) * LANES].astype(F32)
                first = j * LANES % freqs
                factor = inv[k * chans : (k + 1) * chans, first : first + LANES]
                white_ref[j, pl.ds(at, chans), :] = values * factor
        return carry

    lax.fori_loop(0, windows // together, some, 0)


def whiten(spectra):
    windows, chans, width = spectra.shape
    freqs = width // 2
    together = 4
    return call(
        whiten_kernel,
        (spectra,),
        [HBM],
        [
            ((width // LANES, windows * (chans + 8), LANES), F32),
            ((freqs, freqs), BF16),
            ((2, windows, freqs), F32),
            ((2, windows, width), F32),
        ],
        [
            pltpu.VMEM(spectra.shape, BF16),
            pltpu.VMEM((together * chans, freqs), BF16),
            pltpu.VMEM((together * chans, freqs), F32),
            pltpu.SemaphoreType.DMA((windows,)),
        ],
        28,
        "whiten",
    )


def edges_kernel(blocks, chans, src_ref, valid_ref, low_ref, high_ref, white_ref, band, part_ref, raw_ref, *outs):
    picks, edge_ref = outs[:-1], outs[-1]
    windows, width = raw_ref.shape[1:]
    freqs = width // 2
    sources = src_ref.shape[0]
    pitch = chans + 8
    share = bin_share(freqs)
    row = lax.broadcasted_iota(jnp.int32, (windows, 1), 0)
    valid = jnp.zeros((windows, 1), F32)
    for w in range(windows):
        valid = valid + jnp.where(row == w, valid_ref[w].astype(F32), 0.0)
    for k, ref in enumerate((low_ref, high_ref)):
        beside = jnp.concatenate([ref[w] for w in range(windows)], axis=0).astype(F32)
        triple = (part_ref[k] + amplitude(beside)).astype(BF16)
        inverse = inverse_divisor(triple, band[...], share)
        edge_ref[k] = raw_ref[k] * jnp.concatenate([inverse, inverse], axis=1)
    offset = lax.axis_index("chan") * chans
    rows = picks[0].shape[0]
    for r in range(sources):
        at = src_ref[source_at(blocks, r, sources // CHUNKS)] - offset
        inner = valid * ((at > 0) & (at < chans - 1)).astype(F32)
        first = valid * (at == 0).astype(F32)
        last = valid * (at == chans - 1).astype(F32)
        row_at = jnp.clip(at, 0, chans - 1)
        for j in range(width // LANES):
            lanes = slice(j * LANES, (j + 1) * LANES)
            value = inner * white_ref[j, pl.ds(row_at, windows, stride=pitch), :]
            value = value + first * edge_ref[0, :, lanes] + last * edge_ref[1, :, lanes]
            picks[r // rows][r % rows, :, lanes] = value.astype(BF16)


def edges(blocks, chans, valid, sources, low, high, white, band, part, raw):
    _, windows, width = raw.shape
    rows = sources.shape[0] // CHUNKS // 2
    return call(
        functools.partial(edges_kernel, blocks, chans),
        (sources, valid, low, high, white, band, part, raw),
        [SMEM, SMEM] + [VMEM] * 6,
        [((rows, windows, width), BF16)] * (2 * CHUNKS) + [(raw.shape, F32)],
        [],
        8,
        "edges",
    )


def turn_kernel(first, white_ref, edge_ref, out_ref, held):
    _, windows, width = edge_ref.shape
    chans = out_ref.shape[-1]
    tile = LANES
    pitch = 2 * windows + 8
    row = lax.broadcasted_iota(jnp.int32, (8, tile), 0)
    for block in range(out_ref.shape[0] // tile):
        for w in range(windows):
            for half in range(2):
                j = half * (width // 2 // tile) + first + block
                lanes = slice(j * tile, (j + 1) * tile)
                at = w * (chans + 8)
                body = white_ref[j, at : at + chans, :]
                top = jnp.where(row == 0, edge_ref[0, w : w + 1, lanes], body[:8])
                bottom = jnp.where(row == 7, edge_ref[1, w : w + 1, lanes], body[chans - 8 :])
                body = jnp.concatenate([top, body[8 : chans - 8], bottom], axis=0)
                held[pl.ds(half * windows + w, tile, stride=pitch), :] = body.T
        for f in range(tile):
            out_ref[block * tile + f] = held[f * pitch : f * pitch + 2 * windows, :].astype(BF16)


def turn(white, edge, chans, first, tiles):
    _, windows, width = edge.shape
    return call(
        functools.partial(turn_kernel, first),
        (white, edge),
        [VMEM, VMEM],
        [((tiles * LANES, 2 * windows, chans), BF16)],
        [pltpu.VMEM((LANES * (2 * windows + 8), chans), F32)],
        16,
        "turn",
    )[0]


def add_parts_kernel(keep_ref, came_ref, *outs):
    rows = outs[0].shape[0]
    for p, out in enumerate(outs):
        out[...] = keep_ref[p * rows : (p + 1) * rows] + came_ref[p * rows : (p + 1) * rows]


def add_parts(keep, came, after):
    rows, windows, width = keep.shape
    shape = (rows // 4, windows, width)
    return call(add_parts_kernel, (keep, came), [VMEM] * 2, [(shape, BF16)] * 4, [], 8, "add_parts", after)


def own_first_kernel(a_ref, b_ref, c_ref, d_ref, *refs):
    nexts, outs = refs[:3], refs[3:]
    rows = a_ref.shape[0]
    own = a_ref[...] + b_ref[...] + c_ref[...] + d_ref[...]
    for ref, out in zip(nexts, outs):
        out[:rows] = own
        out[rows:] = ref[...]


def own_first(pieces, nexts, after):
    rows, windows, width = pieces[0].shape
    return call(
        own_first_kernel,
        (*pieces, *nexts),
        [VMEM] * 7,
        [((2 * rows, windows, width), BF16)] * 3,
        [],
        8,
        "own_first",
        after,
    )


def part_kernel(sent_ref, b_ref, c_ref, d_ref, piece_ref, mine_ref, own_ref):
    rows = piece_ref.shape[0]
    for p, ref in enumerate((sent_ref, b_ref, c_ref, d_ref)):
        mine_ref[p * rows : (p + 1) * rows] = ref[:rows]
    own_ref[...] = piece_ref[...] + b_ref[rows:] + c_ref[rows:] + d_ref[rows:]


def part(sent, came, piece):
    rows, windows, width = piece.shape
    outs = [((4 * rows, windows, width), BF16), (piece.shape, BF16)]
    return call(part_kernel, (sent, *came, piece), [VMEM] * 5, outs, [], 8, "part")


def add_pair_kernel(keep_ref, *refs):
    out, rows = refs[-1], refs[0].shape[0]
    for k, ref in enumerate(refs[:-1]):
        at = slice(k * rows, (k + 1) * rows)
        out[at] = (keep_ref[at].astype(F32) + ref[...].astype(F32)).astype(BF16)


def add_pair(keep, came, after):
    ins = (keep, *came)
    return call(add_pair_kernel, ins, [VMEM] * len(ins), [(keep.shape, BF16)], [], 8, "add_pair", after)[0]


def bins_kernel(rows_ref, low_ref, high_ref, st, vt):
    rows, windows, width = rows_ref.shape
    held_freqs, depth, chans = low_ref.shape
    freqs = width // 2
    tile = LANES
    group = tile // depth
    for g in range(rows // group):
        pieces = []
        for s in range(g * group, (g + 1) * group):
            v = rows_ref[s].astype(F32)
            pieces += [v[:, :freqs], v[:, freqs:]]
        stack = jnp.concatenate(pieces, axis=0)
        for j in range(freqs // tile):
            t = stack[:, j * tile : (j + 1) * tile].T
            for i in range(group):
                moved = t if i == 0 else pltpu.roll(t, tile - i * depth, 1)
                vt[pl.ds(j * tile * rows + g * group + i, tile, stride=rows), :] = moved

    unroll = 128
    for which, ref in enumerate((low_ref, high_ref)):

        def step(i, carry):
            for k in range(unroll):
                f = i * unroll + k
                at = pl.multiple_of((which * held_freqs + f) * rows, 8)
                lhs = vt[pl.ds(at, rows), 0:depth].astype(BF16)
                x = ref[f]
                crossed = jnp.concatenate([x[windows:], -x[:windows]], axis=0)
                sums = jnp.dot(lhs, jnp.concatenate([x, crossed], axis=1), preferred_element_type=F32)
                st[0, pl.ds(at, rows), :] = sums[:, :chans]
                st[1, pl.ds(at, rows), :] = sums[:, chans:]
            return carry

        lax.fori_loop(0, held_freqs // unroll, step, 0)


def bins(rows, turned, after):
    count, windows, width = rows.shape
    held = width // 2 * count
    return call(
        bins_kernel,
        (rows, *turned),
        [VMEM] * 3,
        [((2, held, turned[0].shape[-1]), F32)],
        [pltpu.VMEM((held, LANES), F32)],
        8,
        "bins",
        after,
    )[0]


def lags_kernel(parts, st, cos_ref, sin_ref, *outs):
    rows = outs[0].shape[0]
    chans = st.shape[-1]
    freqs = st.shape[1] // rows
    me = lax.axis_index("win")
    share = chans // parts
    half = sin_ref.shape[0]
    last_row = lax.broadcasted_iota(jnp.int32, (8, 1), 0) == 7

    def transform(p, carry):
        real, imag = [
            jnp.concatenate([st[i, pl.ds(2 * p + k, freqs, stride=rows), :].astype(BF16) for k in (0, 1)], axis=1)
            for i in (0, 1)
        ]
        even = jnp.dot(cos_ref[...], real, preferred_element_type=F32)
        odd = jnp.dot(sin_ref[...], imag, preferred_element_type=F32)
        tail = odd[half - 8 :] + jnp.where(last_row, even[half : half + 1], 0.0)
        out = jnp.concatenate([even[:half], odd[: half - 8], tail], axis=0)
        for k in range(2):
            flat = out[:, k * chans : (k + 1) * chans].T.astype(BF16)
            for b in range(parts):
                value = flat[b * share : (b + 1) * share, :]
                for slot, to in enumerate(outs):

                    @pl.when(b ^ me == slot)
                    def _():
                        to[2 * p + k] = value

        return carry

    lax.fori_loop(0, rows // 2, transform, 0)


def lags(parts, rows, sums, tables, after):
    chans = sums.shape[-1]
    shape = (rows, chans // parts, LAGS)
    return call(
        functools.partial(lags_kernel, parts),
        (sums, *tables),
        [VMEM] * 3,
        [(shape, BF16)] * parts,
        [],
        8,
        "lags",
        after,
    )


def unfold_kernel(blocks, pairs, *refs):
    ins, mix_ref, earlier, (out_ref, held) = refs[: 3 * pairs], refs[3 * pairs], refs[3 * pairs + 1 : -2], refs[-2:]
    rows, chans, lags = ins[0].shape
    per_chunk = pairs * rows
    pitch = per_chunk + 8
    for pair in range(pairs):
        total = jnp.zeros((rows * chans, lags), F32)
        stay, near, far = [ref[...].reshape(rows * chans, lags) for ref in ins[3 * pair : 3 * pair + 3]]
        near = (stay.astype(F32) + near.astype(F32)).astype(BF16)
        for flat in (near, far):
            total = total + jnp.dot(flat, mix_ref[...], preferred_element_type=F32)
        for r in range(rows):
            at = source_at(blocks, pair * rows + r, per_chunk)
            for j in range(lags // LANES):
                lanes = slice(j * LANES, (j + 1) * LANES)
                held[j, pl.ds(at, chans, stride=pitch), :] = total[r * chans : (r + 1) * chans, lanes]
    first = out_ref.shape[1] - per_chunk
    for c in range(chans):
        if earlier:
            out_ref[c, :first, :] = earlier[0][c]
        for j in range(lags // LANES):
            lanes = slice(j * LANES, (j + 1) * LANES)
            out_ref[c, first:, lanes] = held[j, c * pitch : c * pitch + per_chunk, :].astype(BF16)


def unfold(blocks, ins, mix, earlier):
    rows, chans, lags = ins[0].shape
    per_chunk = len(ins) // 3 * rows
    return call(
        functools.partial(unfold_kernel, blocks, len(ins) // 3),
        (*ins, mix, *earlier),
        [VMEM] * (len(ins) + 1 + len(earlier)),
        [((chans, per_chunk * (1 + len(earlier)), lags), BF16)],
        [pltpu.VMEM((lags // LANES, chans * (per_chunk + 8), LANES), F32)],
        16,
        "unfold",
    )[0]


def meet_x(keep, send, after):
    return add_parts(keep, lax.ppermute(send, "chan", xor_pairs(8, 1)), after)


def over_z(arrays):
    return [lax.ppermute(array, "chan", xor_pairs(8, 2 * p)) for p, array in zip((1, 2, 3), arrays)]


def spread(blocks, picks, turned):
    if blocks != 8:
        return [lax.psum(pick, "chan") for pick in picks]
    pieces_a = meet_x(picks[0], picks[1], turned[:1])
    pieces_b = meet_x(picks[2], picks[3], ())
    sent = own_first([pieces_a[0]] + over_z(pieces_a[1:]), pieces_b[1:], turned[1:])
    mine_a, own_b = part(sent[0], over_z(sent), pieces_b[0])
    theirs_a = lax.ppermute(mine_a, "chan", xor_pairs(8, 1))
    mine_b = jnp.concatenate([own_b] + over_z([own_b] * 3), axis=0)
    return mine_a, theirs_a, mine_b, lax.ppermute(mine_b, "chan", xor_pairs(8, 1))


def lag_tables(freqs, windows):
    half = LAGS // 2
    f = np.arange(freqs)[None, :]
    scale = np.where(f == 0, 1.0, 2.0) * 0.25 / math.sqrt(freqs * windows)
    u = np.arange(half + 16)[:, None]
    cos = np.where(u <= half, scale * np.cos(math.pi * (f * u % (2 * freqs)) / freqs), 0.0)
    u = np.arange(1, half + 1)[:, None]
    sin = -scale * np.sin(math.pi * (f * u % (2 * freqs)) / freqs) * np.where(u == half, -1.0, 1.0)
    return jnp.asarray(cos.astype(ml_dtypes.bfloat16)), jnp.asarray(sin.astype(ml_dtypes.bfloat16))


def lag_mix():
    half = LAGS // 2
    mix = np.zeros((LAGS, LAGS))
    u = np.arange(half)
    mix[u, half + u] = 1
    u = np.arange(1, half)
    mix[u, half - u] = 1
    mix[half - 1 + u, half + u] = 1
    mix[half - 1 + u, half - u] = -1
    mix[LAGS - 1, 0] = 1
    return jnp.asarray(mix.astype(ml_dtypes.bfloat16))


def on_device(blocks, parts, spectra, valid, sources):
    windows, chans, width = spectra.shape
    freqs = width // 2
    forward = [(i, (i + 1) % blocks) for i in range(blocks)]
    backward = [(b, a) for a, b in forward]
    low = lax.ppermute(spectra[:, chans - 1 :, :], "chan", forward)
    high = lax.ppermute(spectra[:, :1, :], "chan", backward)
    white, band, part, raw = whiten(spectra)
    *picks, edge = edges(blocks, chans, valid, sources, low, high, white, band, part, raw)
    tables = lag_tables(freqs, windows)
    mix = lag_mix()
    tiles = freqs // LANES // 2
    turned = [turn(white, edge, chans, i * tiles, tiles) for i in range(2)]
    mine_a, theirs_a, mine_b, theirs_b = spread(blocks, picks, turned)

    def near(send):
        return lax.ppermute(send, "win", xor_pairs(parts, 1))

    def far(leave):
        return lax.ppermute(leave, "win", xor_pairs(parts, 2))

    pairs, cames, waiting = [], [], []

    def send_far(after):
        leave, came = waiting.pop()
        cames.append(far(add_pair(leave, came, after)))

    for i, rows in enumerate((mine_a, theirs_a, mine_b, theirs_b)):
        sums = bins(rows, turned, ())
        after = [mine_b, theirs_a] if i == 0 else cames[i - 2 : i - 1] if i > 1 else []
        stay, send_stay, leave, send_leave = lags(parts, rows.shape[0], sums, tables, after)
        half = rows.shape[0] // 2
        waiting.append((leave, [near(send_leave[:half]), near(send_leave[half:])]))
        send_far(cames[2:3])
        pairs += [(stay, near(send_stay))]
    pairs = [array for (stay, came), far_came in zip(pairs, cames) for array in (stay, came, far_came)]
    first = unfold(blocks, pairs[:6], mix, ())
    return unfold(blocks, pairs[6:], mix, (first,))


def solution(mesh):
    return jax.shard_map(
        functools.partial(on_device, mesh.shape["chan"], mesh.shape["win"]),
        mesh=mesh,
        in_specs=(P("win", "chan", None), P("win"), P()),
        out_specs=P(("chan", "win"), None, None),
        check_vma=False,
    )
```

time: 130 us -> 99.6 us (0.77)
  waiting for transfers between devices: 63.4 us -> 30.2 us
  starting transfers between devices: 28.2 us -> 33.1 us
  local copies, waits for them, and re-layouts: 4.79 us -> 3.47 us
    ppermute x20 -> x29, waiting for transfers between devices: 63.4 us -> 30.2 us  [the longest x9 12.4 us: over_z(): lax.ppermute(array, 'chan', xor_pairs(8, 2 * p))]
    ppermute x20 -> x29, starting transfers between devices: 22.1 us -> 27 us  [the longest x9 13.4 us: over_z(): lax.ppermute(array, 'chan', xor_pairs(8, 2 * p))]
    unnamed x12 -> x15, local copies, waits for them, and re-layouts: 3.51 us -> 2.23 us
    pallas_call x12 -> x22, Pallas kernels: 32.4 us -> 32.2 us  [call(): pl.pallas_call(body, in_specs=[*in_specs] + [ANY] * len(after), out_specs...]
  transfers between devices with their start and end apart: 22 -> 31, of which waited for: 15 -> 11; matrix products, arithmetic and copies ran while one was open for 1% -> 0% of each run, Pallas kernels for 10% -> 26%
where the time goes in v3:
time: 99.6 us; the launch traced here: 99.4 us
  starting transfers between devices  33.1 us (33%)
  Pallas kernels  32.2 us (32%)
  waiting for transfers between devices  30.2 us (30%)
  local copies, waits for them, and re-layouts  3.47 us (3%)
    pallas_call x22, Pallas kernels, call(): pl.pallas_call(body, in_specs=[*in_specs] + [ANY] * len(after), out_specs...  32.2 us
    ppermute x9, starting transfers between devices, over_z(): lax.ppermute(array, 'chan', xor_pairs(8, 2 * p))  13.4 us
    ppermute x9, waiting for transfers between devices, over_z(): lax.ppermute(array, 'chan', xor_pairs(8, 2 * p))  12.4 us
    ppermute x4, waiting for transfers between devices, far(): return lax.ppermute(leave, 'win', xor_pairs(parts, 2))  11.7 us
    ppermute x4, starting transfers between devices, far(): return lax.ppermute(leave, 'win', xor_pairs(parts, 2))  6.11 us
    ppermute x2, waiting for transfers between devices, meet_x(): return add_parts(keep, lax.ppermute(send, 'chan', xor_pairs(8, 1)), after)  5.68 us
    ppermute x12, starting transfers between devices, near(): return lax.ppermute(send, 'win', xor_pairs(parts, 1))  3.26 us
    ppermute x1, starting transfers between devices, on_device(): high = lax.ppermute(spectra[:, :1, :], 'chan', backward)  3.1 us
  transfers between devices with their start and end apart: 31, of which 11 were waited for; matrix products, arithmetic and copies ran while one was open for 0% of the time, Pallas kernels for 26%

profile of v3, /device:TPU:0, one launch (start us, length us, event | category | flops | bytes accessed | tf_op | source)
XLA Modules:
  0.0 99.4 jit_solution(1277187094175305129)
XLA Ops:
  0.0 1.2 %fusion = (bf16[16,1,1024]{2,1,0:T(2,128)(2,1)S(1)}, bf16[16,1,1024]{2,1,0:T(2,128)(2,1)S(1)}) fusion(bf16[16,128,1024]{2,1,0:T(8,128)(2,1)} %refs_0_.2), kind=kLoop, calls=%fused_computation.4 | loop fusion | bytes 131072 | tf_op jit(solution)/shard_map/slice | solution.py:478
  1.2 3.0 %collective-permute-start = (bf16[16,1,1024]{2,1,0:T(2,128)(2,1)S(1)}, bf16[16,1,1024]{2,1,0:T(2,128)(2,1)S(1)}, u32[]{:S(2)}, u32[]{:S(2)}) collective-permute-start(bf16[16,1,1024]{2,1,0:T(2,128)(2,1)S(1)} %get-tuple-element.82), channel_id=1, source_target_pairs={{0,4},{4,8},{8,12},{12,16},{16,20},{20,24},{24,28},{28,0},{1,5},{5... | collective-permute-start | bytes 98312 | tf_op jit(solution)/shard_map/ppermute | solution.py:477
  4.2 3.1 %collective-permute-start.1 = (bf16[16,1,1024]{2,1,0:T(2,128)(2,1)S(1)}, bf16[16,1,1024]{2,1,0:T(2,128)(2,1)S(1)}, u32[]{:S(2)}, u32[]{:S(2)}) collective-permute-start(bf16[16,1,1024]{2,1,0:T(2,128)(2,1)S(1)} %get-tuple-element.81), channel_id=1, source_target_pairs={{4,0},{8,4},{12,8},{16,12},{20,16},{24,20},{28,24},{0,28},{5,1},{9... | collective-permute-start | bytes 98312 | tf_op jit(solution)/shard_map/ppermute | solution.py:478
  7.3 2.2 %copy-done = bf16[16,128,1024]{2,1,0:T(8,128)(2,1)S(1)} copy-done((bf16[16,128,1024]{2,1,0:T(8,128)(2,1)S(1)}, bf16[16,128,1024]{2,1,0:T(8,128)(2,1)}, u32[]{:S(2)}) %copy-start) | copy-done | bytes 4194328
  9.5 4.9 %whiten.1 = (f32[8,2176,128]{2,1,0:T(8,128)S(1)}, bf16[512,512]{1,0:T(8,128)(2,1)S(1)}, f32[2,16,512]{2,1,0:T(8,128)S(1)}, f32[2,16,1024]{2,1,0:T(8,128)S(1)}) custom-call(bf16[16,128,1024]{2,1,0:T(8,128)(2,1)S(1)} %copy-done), custom_call_target="tpu_custom_call" | custom-call | bytes 16 | tf_op jit(solution)/shard_map/whiten/pallas_call | solution.py:33
  14.4 1.7 %edges.1 = (bf16[8,16,1024]{2,1,0:T(8,128)(2,1)S(1)}, bf16[8,16,1024]{2,1,0:T(8,128)(2,1)S(1)}, bf16[8,16,1024]{2,1,0:T(8,128)(2,1)S(1)}, bf16[8,16,1024]{2,1,0:T(8,128)(2,1)S(1)}, f32[2,16,1024]{2,1,0:T(8,128)S(1)}) custom-call(s32[32]{0:T(128)S(1)} %copy-done.4, s32[16]{0:T(128)S(1)} %copy-done.5, bf16[16,1,1024]{2,1,0:T(2,128)(2,1)S(1)} %collective-permute-done.refs_2_, ...), custom_call_target="tpu_custom_call" | custom-call | bytes 16 | tf_op jit(solution)/shard_map/edges/pallas_call | solution.py:33
  16.1 0.1 collective-permute-start.2
  16.2 2.0 %collective-permute-start.6 = (bf16[8,16,1024]{2,1,0:T(8,128)(2,1)S(1)}, bf16[8,16,1024]{2,1,0:T(8,128)(2,1)S(1)}, u32[]{:S(2)}, u32[]{:S(2)}) collective-permute-start(bf16[8,16,1024]{2,1,0:T(8,128)(2,1)S(1)} %get-tuple-element.55), channel_id=1, source_target_pairs={{0,4},{4,0},{8,12},{12,8},{16,20},{20,16},{24,28},{28,24},{1,5},{5... | collective-permute-start | bytes 786440 | tf_op jit(solution)/shard_map/ppermute | solution.py:429
  18.2 1.5 %turn.2.refs_2_.refs_1_ = bf16[256,32,128]{2,1,0:T(8,128)(2,1)S(1)} custom-call(f32[8,2176,128]{2,1,0:T(8,128)S(1)} %get-tuple-element.43.refs_4_.refs_0_, f32[2,16,1024]{2,1,0:T(8,128)S(1)} %get-tuple-element.49.refs_1_), custom_call_target="tpu_custom_call" | custom-call | bytes 16 | tf_op jit(solution)/shard_map/turn/pallas_call | solution.py:33
  19.8 5.7 %collective-permute-done.2.refs_1_ = bf16[8,16,1024]{2,1,0:T(8,128)(2,1)S(1)} collective-permute-done((bf16[8,16,1024]{2,1,0:T(8,128)(2,1)S(1)}, bf16[8,16,1024]{2,1,0:T(8,128)(2,1)S(1)}, u32[]{:S(2)}, u32[]{:S(2)}) %collective-permute-start.2) | collective-permute-done | bytes 262176 | tf_op jit(solution)/shard_map/ppermute | solution.py:429
  25.5 0.1 collective-permute-start.3
  25.6 2.5 %collective-permute-start.4 = (bf16[2,16,1024]{2,1,0:T(8,128)(2,1)S(1)}, bf16[2,16,1024]{2,1,0:T(8,128)(2,1)S(1)}, u32[]{:S(2)}, u32[]{:S(2)}) collective-permute-start(bf16[2,16,1024]{2,1,0:T(8,128)(2,1)S(1)} %get-tuple-element.52), channel_id=1, source_target_pairs={{0,16},{4,20},{8,24},{12,28},{16,0},{20,4},{24,8},{28,12},{1,17},{... | collective-permute-start | bytes 196616 | tf_op jit(solution)/shard_map/ppermute | solution.py:433
  28.0 1.9 %collective-permute-start.5 = (bf16[2,16,1024]{2,1,0:T(8,128)(2,1)S(1)}, bf16[2,16,1024]{2,1,0:T(8,128)(2,1)S(1)}, u32[]{:S(2)}, u32[]{:S(2)}) collective-permute-start(bf16[2,16,1024]{2,1,0:T(8,128)(2,1)S(1)} %get-tuple-element.53), channel_id=1, source_target_pairs={{0,24},{4,28},{8,16},{12,20},{16,8},{20,12},{24,0},{28,4},{1,25},{... | collective-permute-start | bytes 196616 | tf_op jit(solution)/shard_map/ppermute | solution.py:433
  29.9 1.5 %turn.3.refs_7_.refs_2_ = bf16[256,32,128]{2,1,0:T(8,128)(2,1)S(1)} custom-call(f32[8,2176,128]{2,1,0:T(8,128)S(1)} %get-tuple-element.43.refs_4_.refs_0_, f32[2,16,1024]{2,1,0:T(8,128)S(1)} %get-tuple-element.49.refs_1_), custom_call_target="tpu_custom_call" | custom-call | bytes 16 | tf_op jit(solution)/shard_map/turn/pallas_call | solution.py:33
  31.5 3.3 %collective-permute-done.5.refs_3_ = bf16[2,16,1024]{2,1,0:T(8,128)(2,1)S(1)} collective-permute-done((bf16[2,16,1024]{2,1,0:T(8,128)(2,1)S(1)}, bf16[2,16,1024]{2,1,0:T(8,128)(2,1)S(1)}, u32[]{:S(2)}, u32[]{:S(2)}) %collective-permute-start.5) | collective-permute-done | bytes 65568 | tf_op jit(solution)/shard_map/ppermute | solution.py:433
  34.8 0.1 collective-permute-start.7
  34.9 2.1 %collective-permute-start.8 = (bf16[4,16,1024]{2,1,0:T(8,128)(2,1)S(1)}, bf16[4,16,1024]{2,1,0:T(8,128)(2,1)S(1)}, u32[]{:S(2)}, u32[]{:S(2)}) collective-permute-start(bf16[4,16,1024]{2,1,0:T(8,128)(2,1)S(1)} %get-tuple-element.60), channel_id=1, source_target_pairs={{0,16},{4,20},{8,24},{12,28},{16,0},{20,4},{24,8},{28,12},{1,17},{... | collective-permute-start | bytes 393224 | tf_op jit(solution)/shard_map/ppermute | solution.py:433
  37.0 2.3 %collective-permute-start.9 = (bf16[4,16,1024]{2,1,0:T(8,128)(2,1)S(1)}, bf16[4,16,1024]{2,1,0:T(8,128)(2,1)S(1)}, u32[]{:S(2)}, u32[]{:S(2)}) collective-permute-start(bf16[4,16,1024]{2,1,0:T(8,128)(2,1)S(1)} %get-tuple-element.61), channel_id=1, source_target_pairs={{0,24},{4,28},{8,16},{12,20},{16,8},{20,12},{24,0},{28,4},{1,25},{... | collective-permute-start | bytes 393224 | tf_op jit(solution)/shard_map/ppermute | solution.py:433
  39.3 1.8 %collective-permute-done.7.refs_1_ = bf16[4,16,1024]{2,1,0:T(8,128)(2,1)S(1)} collective-permute-done((bf16[4,16,1024]{2,1,0:T(8,128)(2,1)S(1)}, bf16[4,16,1024]{2,1,0:T(8,128)(2,1)S(1)}, u32[]{:S(2)}, u32[]{:S(2)}) %collective-permute-start.7) | collective-permute-done | bytes 131104 | tf_op jit(solution)/shard_map/ppermute | solution.py:433
  41.1 2.9 %collective-permute-done.8.refs_2_ = bf16[4,16,1024]{2,1,0:T(8,128)(2,1)S(1)} collective-permute-done((bf16[4,16,1024]{2,1,0:T(8,128)(2,1)S(1)}, bf16[4,16,1024]{2,1,0:T(8,128)(2,1)S(1)}, u32[]{:S(2)}, u32[]{:S(2)}) %collective-permute-start.8) | collective-permute-done | bytes 131104 | tf_op jit(solution)/shard_map/ppermute | solution.py:433
  44.0 0.0 copy-start.1
  44.0 0.6 collective-permute-start.13
  44.6 2.1 %bins.5.refs_0_ = f32[2,4096,128]{2,1,0:T(8,128)S(1)} custom-call(bf16[8,16,1024]{2,1,0:T(8,128)(2,1)S(1)} %get-tuple-element.64.refs_0_, bf16[256,32,128]{2,1,0:T(8,128)(2,1)S(1)} %turn.2.refs_2_.refs_1_, bf16[256,32,128]{2,1,0:T(8,128)(2,1)S(1)} %turn.3.refs_7_.refs_2_), custom_call_target="tpu_custom_call" | custom-call | bytes 16 | tf_op jit(solution)/shard_map/bins/pallas_call | solution.py:33
  46.8 2.0 %collective-permute-start.10 = (bf16[2,16,1024]{2,1,0:T(8,128)(2,1)S(1)}, bf16[2,16,1024]{2,1,0:T(8,128)(2,1)S(1)}, u32[]{:S(2)}, u32[]{:S(2)}) collective-permute-start(bf16[2,16,1024]{2,1,0:T(8,128)(2,1)S(1)} %get-tuple-element.63), channel_id=1, source_target_pairs={{0,8},{4,12},{8,0},{12,4},{16,24},{20,28},{24,16},{28,20},{1,9},{5... | collective-permute-start | bytes 196616 | tf_op jit(solution)/shard_map/ppermute | solution.py:433
  48.8 0.9 collective-permute-start.11
  49.7 1.6 %collective-permute-start.12 = (bf16[2,16,1024]{2,1,0:T(8,128)(2,1)S(1)}, bf16[2,16,1024]{2,1,0:T(8,128)(2,1)S(1)}, u32[]{:S(2)}, u32[]{:S(2)}) collective-permute-start(bf16[2,16,1024]{2,1,0:T(8,128)(2,1)S(1)} %get-tuple-element.63), channel_id=1, source_target_pairs={{0,24},{4,28},{8,16},{12,20},{16,8},{20,12},{24,0},{28,4},{1,25},{... | collective-permute-start | bytes 196616 | tf_op jit(solution)/shard_map/ppermute | solution.py:433
  51.3 3.1 %collective-permute-done.11 = bf16[2,16,1024]{2,1,0:T(8,128)(2,1)S(1)} collective-permute-done((bf16[2,16,1024]{2,1,0:T(8,128)(2,1)S(1)}, bf16[2,16,1024]{2,1,0:T(8,128)(2,1)S(1)}, u32[]{:S(2)}, u32[]{:S(2)}) %collective-permute-start.11) | collective-permute-done | bytes 65568 | tf_op jit(solution)/shard_map/ppermute | solution.py:433
  54.4 1.4 %collective-permute-done.12 = bf16[2,16,1024]{2,1,0:T(8,128)(2,1)S(1)} collective-permute-done((bf16[2,16,1024]{2,1,0:T(8,128)(2,1)S(1)}, bf16[2,16,1024]{2,1,0:T(8,128)(2,1)S(1)}, u32[]{:S(2)}, u32[]{:S(2)}) %collective-permute-start.12) | collective-permute-done | bytes 65568 | tf_op jit(solution)/shard_map/ppermute | solution.py:433
  55.8 2.7 %lags.4 = (bf16[8,32,512]{2,1,0:T(8,128)(2,1)S(1)}, bf16[8,32,512]{2,1,0:T(8,128)(2,1)S(1)}, bf16[8,32,512]{2,1,0:T(8,128)(2,1)S(1)}, bf16[8,32,512]{2,1,0:T(8,128)(2,1)S(1)}) custom-call(f32[2,4096,128]{2,1,0:T(8,128)S(1)} %bins.5.refs_0_, bf16[272,512]{1,0:T(8,128)(2,1)S(1)} %copy-done.1, bf16[256,512]{1,0:T(8,128)(2,1)S(1)} %copy-done.2, ...), custom_call_target="tpu_custom_call" | custom-call | bytes 16 | tf_op jit(solution)/shard_map/lags/pallas_call | solution.py:33
  58.5 0.1 collective-permute-start.14
  58.6 0.5 collective-permute-start.15
  59.1 2.1 %bins.7.refs_0_ = f32[2,4096,128]{2,1,0:T(8,128)S(1)} custom-call(bf16[8,16,1024]{2,1,0:T(8,128)(2,1)S(1)} %collective-permute-done.13.refs_4_.refs_0_, bf16[256,32,128]{2,1,0:T(8,128)(2,1)S(1)} %turn.2.refs_2_.refs_1_, bf16[256,32,128]{2,1,0:T(8,128)(2,1)S(1)} %turn.3.refs_7_.refs_2_), custom_call_target="tpu_custom_call" | custom-call | bytes 16 | tf_op jit(solution)/shard_map/bins/pallas_call | solution.py:33
  61.2 2.7 %lags.6 = (bf16[8,32,512]{2,1,0:T(8,128)(2,1)S(1)}, bf16[8,32,512]{2,1,0:T(8,128)(2,1)S(1)}, bf16[8,32,512]{2,1,0:T(8,128)(2,1)S(1)}, bf16[8,32,512]{2,1,0:T(8,128)(2,1)S(1)}) custom-call(f32[2,4096,128]{2,1,0:T(8,128)S(1)} %bins.7.refs_0_, bf16[272,512]{1,0:T(8,128)(2,1)S(1)} %copy-done.1, bf16[256,512]{1,0:T(8,128)(2,1)S(1)} %copy-done.2), custom_call_target="tpu_custom_call" | custom-call | bytes 16 | tf_op jit(solution)/shard_map/lags/pallas_call | solution.py:33
  64.0 0.1 add_pair.4
  64.1 1.5 %collective-permute-start.16 = (bf16[8,32,512]{2,1,0:T(8,128)(2,1)S(1)}, bf16[8,32,512]{2,1,0:T(8,128)(2,1)S(1)}, u32[]{:S(2)}, u32[]{:S(2)}) collective-permute-start(bf16[8,32,512]{2,1,0:T(8,128)(2,1)S(1)} %add_pair.4), channel_id=1, source_target_pairs={{0,2},{1,3},{2,0},{3,1},{4,6},{5,7},{6,4},{7,5},{8,10},{9,11},{10,... | collective-permute-start | bytes 786440 | tf_op jit(solution)/shard_map/ppermute | solution.py:491
  65.6 0.1 collective-permute-start.22
  65.7 0.5 collective-permute-start.23
  66.2 1.6 %collective-permute-start.21 = (bf16[8,16,1024]{2,1,0:T(8,128)(2,1)S(1)}, bf16[8,16,1024]{2,1,0:T(8,128)(2,1)S(1)}, u32[]{:S(2)}, u32[]{:S(2)}) collective-permute-start(bf16[8,16,1024]{2,1,0:T(8,128)(2,1)S(1)} %constant_dynamic-update-slice_fusion.refs_0_.refs_3_), channel_id=1, source_target_pairs={{0,4},{4,0},{8,12},{12,8},{16,20},{20,16},{24,28},{28,24},{1,5},{5... | collective-permute-start | bytes 786440 | tf_op jit(solution)/shard_map/ppermute | solution.py:445
  67.8 2.1 %bins.4.refs_0_ = f32[2,4096,128]{2,1,0:T(8,128)S(1)} custom-call(bf16[8,16,1024]{2,1,0:T(8,128)(2,1)S(1)} %constant_dynamic-update-slice_fusion.refs_0_.refs_3_, bf16[256,32,128]{2,1,0:T(8,128)(2,1)S(1)} %turn.2.refs_2_.refs_1_, bf16[256,32,128]{2,1,0:T(8,128)(2,1)S(1)} %turn.3.refs_7_.refs_2_), custom_call_target="tpu_custom_call" | custom-call | bytes 16 | tf_op jit(solution)/shard_map/bins/pallas_call | solution.py:33
  69.9 0.1 add_pair.6
  70.0 0.6 collective-permute-start.24
  70.6 1.8 %collective-permute-done.16.refs_3_.refs_2_ = bf16[8,32,512]{2,1,0:T(8,128)(2,1)S(1)} collective-permute-done((bf16[8,32,512]{2,1,0:T(8,128)(2,1)S(1)}, bf16[8,32,512]{2,1,0:T(8,128)(2,1)S(1)}, u32[]{:S(2)}, u32[]{:S(2)}) %collective-permute-start.16) | collective-permute-done | bytes 262176 | tf_op jit(solution)/shard_map/ppermute | solution.py:491
  72.4 2.7 %lags.5 = (bf16[8,32,512]{2,1,0:T(8,128)(2,1)S(1)}, bf16[8,32,512]{2,1,0:T(8,128)(2,1)S(1)}, bf16[8,32,512]{2,1,0:T(8,128)(2,1)S(1)}, bf16[8,32,512]{2,1,0:T(8,128)(2,1)S(1)}) custom-call(f32[2,4096,128]{2,1,0:T(8,128)S(1)} %bins.4.refs_0_, bf16[272,512]{1,0:T(8,128)(2,1)S(1)} %copy-done.1, bf16[256,512]{1,0:T(8,128)(2,1)S(1)} %copy-done.2, ...), custom_call_target="tpu_custom_call" | custom-call | bytes 16 | tf_op jit(solution)/shard_map/lags/pallas_call | solution.py:33
  75.1 0.1 collective-permute-start.18
  75.2 0.5 collective-permute-start.19
  75.7 2.1 %bins.6.refs_0_ = f32[2,4096,128]{2,1,0:T(8,128)S(1)} custom-call(bf16[8,16,1024]{2,1,0:T(8,128)(2,1)S(1)} %collective-permute-done.21.refs_0_, bf16[256,32,128]{2,1,0:T(8,128)(2,1)S(1)} %turn.2.refs_2_.refs_1_, bf16[256,32,128]{2,1,0:T(8,128)(2,1)S(1)} %turn.3.refs_7_.refs_2_), custom_call_target="tpu_custom_call" | custom-call | bytes 16 | tf_op jit(solution)/shard_map/bins/pallas_call | solution.py:33
  77.9 0.2 collective-permute-done.24.refs_3_.refs_5_
  78.1 2.7 %lags.7 = (bf16[8,32,512]{2,1,0:T(8,128)(2,1)S(1)}, bf16[8,32,512]{2,1,0:T(8,128)(2,1)S(1)}, bf16[8,32,512]{2,1,0:T(8,128)(2,1)S(1)}, bf16[8,32,512]{2,1,0:T(8,128)(2,1)S(1)}) custom-call(f32[2,4096,128]{2,1,0:T(8,128)S(1)} %bins.6.refs_0_, bf16[272,512]{1,0:T(8,128)(2,1)S(1)} %copy-done.1, bf16[256,512]{1,0:T(8,128)(2,1)S(1)} %copy-done.2, ...), custom_call_target="tpu_custom_call" | custom-call | bytes 16 | tf_op jit(solution)/shard_map/lags/pallas_call | solution.py:33
  80.8 0.1 add_pair.5
  80.9 2.2 %collective-permute-start.20 = (bf16[8,32,512]{2,1,0:T(8,128)(2,1)S(1)}, bf16[8,32,512]{2,1,0:T(8,128)(2,1)S(1)}, u32[]{:S(2)}, u32[]{:S(2)}) collective-permute-start(bf16[8,32,512]{2,1,0:T(8,128)(2,1)S(1)} %add_pair.5), channel_id=1, source_target_pairs={{0,2},{1,3},{2,0},{3,1},{4,6},{5,7},{6,4},{7,5},{8,10},{9,11},{10,... | collective-permute-start | bytes 786440 | tf_op jit(solution)/shard_map/ppermute | solution.py:491
  83.1 0.1 collective-permute-start.26
  83.2 0.5 collective-permute-start.27
  83.7 0.1 collective-permute-start.30
  83.8 0.4 collective-permute-start.29
  84.2 0.3 collective-permute-done.26.refs_1_
  84.5 0.1 collective-permute-start.25
  84.7 0.0 collective-permute-done.27.refs_2_
  84.7 0.3 collective-permute-start.17
  85.0 4.6 %collective-permute-done.20.refs_3_.refs_2_ = bf16[8,32,512]{2,1,0:T(8,128)(2,1)S(1)} collective-permute-done((bf16[8,32,512]{2,1,0:T(8,128)(2,1)S(1)}, bf16[8,32,512]{2,1,0:T(8,128)(2,1)S(1)}, u32[]{:S(2)}, u32[]{:S(2)}) %collective-permute-start.20) | collective-permute-done | bytes 262176 | tf_op jit(solution)/shard_map/ppermute | solution.py:491
  89.6 0.1 add_pair.7
  89.7 1.8 %collective-permute-start.28 = (bf16[8,32,512]{2,1,0:T(8,128)(2,1)S(1)}, bf16[8,32,512]{2,1,0:T(8,128)(2,1)S(1)}, u32[]{:S(2)}, u32[]{:S(2)}) collective-permute-start(bf16[8,32,512]{2,1,0:T(8,128)(2,1)S(1)} %add_pair.7), channel_id=1, source_target_pairs={{0,2},{1,3},{2,0},{3,1},{4,6},{5,7},{6,4},{7,5},{8,10},{9,11},{10,... | collective-permute-start | bytes 786440 | tf_op jit(solution)/shard_map/ppermute | solution.py:491
  91.5 0.9 unfold.2.refs_7_
  92.4 5.1 %collective-permute-done.28.refs_5_ = bf16[8,32,512]{2,1,0:T(8,128)(2,1)S(1)} collective-permute-done((bf16[8,32,512]{2,1,0:T(8,128)(2,1)S(1)}, bf16[8,32,512]{2,1,0:T(8,128)(2,1)S(1)}, u32[]{:S(2)}, u32[]{:S(2)}) %collective-permute-start.28) | collective-permute-done | bytes 262176 | tf_op jit(solution)/shard_map/ppermute | solution.py:491
  97.5 1.9 %unfold.3 = bf16[32,32,512]{2,1,0:T(8,128)(2,1)} custom-call(bf16[8,32,512]{2,1,0:T(8,128)(2,1)S(1)} %get-tuple-element.67.refs_0_, bf16[8,32,512]{2,1,0:T(8,128)(2,1)S(1)} %collective-permute-done.17.refs_1_, bf16[8,32,512]{2,1,0:T(8,128)(2,1)S(1)} %collective-permute-done.20.refs_3_.refs_2_, bf16[8,32,512]{2,1,0:T(8,128)(2,1)S(1)} %get-tuple-element.73.refs_3_, ...), custom_call_target="tpu_custom_call" | custom-call | bytes 16 | tf_op jit(solution)/shard_map/unfold/pallas_call | solution.py:33
  (41 shorter events, 0.3 us)
Async XLA Ops:
  0.0 14.4 %copy-start.5 = (s32[16]{0:T(128)S(1)}, s32[16]{0:T(128)}, u32[]{:S(2)}) copy-start(s32[16]{0:T(128)} %refs_1_.5) | copy-start | bytes 196
  0.0 14.4 %copy-start.4 = (s32[32]{0:T(128)S(1)}, s32[32]{0:T(128)}, u32[]{:S(2)}) copy-start(s32[32]{0:T(128)} %refs_0_.3) | copy-start | bytes 388
  1.2 13.2 %collective-permute-start = (bf16[16,1,1024]{2,1,0:T(2,128)(2,1)S(1)}, bf16[16,1,1024]{2,1,0:T(2,128)(2,1)S(1)}, u32[]{:S(2)}, u32[]{:S(2)}) collective-permute-start(bf16[16,1,1024]{2,1,0:T(2,128)(2,1)S(1)} %get-tuple-element.82), channel_id=1, source_target_pairs={{0,4},{4,8},{8,12},{12,16},{16,20},{20,24},{24,28},{28,0},{1,5},{5... | collective-permute-start | bytes 98312 | tf_op jit(solution)/shard_map/ppermute | solution.py:477
  4.2 10.2 %collective-permute-start.1 = (bf16[16,1,1024]{2,1,0:T(2,128)(2,1)S(1)}, bf16[16,1,1024]{2,1,0:T(2,128)(2,1)S(1)}, u32[]{:S(2)}, u32[]{:S(2)}) collective-permute-start(bf16[16,1,1024]{2,1,0:T(2,128)(2,1)S(1)} %get-tuple-element.81), channel_id=1, source_target_pairs={{4,0},{8,4},{12,8},{16,12},{20,16},{24,20},{28,24},{0,28},{5,1},{9... | collective-permute-start | bytes 98312 | tf_op jit(solution)/shard_map/ppermute | solution.py:478
  7.3 2.2 %copy-start = (bf16[16,128,1024]{2,1,0:T(8,128)(2,1)S(1)}, bf16[16,128,1024]{2,1,0:T(8,128)(2,1)}, u32[]{:S(2)}) copy-start(bf16[16,128,1024]{2,1,0:T(8,128)(2,1)} %refs_0_.2) | copy-start | bytes 12582916
  16.1 9.3 %collective-permute-start.2 = (bf16[8,16,1024]{2,1,0:T(8,128)(2,1)S(1)}, bf16[8,16,1024]{2,1,0:T(8,128)(2,1)S(1)}, u32[]{:S(2)}, u32[]{:S(2)}) collective-permute-start(bf16[8,16,1024]{2,1,0:T(8,128)(2,1)S(1)} %get-tuple-element.48), channel_id=1, source_target_pairs={{0,4},{4,0},{8,12},{12,8},{16,20},{20,16},{24,28},{28,24},{1,5},{5... | collective-permute-start | bytes 786440 | tf_op jit(solution)/shard_map/ppermute | solution.py:429
  16.2 15.2 %collective-permute-start.6 = (bf16[8,16,1024]{2,1,0:T(8,128)(2,1)S(1)}, bf16[8,16,1024]{2,1,0:T(8,128)(2,1)S(1)}, u32[]{:S(2)}, u32[]{:S(2)}) collective-permute-start(bf16[8,16,1024]{2,1,0:T(8,128)(2,1)S(1)} %get-tuple-element.55), channel_id=1, source_target_pairs={{0,4},{4,0},{8,12},{12,8},{16,20},{20,16},{24,28},{28,24},{1,5},{5... | collective-permute-start | bytes 786440 | tf_op jit(solution)/shard_map/ppermute | solution.py:429
  25.5 6.0 %collective-permute-start.3 = (bf16[2,16,1024]{2,1,0:T(8,128)(2,1)S(1)}, bf16[2,16,1024]{2,1,0:T(8,128)(2,1)S(1)}, u32[]{:S(2)}, u32[]{:S(2)}) collective-permute-start(bf16[2,16,1024]{2,1,0:T(8,128)(2,1)S(1)} %get-tuple-element.51), channel_id=1, source_target_pairs={{0,8},{4,12},{8,0},{12,4},{16,24},{20,28},{24,16},{28,20},{1,9},{5... | collective-permute-start | bytes 196616 | tf_op jit(solution)/shard_map/ppermute | solution.py:433
  25.6 6.0 %collective-permute-start.4 = (bf16[2,16,1024]{2,1,0:T(8,128)(2,1)S(1)}, bf16[2,16,1024]{2,1,0:T(8,128)(2,1)S(1)}, u32[]{:S(2)}, u32[]{:S(2)}) collective-permute-start(bf16[2,16,1024]{2,1,0:T(8,128)(2,1)S(1)} %get-tuple-element.52), channel_id=1, source_target_pairs={{0,16},{4,20},{8,24},{12,28},{16,0},{20,4},{24,8},{28,12},{1,17},{... | collective-permute-start | bytes 196616 | tf_op jit(solution)/shard_map/ppermute | solution.py:433
  28.0 6.8 %collective-permute-start.5 = (bf16[2,16,1024]{2,1,0:T(8,128)(2,1)S(1)}, bf16[2,16,1024]{2,1,0:T(8,128)(2,1)S(1)}, u32[]{:S(2)}, u32[]{:S(2)}) collective-permute-start(bf16[2,16,1024]{2,1,0:T(8,128)(2,1)S(1)} %get-tuple-element.53), channel_id=1, source_target_pairs={{0,24},{4,28},{8,16},{12,20},{16,8},{20,12},{24,0},{28,4},{1,25},{... | collective-permute-start | bytes 196616 | tf_op jit(solution)/shard_map/ppermute | solution.py:433
  34.8 6.2 %collective-permute-start.7 = (bf16[4,16,1024]{2,1,0:T(8,128)(2,1)S(1)}, bf16[4,16,1024]{2,1,0:T(8,128)(2,1)S(1)}, u32[]{:S(2)}, u32[]{:S(2)}) collective-permute-start(bf16[4,16,1024]{2,1,0:T(8,128)(2,1)S(1)} %get-tuple-element.59.refs_0_), channel_id=1, source_target_pairs={{0,8},{4,12},{8,0},{12,4},{16,24},{20,28},{24,16},{28,20},{1,9},{5... | collective-permute-start | bytes 393224 | tf_op jit(solution)/shard_map/ppermute | solution.py:433
  34.9 9.1 %collective-permute-start.8 = (bf16[4,16,1024]{2,1,0:T(8,128)(2,1)S(1)}, bf16[4,16,1024]{2,1,0:T(8,128)(2,1)S(1)}, u32[]{:S(2)}, u32[]{:S(2)}) collective-permute-start(bf16[4,16,1024]{2,1,0:T(8,128)(2,1)S(1)} %get-tuple-element.60), channel_id=1, source_target_pairs={{0,16},{4,20},{8,24},{12,28},{16,0},{20,4},{24,8},{28,12},{1,17},{... | collective-permute-start | bytes 393224 | tf_op jit(solution)/shard_map/ppermute | solution.py:433
  37.0 7.0 %collective-permute-start.9 = (bf16[4,16,1024]{2,1,0:T(8,128)(2,1)S(1)}, bf16[4,16,1024]{2,1,0:T(8,128)(2,1)S(1)}, u32[]{:S(2)}, u32[]{:S(2)}) collective-permute-start(bf16[4,16,1024]{2,1,0:T(8,128)(2,1)S(1)} %get-tuple-element.61), channel_id=1, source_target_pairs={{0,24},{4,28},{8,16},{12,20},{16,8},{20,12},{24,0},{28,4},{1,25},{... | collective-permute-start | bytes 393224 | tf_op jit(solution)/shard_map/ppermute | solution.py:433
  44.0 11.8 %copy-start.1 = (bf16[272,512]{1,0:T(8,128)(2,1)S(1)}, bf16[272,512]{1,0:T(8,128)(2,1)}, u32[]{:S(2)}) copy-start(bf16[272,512]{1,0:T(8,128)(2,1)} %constant.6.clone.refs_1_) | copy-start | bytes 835588
  44.0 11.7 %copy-start.2 = (bf16[256,512]{1,0:T(8,128)(2,1)S(1)}, bf16[256,512]{1,0:T(8,128)(2,1)}, u32[]{:S(2)}) copy-start(bf16[256,512]{1,0:T(8,128)(2,1)} %constant.7.clone.refs_2_) | copy-start | bytes 786436
  44.0 11.7 %collective-permute-start.13 = (bf16[8,16,1024]{2,1,0:T(8,128)(2,1)S(1)}, bf16[8,16,1024]{2,1,0:T(8,128)(2,1)S(1)}, u32[]{:S(2)}, u32[]{:S(2)}) collective-permute-start(bf16[8,16,1024]{2,1,0:T(8,128)(2,1)S(1)} %get-tuple-element.64.refs_0_), channel_id=1, source_target_pairs={{0,4},{4,0},{8,12},{12,8},{16,20},{20,16},{24,28},{28,24},{1,5},{5... | collective-permute-start | bytes 786440 | tf_op jit(solution)/shard_map/ppermute | solution.py:443
  46.8 4.5 %collective-permute-start.10 = (bf16[2,16,1024]{2,1,0:T(8,128)(2,1)S(1)}, bf16[2,16,1024]{2,1,0:T(8,128)(2,1)S(1)}, u32[]{:S(2)}, u32[]{:S(2)}) collective-permute-start(bf16[2,16,1024]{2,1,0:T(8,128)(2,1)S(1)} %get-tuple-element.63), channel_id=1, source_target_pairs={{0,8},{4,12},{8,0},{12,4},{16,24},{20,28},{24,16},{28,20},{1,9},{5... | collective-permute-start | bytes 196616 | tf_op jit(solution)/shard_map/ppermute | solution.py:433
  48.8 5.5 %collective-permute-start.11 = (bf16[2,16,1024]{2,1,0:T(8,128)(2,1)S(1)}, bf16[2,16,1024]{2,1,0:T(8,128)(2,1)S(1)}, u32[]{:S(2)}, u32[]{:S(2)}) collective-permute-start(bf16[2,16,1024]{2,1,0:T(8,128)(2,1)S(1)} %get-tuple-element.63), channel_id=1, source_target_pairs={{0,16},{4,20},{8,24},{12,28},{16,0},{20,4},{24,8},{28,12},{1,17},{... | collective-permute-start | bytes 196616 | tf_op jit(solution)/shard_map/ppermute | solution.py:433
  49.7 6.1 %collective-permute-start.12 = (bf16[2,16,1024]{2,1,0:T(8,128)(2,1)S(1)}, bf16[2,16,1024]{2,1,0:T(8,128)(2,1)S(1)}, u32[]{:S(2)}, u32[]{:S(2)}) collective-permute-start(bf16[2,16,1024]{2,1,0:T(8,128)(2,1)S(1)} %get-tuple-element.63), channel_id=1, source_target_pairs={{0,24},{4,28},{8,16},{12,20},{16,8},{20,12},{24,0},{28,4},{1,25},{... | collective-permute-start | bytes 196616 | tf_op jit(solution)/shard_map/ppermute | solution.py:433
  58.5 5.4 %collective-permute-start.14 = (bf16[4,32,512]{2,1,0:T(8,128)(2,1)S(1)}, bf16[4,32,512]{2,1,0:T(8,128)(2,1)S(1)}, u32[]{:S(2)}, u32[]{:S(2)}) collective-permute-start(bf16[4,32,512]{2,1,0:T(8,128)(2,1)S(1)} %get-tuple-element.90), channel_id=1, source_target_pairs={{0,1},{1,0},{2,3},{3,2},{4,5},{5,4},{6,7},{7,6},{8,9},{9,8},{10,11... | collective-permute-start | bytes 393224 | tf_op jit(solution)/shard_map/ppermute | solution.py:488
  58.6 5.4 %collective-permute-start.15 = (bf16[4,32,512]{2,1,0:T(8,128)(2,1)S(1)}, bf16[4,32,512]{2,1,0:T(8,128)(2,1)S(1)}, u32[]{:S(2)}, u32[]{:S(2)}) collective-permute-start(bf16[4,32,512]{2,1,0:T(8,128)(2,1)S(1)} %get-tuple-element.89), channel_id=1, source_target_pairs={{0,1},{1,0},{2,3},{3,2},{4,5},{5,4},{6,7},{7,6},{8,9},{9,8},{10,11... | collective-permute-start | bytes 393224 | tf_op jit(solution)/shard_map/ppermute | solution.py:488
  64.1 8.3 %collective-permute-start.16 = (bf16[8,32,512]{2,1,0:T(8,128)(2,1)S(1)}, bf16[8,32,512]{2,1,0:T(8,128)(2,1)S(1)}, u32[]{:S(2)}, u32[]{:S(2)}) collective-permute-start(bf16[8,32,512]{2,1,0:T(8,128)(2,1)S(1)} %add_pair.4), channel_id=1, source_target_pairs={{0,2},{1,3},{2,0},{3,1},{4,6},{5,7},{6,4},{7,5},{8,10},{9,11},{10,... | collective-permute-start | bytes 786440 | tf_op jit(solution)/shard_map/ppermute | solution.py:491
  65.6 4.3 %collective-permute-start.22 = (bf16[4,32,512]{2,1,0:T(8,128)(2,1)S(1)}, bf16[4,32,512]{2,1,0:T(8,128)(2,1)S(1)}, u32[]{:S(2)}, u32[]{:S(2)}) collective-permute-start(bf16[4,32,512]{2,1,0:T(8,128)(2,1)S(1)} %get-tuple-element.86), channel_id=1, source_target_pairs={{0,1},{1,0},{2,3},{3,2},{4,5},{5,4},{6,7},{7,6},{8,9},{9,8},{10,11... | collective-permute-start | bytes 393224 | tf_op jit(solution)/shard_map/ppermute | solution.py:488
  65.7 4.2 %collective-permute-start.23 = (bf16[4,32,512]{2,1,0:T(8,128)(2,1)S(1)}, bf16[4,32,512]{2,1,0:T(8,128)(2,1)S(1)}, u32[]{:S(2)}, u32[]{:S(2)}) collective-permute-start(bf16[4,32,512]{2,1,0:T(8,128)(2,1)S(1)} %get-tuple-element.85), channel_id=1, source_target_pairs={{0,1},{1,0},{2,3},{3,2},{4,5},{5,4},{6,7},{7,6},{8,9},{9,8},{10,11... | collective-permute-start | bytes 393224 | tf_op jit(solution)/shard_map/ppermute | solution.py:488
  66.2 9.5 %collective-permute-start.21 = (bf16[8,16,1024]{2,1,0:T(8,128)(2,1)S(1)}, bf16[8,16,1024]{2,1,0:T(8,128)(2,1)S(1)}, u32[]{:S(2)}, u32[]{:S(2)}) collective-permute-start(bf16[8,16,1024]{2,1,0:T(8,128)(2,1)S(1)} %constant_dynamic-update-slice_fusion.refs_0_.refs_3_), channel_id=1, source_target_pairs={{0,4},{4,0},{8,12},{12,8},{16,20},{20,16},{24,28},{28,24},{1,5},{5... | collective-permute-start | bytes 786440 | tf_op jit(solution)/shard_map/ppermute | solution.py:445
  70.0 8.1 %collective-permute-start.24 = (bf16[8,32,512]{2,1,0:T(8,128)(2,1)S(1)}, bf16[8,32,512]{2,1,0:T(8,128)(2,1)S(1)}, u32[]{:S(2)}, u32[]{:S(2)}) collective-permute-start(bf16[8,32,512]{2,1,0:T(8,128)(2,1)S(1)} %add_pair.6), channel_id=1, source_target_pairs={{0,2},{1,3},{2,0},{3,1},{4,6},{5,7},{6,4},{7,5},{8,10},{9,11},{10,... | collective-permute-start | bytes 786440 | tf_op jit(solution)/shard_map/ppermute | solution.py:491
  75.1 5.6 %collective-permute-start.18 = (bf16[4,32,512]{2,1,0:T(8,128)(2,1)S(1)}, bf16[4,32,512]{2,1,0:T(8,128)(2,1)S(1)}, u32[]{:S(2)}, u32[]{:S(2)}) collective-permute-start(bf16[4,32,512]{2,1,0:T(8,128)(2,1)S(1)} %get-tuple-element.88), channel_id=1, source_target_pairs={{0,1},{1,0},{2,3},{3,2},{4,5},{5,4},{6,7},{7,6},{8,9},{9,8},{10,11... | collective-permute-start | bytes 393224 | tf_op jit(solution)/shard_map/ppermute | solution.py:488
  75.2 5.6 %collective-permute-start.19 = (bf16[4,32,512]{2,1,0:T(8,128)(2,1)S(1)}, bf16[4,32,512]{2,1,0:T(8,128)(2,1)S(1)}, u32[]{:S(2)}, u32[]{:S(2)}) collective-permute-start(bf16[4,32,512]{2,1,0:T(8,128)(2,1)S(1)} %get-tuple-element.87), channel_id=1, source_target_pairs={{0,1},{1,0},{2,3},{3,2},{4,5},{5,4},{6,7},{7,6},{8,9},{9,8},{10,11... | collective-permute-start | bytes 393224 | tf_op jit(solution)/shard_map/ppermute | solution.py:488
  77.9 13.6 %copy-start.3 = (bf16[512,512]{1,0:T(8,128)(2,1)S(1)}, bf16[512,512]{1,0:T(8,128)(2,1)}, u32[]{:S(2)}) copy-start(bf16[512,512]{1,0:T(8,128)(2,1)} %constant.8.clone.refs_6_) | copy-start | bytes 1572868
  80.9 8.8 %collective-permute-start.20 = (bf16[8,32,512]{2,1,0:T(8,128)(2,1)S(1)}, bf16[8,32,512]{2,1,0:T(8,128)(2,1)S(1)}, u32[]{:S(2)}, u32[]{:S(2)}) collective-permute-start(bf16[8,32,512]{2,1,0:T(8,128)(2,1)S(1)} %add_pair.5), channel_id=1, source_target_pairs={{0,2},{1,3},{2,0},{3,1},{4,6},{5,7},{6,4},{7,5},{8,10},{9,11},{10,... | collective-permute-start | bytes 786440 | tf_op jit(solution)/shard_map/ppermute | solution.py:491
  83.1 1.4 %collective-permute-start.26 = (bf16[4,32,512]{2,1,0:T(8,128)(2,1)S(1)}, bf16[4,32,512]{2,1,0:T(8,128)(2,1)S(1)}, u32[]{:S(2)}, u32[]{:S(2)}) collective-permute-start(bf16[4,32,512]{2,1,0:T(8,128)(2,1)S(1)} %get-tuple-element.84), channel_id=1, source_target_pairs={{0,1},{1,0},{2,3},{3,2},{4,5},{5,4},{6,7},{7,6},{8,9},{9,8},{10,11... | collective-permute-start | bytes 393224 | tf_op jit(solution)/shard_map/ppermute | solution.py:488
  83.2 1.5 %collective-permute-start.27 = (bf16[4,32,512]{2,1,0:T(8,128)(2,1)S(1)}, bf16[4,32,512]{2,1,0:T(8,128)(2,1)S(1)}, u32[]{:S(2)}, u32[]{:S(2)}) collective-permute-start(bf16[4,32,512]{2,1,0:T(8,128)(2,1)S(1)} %get-tuple-element.83), channel_id=1, source_target_pairs={{0,1},{1,0},{2,3},{3,2},{4,5},{5,4},{6,7},{7,6},{8,9},{9,8},{10,11... | collective-permute-start | bytes 393224 | tf_op jit(solution)/shard_map/ppermute | solution.py:488
  83.7 7.8 %collective-permute-start.30 = (bf16[8,32,512]{2,1,0:T(8,128)(2,1)S(1)}, bf16[8,32,512]{2,1,0:T(8,128)(2,1)S(1)}, u32[]{:S(2)}, u32[]{:S(2)}) collective-permute-start(bf16[8,32,512]{2,1,0:T(8,128)(2,1)S(1)} %get-tuple-element.80), channel_id=1, source_target_pairs={{0,1},{1,0},{2,3},{3,2},{4,5},{5,4},{6,7},{7,6},{8,9},{9,8},{10,11... | collective-permute-start | bytes 786440 | tf_op jit(solution)/shard_map/ppermute | solution.py:488
  83.8 7.7 %collective-permute-start.29 = (bf16[8,32,512]{2,1,0:T(8,128)(2,1)S(1)}, bf16[8,32,512]{2,1,0:T(8,128)(2,1)S(1)}, u32[]{:S(2)}, u32[]{:S(2)}) collective-permute-start(bf16[8,32,512]{2,1,0:T(8,128)(2,1)S(1)} %get-tuple-element.78), channel_id=1, source_target_pairs={{0,1},{1,0},{2,3},{3,2},{4,5},{5,4},{6,7},{7,6},{8,9},{9,8},{10,11... | collective-permute-start | bytes 786440 | tf_op jit(solution)/shard_map/ppermute | solution.py:488
  84.5 7.9 %collective-permute-start.25 = (bf16[8,32,512]{2,1,0:T(8,128)(2,1)S(1)}, bf16[8,32,512]{2,1,0:T(8,128)(2,1)S(1)}, u32[]{:S(2)}, u32[]{:S(2)}) collective-permute-start(bf16[8,32,512]{2,1,0:T(8,128)(2,1)S(1)} %get-tuple-element.74), channel_id=1, source_target_pairs={{0,1},{1,0},{2,3},{3,2},{4,5},{5,4},{6,7},{7,6},{8,9},{9,8},{10,11... | collective-permute-start | bytes 786440 | tf_op jit(solution)/shard_map/ppermute | solution.py:488
  84.7 7.7 %collective-permute-start.17 = (bf16[8,32,512]{2,1,0:T(8,128)(2,1)S(1)}, bf16[8,32,512]{2,1,0:T(8,128)(2,1)S(1)}, u32[]{:S(2)}, u32[]{:S(2)}) collective-permute-start(bf16[8,32,512]{2,1,0:T(8,128)(2,1)S(1)} %get-tuple-element.68), channel_id=1, source_target_pairs={{0,1},{1,0},{2,3},{3,2},{4,5},{5,4},{6,7},{7,6},{8,9},{9,8},{10,11... | collective-permute-start | bytes 786440 | tf_op jit(solution)/shard_map/ppermute | solution.py:488
  89.7 7.8 %collective-permute-start.28 = (bf16[8,32,512]{2,1,0:T(8,128)(2,1)S(1)}, bf16[8,32,512]{2,1,0:T(8,128)(2,1)S(1)}, u32[]{:S(2)}, u32[]{:S(2)}) collective-permute-start(bf16[8,32,512]{2,1,0:T(8,128)(2,1)S(1)} %add_pair.7), channel_id=1, source_target_pairs={{0,2},{1,3},{2,0},{3,1},{4,6},{5,7},{6,4},{7,5},{8,10},{9,11},{10,... | collective-permute-start | bytes 786440 | tf_op jit(solution)/shard_map/ppermute | solution.py:491

commit v4 on v3

--- a/solution.py
+++ b/solution.py
@@ -15,6 +15,19 @@
 EPSILON = 1e-06
 CHUNKS = 2
 LANES = 128
+AFTER = {
+    "own_first": ("turned0", "turned1"),
+    "lags2": ("far0",),
+    "lags3": ("far1", "sums2", "theirs_b"),
+    "lags1": ("other1",),
+    "end0": ("far1",),
+    "bins1": ("other1",),
+    "bins2": ("leave1",),
+    "lags0": ("mine_a",),
+    "part": ("mine_a", "turned0"),
+    "gather": ("sums0",),
+    "meet_a": ("turned0",),
+}
 F32 = jnp.float32
 BF16 = jnp.bfloat16
 MIB = 1024 * 1024
@@ -193,36 +206,61 @@
     )
 
 
-def turn_kernel(first, white_ref, edge_ref, out_ref, held):
-    _, windows, width = edge_ref.shape
-    chans = out_ref.shape[-1]
+def halve_kernel(white_ref, edge_ref, keep_ref, send_ref):
+    windows, chans, width = keep_ref.shape
+    share = chans // 2
+    blocks = white_ref.shape[1] // windows // share
+    pitch = white_ref.shape[1] // windows
+    me = lax.axis_index("win")
+    row = lax.broadcasted_iota(jnp.int32, (8, LANES), 0)
+
+    for w in range(windows):
+        for out, first in ((keep_ref, me), (send_ref, me ^ 1)):
+            for q in range(2):
+                block = first ^ (2 * q)
+                at = pl.multiple_of(w * pitch + block * share, 8)
+                for j in range(width // LANES):
+                    lanes = slice(j * LANES, (j + 1) * LANES)
+                    body = white_ref[j, pl.ds(at, share), :]
+                    top = jnp.where((row == 0) & (block == 0), edge_ref[0, w : w + 1, lanes], body[:8])
+                    low = jnp.where((row == 7) & (block == blocks - 1), edge_ref[1, w : w + 1, lanes], body[share - 8 :])
+                    body = jnp.concatenate([top, body[8 : share - 8], low], axis=0)
+                    out[w, q * share : (q + 1) * share, lanes] = body.astype(BF16)
+
+
+def halve(parts, white, edge, chans):
+    _, windows, width = edge.shape
+    shape = (windows, 2 * chans // parts, width)
+    return call(halve_kernel, (white, edge), [VMEM] * 2, [(shape, BF16)] * 2, [], 8, "halve")
+
+
+def turn_kernel(white_ref, out_ref, held):
+    windows, chans, width = white_ref.shape
     tile = LANES
     pitch = 2 * windows + 8
-    row = lax.broadcasted_iota(jnp.int32, (8, tile), 0)
-    for block in range(out_ref.shape[0] // tile):
+
+    def block(b, carry):
         for w in range(windows):
             for half in range(2):
-                j = half * (width // 2 // tile) + first + block
-                lanes = slice(j * tile, (j + 1) * tile)
-                at = w * (chans + 8)
-                body = white_ref[j, at : at + chans, :]
-                top = jnp.where(row == 0, edge_ref[0, w : w + 1, lanes], body[:8])
-                bottom = jnp.where(row == 7, edge_ref[1, w : w + 1, lanes], body[chans - 8 :])
-                body = jnp.concatenate([top, body[8 : chans - 8], bottom], axis=0)
-                held[pl.ds(half * windows + w, tile, stride=pitch), :] = body.T
+                at = pl.multiple_of(half * (width // 2) + b * tile, tile)
+                body = white_ref[w, :, pl.ds(at, tile)].astype(F32)
+                held[pl.ds(half * windows + w, tile, stride=pitch), :] = jnp.concatenate([body, body], axis=0).T
         for f in range(tile):
-            out_ref[block * tile + f] = held[f * pitch : f * pitch + 2 * windows, :].astype(BF16)
-
-
-def turn(white, edge, chans, first, tiles):
-    _, windows, width = edge.shape
+            out_ref[b * tile + f] = held[f * pitch : f * pitch + 2 * windows, :].astype(BF16)
+        return carry
+
+    lax.fori_loop(0, width // 2 // tile, block, 0)
+
+
+def turn(white):
+    windows, chans, width = white.shape
     return call(
-        functools.partial(turn_kernel, first),
-        (white, edge),
-        [VMEM, VMEM],
-        [((tiles * LANES, 2 * windows, chans), BF16)],
-        [pltpu.VMEM((LANES * (2 * windows + 8), chans), F32)],
-        16,
+        turn_kernel,
+        (white,),
+        [VMEM],
+        [((width // 2, 2 * windows, 2 * chans), BF16)],
+        [pltpu.VMEM((LANES * (2 * windows + 8), LANES), F32)],
+        8,
         "turn",
     )[0]
 
@@ -262,94 +300,88 @@
     )
 
 
-def part_kernel(sent_ref, b_ref, c_ref, d_ref, piece_ref, mine_ref, own_ref):
-    rows = piece_ref.shape[0]
+def gather_kernel(sent_ref, b_ref, c_ref, d_ref, mine_ref):
+    rows = mine_ref.shape[0] // 4
     for p, ref in enumerate((sent_ref, b_ref, c_ref, d_ref)):
         mine_ref[p * rows : (p + 1) * rows] = ref[:rows]
+
+
+def gather(parts_by_z, rows, after=()):
+    shape = (4 * rows, *parts_by_z[0].shape[1:])
+    return call(gather_kernel, parts_by_z, [VMEM] * 4, [(shape, BF16)], [], 8, "gather", after)[0]
+
+
+def part_kernel(b_ref, c_ref, d_ref, piece_ref, own_ref):
+    rows = piece_ref.shape[0]
     own_ref[...] = piece_ref[...] + b_ref[rows:] + c_ref[rows:] + d_ref[rows:]
 
 
-def part(sent, came, piece):
-    rows, windows, width = piece.shape
-    outs = [((4 * rows, windows, width), BF16), (piece.shape, BF16)]
-    return call(part_kernel, (sent, *came, piece), [VMEM] * 5, outs, [], 8, "part")
-
-
-def add_pair_kernel(keep_ref, *refs):
-    out, rows = refs[-1], refs[0].shape[0]
-    for k, ref in enumerate(refs[:-1]):
-        at = slice(k * rows, (k + 1) * rows)
-        out[at] = (keep_ref[at].astype(F32) + ref[...].astype(F32)).astype(BF16)
-
-
-def add_pair(keep, came, after):
-    ins = (keep, *came)
-    return call(add_pair_kernel, ins, [VMEM] * len(ins), [(keep.shape, BF16)], [], 8, "add_pair", after)[0]
-
-
-def bins_kernel(rows_ref, low_ref, high_ref, st, vt):
-    rows, windows, width = rows_ref.shape
-    held_freqs, depth, chans = low_ref.shape
+def part(came, piece, after=()):
+    return call(part_kernel, (*came, piece), [VMEM] * 4, [(piece.shape, BF16)], [], 8, "part", after)[0]
+
+
+def bins_kernel(own_ref, other_ref, low_ref, high_ref, st, vt):
+    rows, windows, width = own_ref.shape
+    depth, lanes = low_ref.shape[1:]
     freqs = width // 2
     tile = LANES
-    group = tile // depth
-    for g in range(rows // group):
-        pieces = []
-        for s in range(g * group, (g + 1) * group):
-            v = rows_ref[s].astype(F32)
-            pieces += [v[:, :freqs], v[:, freqs:]]
-        stack = jnp.concatenate(pieces, axis=0)
-        for j in range(freqs // tile):
-            t = stack[:, j * tile : (j + 1) * tile].T
-            for i in range(group):
-                moved = t if i == 0 else pltpu.roll(t, tile - i * depth, 1)
-                vt[pl.ds(j * tile * rows + g * group + i, tile, stride=rows), :] = moved
-
-    unroll = 128
-    for which, ref in enumerate((low_ref, high_ref)):
-
-        def step(i, carry):
-            for k in range(unroll):
-                f = i * unroll + k
-                at = pl.multiple_of((which * held_freqs + f) * rows, 8)
-                lhs = vt[pl.ds(at, rows), 0:depth].astype(BF16)
-                x = ref[f]
-                crossed = jnp.concatenate([x[windows:], -x[:windows]], axis=0)
-                sums = jnp.dot(lhs, jnp.concatenate([x, crossed], axis=1), preferred_element_type=F32)
-                st[0, pl.ds(at, rows), :] = sums[:, :chans]
-                st[1, pl.ds(at, rows), :] = sums[:, chans:]
-            return carry
-
-        lax.fori_loop(0, held_freqs // unroll, step, 0)
-
-
-def bins(rows, turned, after):
-    count, windows, width = rows.shape
+    pairs = rows // 2
+    for p in range(pairs):
+        whole, crossed = [], []
+        for s in (2 * p, 2 * p + 1):
+            for ref in (own_ref, other_ref):
+                v = ref[s].astype(F32)
+                whole += [v[:, :freqs], v[:, freqs:]]
+                crossed += [-v[:, freqs:], v[:, :freqs]]
+        for k, pieces in enumerate((whole, crossed)):
+            stack = jnp.concatenate(pieces, axis=0)
+            for j in range(freqs // tile):
+                turned = stack[:, j * tile : (j + 1) * tile].T
+                at = j * tile * 2 * rows + k * pairs + p
+                vt[pl.ds(at, tile, stride=2 * rows), :] = turned
+                vt[pl.ds(at + rows, tile, stride=2 * rows), :] = pltpu.roll(turned, tile // 2, 1)
+
+    first = lax.broadcasted_iota(jnp.int32, (rows, lanes), 1) < lanes // 2
+    unroll = 256
+
+    def step(i, carry):
+        for k in range(unroll):
+            f = i * unroll + k
+            lhs = vt[pl.ds(pl.multiple_of(f * 2 * rows, 8), 2 * rows), : 2 * depth].astype(BF16)
+            x = jnp.concatenate([low_ref[f], high_ref[f]], axis=0)
+            sums = jnp.dot(lhs, x, preferred_element_type=F32)
+            st[pl.ds(pl.multiple_of(f * rows, 8), rows), :] = jnp.where(first, sums[:rows], sums[rows:])
+        return carry
+
+    lax.fori_loop(0, freqs // unroll, step, 0)
+
+
+def bins(own, other, turned, after):
+    count, windows, width = own.shape
     held = width // 2 * count
     return call(
         bins_kernel,
-        (rows, *turned),
-        [VMEM] * 3,
-        [((2, held, turned[0].shape[-1]), F32)],
-        [pltpu.VMEM((held, LANES), F32)],
-        8,
+        (own, other, *turned),
+        [VMEM] * 4,
+        [((held, LANES), F32)],
+        [pltpu.VMEM((2 * held, LANES), F32)],
+        10,
         "bins",
         after,
     )[0]
 
 
-def lags_kernel(parts, st, cos_ref, sin_ref, *outs):
-    rows = outs[0].shape[0]
-    chans = st.shape[-1]
-    freqs = st.shape[1] // rows
-    me = lax.axis_index("win")
-    share = chans // parts
+def lags_kernel(st, cos_ref, sin_ref, stay_ref, leave_ref):
+    rows, share = stay_ref.shape[:2]
+    pairs = rows // 2
+    freqs = st.shape[0] // rows
     half = sin_ref.shape[0]
     last_row = lax.broadcasted_iota(jnp.int32, (8, 1), 0) == 7
-
-    def transform(p, carry):
+    for q in range(pairs // 2):
         real, imag = [
-            jnp.concatenate([st[i, pl.ds(2 * p + k, freqs, stride=rows), :].astype(BF16) for k in (0, 1)], axis=1)
+            jnp.concatenate(
+                [st[pl.ds(i * pairs + 2 * q + k, freqs, stride=rows), :].astype(BF16) for k in (0, 1)], axis=1
+            )
             for i in (0, 1)
         ]
         even = jnp.dot(cos_ref[...], real, preferred_element_type=F32)
@@ -357,45 +389,27 @@
         tail = odd[half - 8 :] + jnp.where(last_row, even[half : half + 1], 0.0)
         out = jnp.concatenate([even[:half], odd[: half - 8], tail], axis=0)
         for k in range(2):
-            flat = out[:, k * chans : (k + 1) * chans].T.astype(BF16)
-            for b in range(parts):
-                value = flat[b * share : (b + 1) * share, :]
-                for slot, to in enumerate(outs):
-
-                    @pl.when(b ^ me == slot)
-                    def _():
-                        to[2 * p + k] = value
-
-        return carry
-
-    lax.fori_loop(0, rows // 2, transform, 0)
-
-
-def lags(parts, rows, sums, tables, after):
-    chans = sums.shape[-1]
-    shape = (rows, chans // parts, LAGS)
-    return call(
-        functools.partial(lags_kernel, parts),
-        (sums, *tables),
-        [VMEM] * 3,
-        [(shape, BF16)] * parts,
-        [],
-        8,
-        "lags",
-        after,
-    )
+            flat = out[:, k * LANES : (k + 1) * LANES].T.astype(BF16)
+            for s in range(2):
+                at = 2 * share * s
+                stay_ref[4 * q + 2 * k + s] = flat[at : at + share]
+                leave_ref[4 * q + 2 * k + s] = flat[at + share : at + 2 * share]
+
+
+def lags(share, rows, sums, tables, after):
+    shape = (rows, share, LAGS)
+    return call(lags_kernel, (sums, *tables), [VMEM] * 3, [(shape, BF16)] * 2, [], 10, "lags", after)
 
 
 def unfold_kernel(blocks, pairs, *refs):
-    ins, mix_ref, earlier, (out_ref, held) = refs[: 3 * pairs], refs[3 * pairs], refs[3 * pairs + 1 : -2], refs[-2:]
+    ins, mix_ref, earlier, (out_ref, held) = refs[: 2 * pairs], refs[2 * pairs], refs[2 * pairs + 1 : -2], refs[-2:]
     rows, chans, lags = ins[0].shape
     per_chunk = pairs * rows
     pitch = per_chunk + 8
     for pair in range(pairs):
         total = jnp.zeros((rows * chans, lags), F32)
-        stay, near, far = [ref[...].reshape(rows * chans, lags) for ref in ins[3 * pair : 3 * pair + 3]]
-        near = (stay.astype(F32) + near.astype(F32)).astype(BF16)
-        for flat in (near, far):
+        for ref in ins[2 * pair : 2 * pair + 2]:
+            flat = ref[...].reshape(rows * chans, lags)
             total = total + jnp.dot(flat, mix_ref[...], preferred_element_type=F32)
         for r in range(rows):
             at = source_at(blocks, pair * rows + r, per_chunk)
@@ -411,17 +425,18 @@
             out_ref[c, first:, lanes] = held[j, c * pitch : c * pitch + per_chunk, :].astype(BF16)
 
 
-def unfold(blocks, ins, mix, earlier):
+def unfold(blocks, ins, mix, earlier, after):
     rows, chans, lags = ins[0].shape
-    per_chunk = len(ins) // 3 * rows
+    per_chunk = len(ins) // 2 * rows
     return call(
-        functools.partial(unfold_kernel, blocks, len(ins) // 3),
+        functools.partial(unfold_kernel, blocks, len(ins) // 2),
         (*ins, mix, *earlier),
         [VMEM] * (len(ins) + 1 + len(earlier)),
         [((chans, per_chunk * (1 + len(earlier)), lags), BF16)],
         [pltpu.VMEM((lags // LANES, chans * (per_chunk + 8), LANES), F32)],
         16,
         "unfold",
+        after,
     )[0]
 
 
@@ -433,16 +448,8 @@
     return [lax.ppermute(array, "chan", xor_pairs(8, 2 * p)) for p, array in zip((1, 2, 3), arrays)]
 
 
-def spread(blocks, picks, turned):
-    if blocks != 8:
-        return [lax.psum(pick, "chan") for pick in picks]
-    pieces_a = meet_x(picks[0], picks[1], turned[:1])
-    pieces_b = meet_x(picks[2], picks[3], ())
-    sent = own_first([pieces_a[0]] + over_z(pieces_a[1:]), pieces_b[1:], turned[1:])
-    mine_a, own_b = part(sent[0], over_z(sent), pieces_b[0])
-    theirs_a = lax.ppermute(mine_a, "chan", xor_pairs(8, 1))
-    mine_b = jnp.concatenate([own_b] + over_z([own_b] * 3), axis=0)
-    return mine_a, theirs_a, mine_b, lax.ppermute(mine_b, "chan", xor_pairs(8, 1))
+def over_x(array):
+    return lax.ppermute(array, "chan", xor_pairs(8, 1))
 
 
 def lag_tables(freqs, windows):
@@ -476,37 +483,66 @@
     backward = [(b, a) for a, b in forward]
     low = lax.ppermute(spectra[:, chans - 1 :, :], "chan", forward)
     high = lax.ppermute(spectra[:, :1, :], "chan", backward)
-    white, band, part, raw = whiten(spectra)
-    *picks, edge = edges(blocks, chans, valid, sources, low, high, white, band, part, raw)
+    white, band, edge_sums, raw = whiten(spectra)
+    *picks, edge = edges(blocks, chans, valid, sources, low, high, white, band, edge_sums, raw)
     tables = lag_tables(freqs, windows)
     mix = lag_mix()
-    tiles = freqs // LANES // 2
-    turned = [turn(white, edge, chans, i * tiles, tiles) for i in range(2)]
-    mine_a, theirs_a, mine_b, theirs_b = spread(blocks, picks, turned)
-
-    def near(send):
-        return lax.ppermute(send, "win", xor_pairs(parts, 1))
-
-    def far(leave):
-        return lax.ppermute(leave, "win", xor_pairs(parts, 2))
-
-    pairs, cames, waiting = [], [], []
-
-    def send_far(after):
-        leave, came = waiting.pop()
-        cames.append(far(add_pair(leave, came, after)))
-
-    for i, rows in enumerate((mine_a, theirs_a, mine_b, theirs_b)):
-        sums = bins(rows, turned, ())
-        after = [mine_b, theirs_a] if i == 0 else cames[i - 2 : i - 1] if i > 1 else []
-        stay, send_stay, leave, send_leave = lags(parts, rows.shape[0], sums, tables, after)
-        half = rows.shape[0] // 2
-        waiting.append((leave, [near(send_leave[:half]), near(send_leave[half:])]))
-        send_far(cames[2:3])
-        pairs += [(stay, near(send_stay))]
-    pairs = [array for (stay, came), far_came in zip(pairs, cames) for array in (stay, came, far_came)]
-    first = unfold(blocks, pairs[:6], mix, ())
-    return unfold(blocks, pairs[6:], mix, (first,))
+
+    def near(array):
+        return lax.ppermute(array, "win", xor_pairs(parts, 1))
+
+    def far(array):
+        return lax.ppermute(array, "win", xor_pairs(parts, 2))
+
+    keep, send = halve(parts, white, edge, chans)
+    turned = [turn(keep), turn(near(send))]
+    made = {"turned0": turned[0], "turned1": turned[1]}
+    ends = []
+
+    def after(name):
+        return [made[key] for key in AFTER.get(name, ()) if key in made]
+
+    def swap(name, rows):
+        made[name] = rows
+        made[name + "_near"] = near(rows)
+
+    def put(i, name):
+        made[f"sums{i}"] = bins(made[name], made[name + "_near"], turned, after(f"bins{i}"))
+
+    def transform(i):
+        sums = made[f"sums{i}"]
+        stay, leave = lags(chans // parts, sums.shape[0] // freqs, sums, tables, after(f"lags{i}"))
+        made[f"leave{i}"] = leave
+        made[f"far{i}"] = far(leave)
+        ends.extend([stay, made[f"far{i}"]])
+
+    def end(chunk, earlier):
+        return unfold(blocks, ends[4 * chunk : 4 * chunk + 4], mix, earlier, after(f"end{chunk}"))
+
+    if blocks == 8:
+        pieces_a = meet_x(picks[0], picks[1], after("meet_a"))
+        pieces_b = meet_x(picks[2], picks[3], ())
+        sent = own_first([pieces_a[0]] + over_z(pieces_a[1:]), pieces_b[1:], after("own_first"))
+        came = over_z(sent)
+        rows = pieces_b[0].shape[0]
+        swap("mine_a", gather((sent[0], *came), rows))
+        swap("theirs_a", over_x(made["mine_a"]))
+        made["own_b"] = own_b = part(came, pieces_b[0], after("part"))
+        others = over_z([own_b] * 3)
+        made["other0"], made["other1"], made["other2"] = others
+        put(0, "mine_a")
+        transform(0)
+        swap("mine_b", gather((own_b, *others), rows, after("gather")))
+        swap("theirs_b", over_x(made["mine_b"]))
+    else:
+        for name, pick in zip(("mine_a", "theirs_a", "mine_b", "theirs_b"), picks):
+            swap(name, lax.psum(pick, "chan"))
+        put(0, "mine_a")
+        transform(0)
+    for i, name in ((1, "theirs_a"), (2, "mine_b"), (3, "theirs_b")):
+        put(i, name)
+        transform(i)
+    return end(1, (end(0, ()),))
 
 
 def solution(mesh):

time: 99.6 us -> 90.5 us (0.909)
  waiting for transfers between devices: 30.2 us -> 24 us
  starting transfers between devices: 33.1 us -> 28.6 us
  Pallas kernels: 32.2 us -> 33.7 us
    ppermute x18 -> x11, waiting for transfers between devices: 12.1 us -> 7.39 us  [the longest x4 6.31 us: far(): return lax.ppermute(array, 'win', xor_pairs(parts, 2))]
    ppermute x18 -> x11, starting transfers between devices: 11.5 us -> 8.06 us  [the longest x4 4.72 us: far(): return lax.ppermute(array, 'win', xor_pairs(parts, 2))]
    ppermute x1, starting transfers between devices: 2.99 us -> 0.01 us  [on_device(): low = lax.ppermute(spectra[:, chans - 1:, :], 'chan', forward)]
    ppermute x1, starting transfers between devices: 3.1 us -> 6.03 us  [on_device(): high = lax.ppermute(spectra[:, :1, :], 'chan', backward)]
    pallas_call x22 -> x21, Pallas kernels: 32.2 us -> 33.7 us  [call(): pl.pallas_call(body, in_specs=[*in_specs] + [ANY] * len(after), out_specs...]
    ppermute x9, waiting for transfers between devices: 12.4 us -> 11 us  [over_z(): lax.ppermute(array, 'chan', xor_pairs(8, 2 * p))]
    unnamed x15 -> x12, local copies, waits for them, and re-layouts: 2.23 us -> 2.22 us
  transfers between devices with their start and end apart: 31 -> 24, of which waited for: 11 -> 10; matrix products, arithmetic and copies ran while one was open for 0% -> 0% of each run, Pallas kernels for 26% -> 33%
where the time goes in v4:
time: 90.5 us; the launch traced here: 90 us
  Pallas kernels  33.7 us (37%)
  starting transfers between devices  28.6 us (32%)
  waiting for transfers between devices  24 us (27%)
  local copies, waits for them, and re-layouts  3.35 us (4%)
    pallas_call x21, Pallas kernels, call(): pl.pallas_call(body, in_specs=[*in_specs] + [ANY] * len(after), out_specs...  33.7 us
    ppermute x9, starting transfers between devices, over_z(): lax.ppermute(array, 'chan', xor_pairs(8, 2 * p))  12.5 us
    ppermute x9, waiting for transfers between devices, over_z(): lax.ppermute(array, 'chan', xor_pairs(8, 2 * p))  11 us
    ppermute x4, waiting for transfers between devices, far(): return lax.ppermute(array, 'win', xor_pairs(parts, 2))  6.31 us
    ppermute x1, starting transfers between devices, on_device(): high = lax.ppermute(spectra[:, :1, :], 'chan', backward)  6.03 us
    ppermute x2, waiting for transfers between devices, meet_x(): return add_parts(keep, lax.ppermute(send, 'chan', xor_pairs(8, 1)), after)  5.63 us
    ppermute x4, starting transfers between devices, far(): return lax.ppermute(array, 'win', xor_pairs(parts, 2))  4.72 us
    ppermute x2, starting transfers between devices, over_x(): return lax.ppermute(array, 'chan', xor_pairs(8, 1))  2.97 us
  transfers between devices with their start and end apart: 24, of which 10 were waited for; matrix products, arithmetic and copies ran while one was open for 0% of the time, Pallas kernels for 33%

profile of v4, /device:TPU:0, one launch (start us, length us, event | category | flops | bytes accessed | tf_op | source)
XLA Modules:
  0.0 90.0 jit_solution(18376902452594138450)
XLA Ops:
  0.0 1.1 %fusion = (bf16[16,1,1024]{2,1,0:T(2,128)(2,1)S(1)}, bf16[16,1,1024]{2,1,0:T(2,128)(2,1)S(1)}) fusion(bf16[16,128,1024]{2,1,0:T(8,128)(2,1)} %refs_0_.2), kind=kLoop, calls=%fused_computation | loop fusion | bytes 131072 | tf_op jit(solution)/shard_map/slice | solution.py:485
  1.1 6.0 %collective-permute-start.1 = (bf16[16,1,1024]{2,1,0:T(2,128)(2,1)S(1)}, bf16[16,1,1024]{2,1,0:T(2,128)(2,1)S(1)}, u32[]{:S(2)}, u32[]{:S(2)}) collective-permute-start(bf16[16,1,1024]{2,1,0:T(2,128)(2,1)S(1)} %get-tuple-element.65), channel_id=1, source_target_pairs={{4,0},{8,4},{12,8},{16,12},{20,16},{24,20},{28,24},{0,28},{5,1},{9... | collective-permute-start | bytes 98312 | tf_op jit(solution)/shard_map/ppermute | solution.py:485
  7.2 0.0 collective-permute-start
  7.2 2.2 %copy-done = bf16[16,128,1024]{2,1,0:T(8,128)(2,1)S(1)} copy-done((bf16[16,128,1024]{2,1,0:T(8,128)(2,1)S(1)}, bf16[16,128,1024]{2,1,0:T(8,128)(2,1)}, u32[]{:S(2)}) %copy-start) | copy-done | bytes 4194328
  9.4 4.9 %whiten.1 = (f32[8,2176,128]{2,1,0:T(8,128)S(1)}, bf16[512,512]{1,0:T(8,128)(2,1)S(1)}, f32[2,16,512]{2,1,0:T(8,128)S(1)}, f32[2,16,1024]{2,1,0:T(8,128)S(1)}) custom-call(bf16[16,128,1024]{2,1,0:T(8,128)(2,1)S(1)} %copy-done), custom_call_target="tpu_custom_call" | custom-call | bytes 16 | tf_op jit(solution)/shard_map/whiten/pallas_call | solution.py:46
  14.3 0.0 collective-permute-done.refs_2_
  14.3 1.7 %edges.1 = (bf16[8,16,1024]{2,1,0:T(8,128)(2,1)S(1)}, bf16[8,16,1024]{2,1,0:T(8,128)(2,1)S(1)}, bf16[8,16,1024]{2,1,0:T(8,128)(2,1)S(1)}, bf16[8,16,1024]{2,1,0:T(8,128)(2,1)S(1)}, f32[2,16,1024]{2,1,0:T(8,128)S(1)}) custom-call(s32[32]{0:T(128)S(1)} %copy-done.4, s32[16]{0:T(128)S(1)} %copy-done.5, bf16[16,1,1024]{2,1,0:T(2,128)(2,1)S(1)} %collective-permute-done.refs_2_, ...), custom_call_target="tpu_custom_call" | custom-call | bytes 16 | tf_op jit(solution)/shard_map/edges/pallas_call | solution.py:46
  16.0 0.6 halve.1
  16.7 0.1 collective-permute-start.7
  16.7 0.1 collective-permute-start.2
  16.8 2.0 %collective-permute-start.6 = (bf16[8,16,1024]{2,1,0:T(8,128)(2,1)S(1)}, bf16[8,16,1024]{2,1,0:T(8,128)(2,1)S(1)}, u32[]{:S(2)}, u32[]{:S(2)}) collective-permute-start(bf16[8,16,1024]{2,1,0:T(8,128)(2,1)S(1)} %get-tuple-element.48), channel_id=1, source_target_pairs={{0,4},{4,0},{8,12},{12,8},{16,20},{20,16},{24,28},{28,24},{1,5},{5... | collective-permute-start | bytes 786440 | tf_op jit(solution)/shard_map/ppermute | solution.py:444
  18.8 2.1 %turn.2.refs_2_.refs_7_.refs_5_ = bf16[512,32,128]{2,1,0:T(8,128)(2,1)S(1)} custom-call(bf16[16,64,1024]{2,1,0:T(8,128)(2,1)S(1)} %get-tuple-element.42.refs_0_), custom_call_target="tpu_custom_call" | custom-call | bytes 16 | tf_op jit(solution)/shard_map/turn/pallas_call | solution.py:46
  21.0 4.9 %collective-permute-done.2.refs_1_ = bf16[8,16,1024]{2,1,0:T(8,128)(2,1)S(1)} collective-permute-done((bf16[8,16,1024]{2,1,0:T(8,128)(2,1)S(1)}, bf16[8,16,1024]{2,1,0:T(8,128)(2,1)S(1)}, u32[]{:S(2)}, u32[]{:S(2)}) %collective-permute-start.2) | collective-permute-done | bytes 262176 | tf_op jit(solution)/shard_map/ppermute | solution.py:444
  25.9 0.1 collective-permute-start.3
  26.0 3.9 %collective-permute-start.4 = (bf16[2,16,1024]{2,1,0:T(8,128)(2,1)S(1)}, bf16[2,16,1024]{2,1,0:T(8,128)(2,1)S(1)}, u32[]{:S(2)}, u32[]{:S(2)}) collective-permute-start(bf16[2,16,1024]{2,1,0:T(8,128)(2,1)S(1)} %get-tuple-element.45), channel_id=1, source_target_pairs={{0,16},{4,20},{8,24},{12,28},{16,0},{20,4},{24,8},{28,12},{1,17},{... | collective-permute-start | bytes 196616 | tf_op jit(solution)/shard_map/ppermute | solution.py:448
  29.9 0.5 collective-permute-start.5
  30.4 0.7 collective-permute-done.6.refs_1_
  31.1 0.0 collective-permute-done.7.refs_0_
  31.1 2.1 %turn.3.refs_8_.refs_3_ = bf16[512,32,128]{2,1,0:T(8,128)(2,1)S(1)} custom-call(bf16[16,64,1024]{2,1,0:T(8,128)(2,1)S(1)} %collective-permute-done.7.refs_0_), custom_call_target="tpu_custom_call" | custom-call | bytes 16 | tf_op jit(solution)/shard_map/turn/pallas_call | solution.py:46
  33.3 0.0 collective-permute-done.3.refs_1_
  33.3 1.0 %collective-permute-done.4.refs_2_ = bf16[2,16,1024]{2,1,0:T(8,128)(2,1)S(1)} collective-permute-done((bf16[2,16,1024]{2,1,0:T(8,128)(2,1)S(1)}, bf16[2,16,1024]{2,1,0:T(8,128)(2,1)S(1)}, u32[]{:S(2)}, u32[]{:S(2)}) %collective-permute-start.4) | collective-permute-done | bytes 65568 | tf_op jit(solution)/shard_map/ppermute | solution.py:448
  34.3 1.7 %collective-permute-done.5.refs_3_ = bf16[2,16,1024]{2,1,0:T(8,128)(2,1)S(1)} collective-permute-done((bf16[2,16,1024]{2,1,0:T(8,128)(2,1)S(1)}, bf16[2,16,1024]{2,1,0:T(8,128)(2,1)S(1)}, u32[]{:S(2)}, u32[]{:S(2)}) %collective-permute-start.5) | collective-permute-done | bytes 65568 | tf_op jit(solution)/shard_map/ppermute | solution.py:448
  36.0 1.3 %collective-permute-start.9 = (bf16[4,16,1024]{2,1,0:T(8,128)(2,1)S(1)}, bf16[4,16,1024]{2,1,0:T(8,128)(2,1)S(1)}, u32[]{:S(2)}, u32[]{:S(2)}) collective-permute-start(bf16[4,16,1024]{2,1,0:T(8,128)(2,1)S(1)} %get-tuple-element.54), channel_id=1, source_target_pairs={{0,16},{4,20},{8,24},{12,28},{16,0},{20,4},{24,8},{28,12},{1,17},{... | collective-permute-start | bytes 393224 | tf_op jit(solution)/shard_map/ppermute | solution.py:448
  37.3 0.7 collective-permute-start.10
  38.0 1.5 %collective-permute-start.8 = (bf16[4,16,1024]{2,1,0:T(8,128)(2,1)S(1)}, bf16[4,16,1024]{2,1,0:T(8,128)(2,1)S(1)}, u32[]{:S(2)}, u32[]{:S(2)}) collective-permute-start(bf16[4,16,1024]{2,1,0:T(8,128)(2,1)S(1)} %get-tuple-element.53.refs_0_), channel_id=1, source_target_pairs={{0,8},{4,12},{8,0},{12,4},{16,24},{20,28},{24,16},{28,20},{1,9},{5... | collective-permute-start | bytes 393224 | tf_op jit(solution)/shard_map/ppermute | solution.py:448
  39.6 7.1 %collective-permute-done.9.refs_2_.refs_1_ = bf16[4,16,1024]{2,1,0:T(8,128)(2,1)S(1)} collective-permute-done((bf16[4,16,1024]{2,1,0:T(8,128)(2,1)S(1)}, bf16[4,16,1024]{2,1,0:T(8,128)(2,1)S(1)}, u32[]{:S(2)}, u32[]{:S(2)}) %collective-permute-start.9) | collective-permute-done | bytes 131104 | tf_op jit(solution)/shard_map/ppermute | solution.py:448
  46.6 0.0 collective-permute-done.10.refs_3_.refs_2_
  46.6 0.7 collective-permute-done.8.refs_1_.refs_0_
  47.4 1.6 %collective-permute-start.16 = (bf16[8,16,1024]{2,1,0:T(8,128)(2,1)S(1)}, bf16[8,16,1024]{2,1,0:T(8,128)(2,1)S(1)}, u32[]{:S(2)}, u32[]{:S(2)}) collective-permute-start(bf16[8,16,1024]{2,1,0:T(8,128)(2,1)S(1)} %gather.2.refs_4_.refs_0_.refs_3_), channel_id=1, source_target_pairs={{0,4},{4,0},{8,12},{12,8},{16,20},{20,16},{24,28},{28,24},{1,5},{5... | collective-permute-start | bytes 786440 | tf_op jit(solution)/shard_map/ppermute | solution.py:452
  49.0 0.0 collective-permute-start.14
  49.1 1.4 %collective-permute-start.13 = (bf16[2,16,1024]{2,1,0:T(8,128)(2,1)S(1)}, bf16[2,16,1024]{2,1,0:T(8,128)(2,1)S(1)}, u32[]{:S(2)}, u32[]{:S(2)}) collective-permute-start(bf16[2,16,1024]{2,1,0:T(8,128)(2,1)S(1)} %part.1.refs_0_), channel_id=1, source_target_pairs={{0,24},{4,28},{8,16},{12,20},{16,8},{20,12},{24,0},{28,4},{1,25},{... | collective-permute-start | bytes 196616 | tf_op jit(solution)/shard_map/ppermute | solution.py:448
  50.4 2.1 %collective-permute-start.12 = (bf16[2,16,1024]{2,1,0:T(8,128)(2,1)S(1)}, bf16[2,16,1024]{2,1,0:T(8,128)(2,1)S(1)}, u32[]{:S(2)}, u32[]{:S(2)}) collective-permute-start(bf16[2,16,1024]{2,1,0:T(8,128)(2,1)S(1)} %part.1.refs_0_), channel_id=1, source_target_pairs={{0,16},{4,20},{8,24},{12,28},{16,0},{20,4},{24,8},{28,12},{1,17},{... | collective-permute-start | bytes 196616 | tf_op jit(solution)/shard_map/ppermute | solution.py:448
  52.6 1.0 %collective-permute-start.11 = (bf16[2,16,1024]{2,1,0:T(8,128)(2,1)S(1)}, bf16[2,16,1024]{2,1,0:T(8,128)(2,1)S(1)}, u32[]{:S(2)}, u32[]{:S(2)}) collective-permute-start(bf16[2,16,1024]{2,1,0:T(8,128)(2,1)S(1)} %part.1.refs_0_), channel_id=1, source_target_pairs={{0,8},{4,12},{8,0},{12,4},{16,24},{20,28},{24,16},{28,20},{1,9},{5... | collective-permute-start | bytes 196616 | tf_op jit(solution)/shard_map/ppermute | solution.py:448
  53.5 1.1 %collective-permute-done.16.refs_0_ = bf16[8,16,1024]{2,1,0:T(8,128)(2,1)S(1)} collective-permute-done((bf16[8,16,1024]{2,1,0:T(8,128)(2,1)S(1)}, bf16[8,16,1024]{2,1,0:T(8,128)(2,1)S(1)}, u32[]{:S(2)}, u32[]{:S(2)}) %collective-permute-start.16) | collective-permute-done | bytes 262176 | tf_op jit(solution)/shard_map/ppermute | solution.py:452
  54.6 0.0 collective-permute-start.17
  54.6 0.0 collective-permute-done.14.refs_1_
  54.6 4.1 %bins.4.refs_4_.refs_0_ = f32[4096,128]{1,0:T(8,128)S(1)} custom-call(bf16[8,16,1024]{2,1,0:T(8,128)(2,1)S(1)} %gather.2.refs_4_.refs_0_.refs_3_, bf16[8,16,1024]{2,1,0:T(8,128)(2,1)S(1)} %collective-permute-done.14.refs_1_, bf16[512,32,128]{2,1,0:T(8,128)(2,1)S(1)} %turn.2.refs_2_.refs_7_.refs_5_, bf16[512,32,128]{2,1,0:T(8,128)(2,1)S(1)} %turn.3.refs_8_.refs_3_), custom_call_target="tpu_custom_call" | custom-call | bytes 16 | tf_op jit(solution)/shard_map/bins/pallas_call | solution.py:46
  58.7 0.0 copy-start.1
  58.7 0.0 copy-start.2
  58.8 0.5 collective-permute-done.12.refs_2_.refs_4_.refs_3_
  59.3 0.0 collective-permute-done.11.refs_1_
  59.3 1.3 %collective-permute-start.20 = (bf16[8,16,1024]{2,1,0:T(8,128)(2,1)S(1)}, bf16[8,16,1024]{2,1,0:T(8,128)(2,1)S(1)}, u32[]{:S(2)}, u32[]{:S(2)}) collective-permute-start(bf16[8,16,1024]{2,1,0:T(8,128)(2,1)S(1)} %gather.3.refs_0_), channel_id=1, source_target_pairs={{0,4},{4,0},{8,12},{12,8},{16,20},{20,16},{24,28},{28,24},{1,5},{5... | collective-permute-start | bytes 786440 | tf_op jit(solution)/shard_map/ppermute | solution.py:452
  60.6 0.2 collective-permute-start.15
  60.8 0.6 lags.5
  61.5 1.6 %collective-permute-start.18 = (bf16[8,32,512]{2,1,0:T(8,128)(2,1)S(1)}, bf16[8,32,512]{2,1,0:T(8,128)(2,1)S(1)}, u32[]{:S(2)}, u32[]{:S(2)}) collective-permute-start(bf16[8,32,512]{2,1,0:T(8,128)(2,1)S(1)} %get-tuple-element.58), channel_id=1, source_target_pairs={{0,2},{1,3},{2,0},{3,1},{4,6},{5,7},{6,4},{7,5},{8,10},{9,11},{10,... | collective-permute-start | bytes 786440 | tf_op jit(solution)/shard_map/ppermute | solution.py:495
  63.1 0.0 collective-permute-done.17.refs_1_
  63.1 4.3 %bins.5.refs_0_ = f32[4096,128]{1,0:T(8,128)S(1)} custom-call(bf16[8,16,1024]{2,1,0:T(8,128)(2,1)S(1)} %collective-permute-done.16.refs_0_, bf16[8,16,1024]{2,1,0:T(8,128)(2,1)S(1)} %collective-permute-done.17.refs_1_, bf16[512,32,128]{2,1,0:T(8,128)(2,1)S(1)} %turn.2.refs_2_.refs_7_.refs_5_, bf16[512,32,128]{2,1,0:T(8,128)(2,1)S(1)} %turn.3.refs_8_.refs_3_, ...), custom_call_target="tpu_custom_call" | custom-call | bytes 16 | tf_op jit(solution)/shard_map/bins/pallas_call | solution.py:46
  67.4 0.6 lags.4
  68.1 0.0 collective-permute-done.20.refs_0_.refs_5_
  68.1 0.1 collective-permute-start.21
  68.1 1.0 %collective-permute-start.22 = (bf16[8,32,512]{2,1,0:T(8,128)(2,1)S(1)}, bf16[8,32,512]{2,1,0:T(8,128)(2,1)S(1)}, u32[]{:S(2)}, u32[]{:S(2)}) collective-permute-start(bf16[8,32,512]{2,1,0:T(8,128)(2,1)S(1)} %get-tuple-element.57.refs_4_), channel_id=1, source_target_pairs={{0,2},{1,3},{2,0},{3,1},{4,6},{5,7},{6,4},{7,5},{8,10},{9,11},{10,... | collective-permute-start | bytes 786440 | tf_op jit(solution)/shard_map/ppermute | solution.py:495
  69.1 4.1 %bins.6.refs_0_.refs_4_ = f32[4096,128]{1,0:T(8,128)S(1)} custom-call(bf16[8,16,1024]{2,1,0:T(8,128)(2,1)S(1)} %gather.3.refs_0_, bf16[8,16,1024]{2,1,0:T(8,128)(2,1)S(1)} %collective-permute-done.15.refs_1_, bf16[512,32,128]{2,1,0:T(8,128)(2,1)S(1)} %turn.2.refs_2_.refs_7_.refs_5_, bf16[512,32,128]{2,1,0:T(8,128)(2,1)S(1)} %turn.3.refs_8_.refs_3_, ...), custom_call_target="tpu_custom_call" | custom-call | bytes 16 | tf_op jit(solution)/shard_map/bins/pallas_call | solution.py:46
  73.3 0.0 collective-permute-done.18.refs_3_.refs_1_
  73.3 0.6 lags.6
  73.9 1.2 %collective-permute-start.19 = (bf16[8,32,512]{2,1,0:T(8,128)(2,1)S(1)}, bf16[8,32,512]{2,1,0:T(8,128)(2,1)S(1)}, u32[]{:S(2)}, u32[]{:S(2)}) collective-permute-start(bf16[8,32,512]{2,1,0:T(8,128)(2,1)S(1)} %get-tuple-element.60), channel_id=1, source_target_pairs={{0,2},{1,3},{2,0},{3,1},{4,6},{5,7},{6,4},{7,5},{8,10},{9,11},{10,... | collective-permute-start | bytes 786440 | tf_op jit(solution)/shard_map/ppermute | solution.py:495
  75.1 0.0 collective-permute-done.21.refs_1_
  75.1 4.1 %bins.7.refs_0_ = f32[4096,128]{1,0:T(8,128)S(1)} custom-call(bf16[8,16,1024]{2,1,0:T(8,128)(2,1)S(1)} %collective-permute-done.20.refs_0_.refs_5_, bf16[8,16,1024]{2,1,0:T(8,128)(2,1)S(1)} %collective-permute-done.21.refs_1_, bf16[512,32,128]{2,1,0:T(8,128)(2,1)S(1)} %turn.2.refs_2_.refs_7_.refs_5_, bf16[512,32,128]{2,1,0:T(8,128)(2,1)S(1)} %turn.3.refs_8_.refs_3_), custom_call_target="tpu_custom_call" | custom-call | bytes 16 | tf_op jit(solution)/shard_map/bins/pallas_call | solution.py:46
  79.3 0.0 copy-start.3
  79.3 0.6 lags.7
  79.9 1.0 %collective-permute-start.23 = (bf16[8,32,512]{2,1,0:T(8,128)(2,1)S(1)}, bf16[8,32,512]{2,1,0:T(8,128)(2,1)S(1)}, u32[]{:S(2)}, u32[]{:S(2)}) collective-permute-start(bf16[8,32,512]{2,1,0:T(8,128)(2,1)S(1)} %get-tuple-element.62), channel_id=1, source_target_pairs={{0,2},{1,3},{2,0},{3,1},{4,6},{5,7},{6,4},{7,5},{8,10},{9,11},{10,... | collective-permute-start | bytes 786440 | tf_op jit(solution)/shard_map/ppermute | solution.py:495
  80.9 0.9 unfold.2.refs_5_
  81.8 0.7 collective-permute-done.19.refs_1_
  82.5 5.6 %collective-permute-done.23.refs_3_ = bf16[8,32,512]{2,1,0:T(8,128)(2,1)S(1)} collective-permute-done((bf16[8,32,512]{2,1,0:T(8,128)(2,1)S(1)}, bf16[8,32,512]{2,1,0:T(8,128)(2,1)S(1)}, u32[]{:S(2)}, u32[]{:S(2)}) %collective-permute-start.23) | collective-permute-done | bytes 262176 | tf_op jit(solution)/shard_map/ppermute | solution.py:495
  88.1 1.9 %unfold.3 = bf16[32,32,512]{2,1,0:T(8,128)(2,1)} custom-call(bf16[8,32,512]{2,1,0:T(8,128)(2,1)S(1)} %get-tuple-element.59.refs_0_, bf16[8,32,512]{2,1,0:T(8,128)(2,1)S(1)} %collective-permute-done.19.refs_1_, bf16[8,32,512]{2,1,0:T(8,128)(2,1)S(1)} %get-tuple-element.61.refs_2_, bf16[8,32,512]{2,1,0:T(8,128)(2,1)S(1)} %collective-permute-done.23.refs_3_, ...), custom_call_target="tpu_custom_call" | custom-call | bytes 16 | tf_op jit(solution)/shard_map/unfold/pallas_call | solution.py:46
  (18 shorter events, 0.2 us)
Async XLA Ops:
  1.1 13.2 %collective-permute-start.1 = (bf16[16,1,1024]{2,1,0:T(2,128)(2,1)S(1)}, bf16[16,1,1024]{2,1,0:T(2,128)(2,1)S(1)}, u32[]{:S(2)}, u32[]{:S(2)}) collective-permute-start(bf16[16,1,1024]{2,1,0:T(2,128)(2,1)S(1)} %get-tuple-element.65), channel_id=1, source_target_pairs={{4,0},{8,4},{12,8},{16,12},{20,16},{24,20},{28,24},{0,28},{5,1},{9... | collective-permute-start | bytes 98312 | tf_op jit(solution)/shard_map/ppermute | solution.py:485
  7.2 7.1 %collective-permute-start = (bf16[16,1,1024]{2,1,0:T(2,128)(2,1)S(1)}, bf16[16,1,1024]{2,1,0:T(2,128)(2,1)S(1)}, u32[]{:S(2)}, u32[]{:S(2)}) collective-permute-start(bf16[16,1,1024]{2,1,0:T(2,128)(2,1)S(1)} %get-tuple-element.66), channel_id=1, source_target_pairs={{0,4},{4,8},{8,12},{12,16},{16,20},{20,24},{24,28},{28,0},{1,5},{5... | collective-permute-start | bytes 98312 | tf_op jit(solution)/shard_map/ppermute | solution.py:484
  7.2 2.2 %copy-start = (bf16[16,128,1024]{2,1,0:T(8,128)(2,1)S(1)}, bf16[16,128,1024]{2,1,0:T(8,128)(2,1)}, u32[]{:S(2)}) copy-start(bf16[16,128,1024]{2,1,0:T(8,128)(2,1)} %refs_0_.2) | copy-start | bytes 12582916
  9.4 5.0 %copy-start.4 = (s32[32]{0:T(128)S(1)}, s32[32]{0:T(128)}, u32[]{:S(2)}) copy-start(s32[32]{0:T(128)} %refs_0_.3) | copy-start | bytes 388
  9.4 5.0 %copy-start.5 = (s32[16]{0:T(128)S(1)}, s32[16]{0:T(128)}, u32[]{:S(2)}) copy-start(s32[16]{0:T(128)} %refs_1_.5) | copy-start | bytes 196
  16.7 14.5 %collective-permute-start.7 = (bf16[16,64,1024]{2,1,0:T(8,128)(2,1)S(1)}, bf16[16,64,1024]{2,1,0:T(8,128)(2,1)S(1)}, u32[]{:S(2)}, u32[]{:S(2)}) collective-permute-start(bf16[16,64,1024]{2,1,0:T(8,128)(2,1)S(1)} %get-tuple-element.52), channel_id=1, source_target_pairs={{0,1},{1,0},{2,3},{3,2},{4,5},{5,4},{6,7},{7,6},{8,9},{9,8},{10,11... | collective-permute-start | bytes 6291464 | tf_op jit(solution)/shard_map/ppermute | solution.py:492
  16.7 9.2 %collective-permute-start.2 = (bf16[8,16,1024]{2,1,0:T(8,128)(2,1)S(1)}, bf16[8,16,1024]{2,1,0:T(8,128)(2,1)S(1)}, u32[]{:S(2)}, u32[]{:S(2)}) collective-permute-start(bf16[8,16,1024]{2,1,0:T(8,128)(2,1)S(1)} %get-tuple-element.40), channel_id=1, source_target_pairs={{0,4},{4,0},{8,12},{12,8},{16,20},{20,16},{24,28},{28,24},{1,5},{5... | collective-permute-start | bytes 786440 | tf_op jit(solution)/shard_map/ppermute | solution.py:444
  16.8 14.3 %collective-permute-start.6 = (bf16[8,16,1024]{2,1,0:T(8,128)(2,1)S(1)}, bf16[8,16,1024]{2,1,0:T(8,128)(2,1)S(1)}, u32[]{:S(2)}, u32[]{:S(2)}) collective-permute-start(bf16[8,16,1024]{2,1,0:T(8,128)(2,1)S(1)} %get-tuple-element.48), channel_id=1, source_target_pairs={{0,4},{4,0},{8,12},{12,8},{16,20},{20,16},{24,28},{28,24},{1,5},{5... | collective-permute-start | bytes 786440 | tf_op jit(solution)/shard_map/ppermute | solution.py:444
  25.9 7.3 %collective-permute-start.3 = (bf16[2,16,1024]{2,1,0:T(8,128)(2,1)S(1)}, bf16[2,16,1024]{2,1,0:T(8,128)(2,1)S(1)}, u32[]{:S(2)}, u32[]{:S(2)}) collective-permute-start(bf16[2,16,1024]{2,1,0:T(8,128)(2,1)S(1)} %get-tuple-element.44), channel_id=1, source_target_pairs={{0,8},{4,12},{8,0},{12,4},{16,24},{20,28},{24,16},{28,20},{1,9},{5... | collective-permute-start | bytes 196616 | tf_op jit(solution)/shard_map/ppermute | solution.py:448
  26.0 8.3 %collective-permute-start.4 = (bf16[2,16,1024]{2,1,0:T(8,128)(2,1)S(1)}, bf16[2,16,1024]{2,1,0:T(8,128)(2,1)S(1)}, u32[]{:S(2)}, u32[]{:S(2)}) collective-permute-start(bf16[2,16,1024]{2,1,0:T(8,128)(2,1)S(1)} %get-tuple-element.45), channel_id=1, source_target_pairs={{0,16},{4,20},{8,24},{12,28},{16,0},{20,4},{24,8},{28,12},{1,17},{... | collective-permute-start | bytes 196616 | tf_op jit(solution)/shard_map/ppermute | solution.py:448
  29.9 6.1 %collective-permute-start.5 = (bf16[2,16,1024]{2,1,0:T(8,128)(2,1)S(1)}, bf16[2,16,1024]{2,1,0:T(8,128)(2,1)S(1)}, u32[]{:S(2)}, u32[]{:S(2)}) collective-permute-start(bf16[2,16,1024]{2,1,0:T(8,128)(2,1)S(1)} %get-tuple-element.46), channel_id=1, source_target_pairs={{0,24},{4,28},{8,16},{12,20},{16,8},{20,12},{24,0},{28,4},{1,25},{... | collective-permute-start | bytes 196616 | tf_op jit(solution)/shard_map/ppermute | solution.py:448
  36.0 10.6 %collective-permute-start.9 = (bf16[4,16,1024]{2,1,0:T(8,128)(2,1)S(1)}, bf16[4,16,1024]{2,1,0:T(8,128)(2,1)S(1)}, u32[]{:S(2)}, u32[]{:S(2)}) collective-permute-start(bf16[4,16,1024]{2,1,0:T(8,128)(2,1)S(1)} %get-tuple-element.54), channel_id=1, source_target_pairs={{0,16},{4,20},{8,24},{12,28},{16,0},{20,4},{24,8},{28,12},{1,17},{... | collective-permute-start | bytes 393224 | tf_op jit(solution)/shard_map/ppermute | solution.py:448
  37.3 9.3 %collective-permute-start.10 = (bf16[4,16,1024]{2,1,0:T(8,128)(2,1)S(1)}, bf16[4,16,1024]{2,1,0:T(8,128)(2,1)S(1)}, u32[]{:S(2)}, u32[]{:S(2)}) collective-permute-start(bf16[4,16,1024]{2,1,0:T(8,128)(2,1)S(1)} %get-tuple-element.55), channel_id=1, source_target_pairs={{0,24},{4,28},{8,16},{12,20},{16,8},{20,12},{24,0},{28,4},{1,25},{... | collective-permute-start | bytes 393224 | tf_op jit(solution)/shard_map/ppermute | solution.py:448
  38.0 9.4 %collective-permute-start.8 = (bf16[4,16,1024]{2,1,0:T(8,128)(2,1)S(1)}, bf16[4,16,1024]{2,1,0:T(8,128)(2,1)S(1)}, u32[]{:S(2)}, u32[]{:S(2)}) collective-permute-start(bf16[4,16,1024]{2,1,0:T(8,128)(2,1)S(1)} %get-tuple-element.53.refs_0_), channel_id=1, source_target_pairs={{0,8},{4,12},{8,0},{12,4},{16,24},{20,28},{24,16},{28,20},{1,9},{5... | collective-permute-start | bytes 393224 | tf_op jit(solution)/shard_map/ppermute | solution.py:448
  47.4 7.2 %collective-permute-start.16 = (bf16[8,16,1024]{2,1,0:T(8,128)(2,1)S(1)}, bf16[8,16,1024]{2,1,0:T(8,128)(2,1)S(1)}, u32[]{:S(2)}, u32[]{:S(2)}) collective-permute-start(bf16[8,16,1024]{2,1,0:T(8,128)(2,1)S(1)} %gather.2.refs_4_.refs_0_.refs_3_), channel_id=1, source_target_pairs={{0,4},{4,0},{8,12},{12,8},{16,20},{20,16},{24,28},{28,24},{1,5},{5... | collective-permute-start | bytes 786440 | tf_op jit(solution)/shard_map/ppermute | solution.py:452
  49.0 5.5 %collective-permute-start.14 = (bf16[8,16,1024]{2,1,0:T(8,128)(2,1)S(1)}, bf16[8,16,1024]{2,1,0:T(8,128)(2,1)S(1)}, u32[]{:S(2)}, u32[]{:S(2)}) collective-permute-start(bf16[8,16,1024]{2,1,0:T(8,128)(2,1)S(1)} %gather.2.refs_4_.refs_0_.refs_3_), channel_id=1, source_target_pairs={{0,1},{1,0},{2,3},{3,2},{4,5},{5,4},{6,7},{7,6},{8,9},{9,8},{10,11... | collective-permute-start | bytes 786440 | tf_op jit(solution)/shard_map/ppermute | solution.py:492
  49.1 9.7 %collective-permute-start.13 = (bf16[2,16,1024]{2,1,0:T(8,128)(2,1)S(1)}, bf16[2,16,1024]{2,1,0:T(8,128)(2,1)S(1)}, u32[]{:S(2)}, u32[]{:S(2)}) collective-permute-start(bf16[2,16,1024]{2,1,0:T(8,128)(2,1)S(1)} %part.1.refs_0_), channel_id=1, source_target_pairs={{0,24},{4,28},{8,16},{12,20},{16,8},{20,12},{24,0},{28,4},{1,25},{... | collective-permute-start | bytes 196616 | tf_op jit(solution)/shard_map/ppermute | solution.py:448
  50.4 8.8 %collective-permute-start.12 = (bf16[2,16,1024]{2,1,0:T(8,128)(2,1)S(1)}, bf16[2,16,1024]{2,1,0:T(8,128)(2,1)S(1)}, u32[]{:S(2)}, u32[]{:S(2)}) collective-permute-start(bf16[2,16,1024]{2,1,0:T(8,128)(2,1)S(1)} %part.1.refs_0_), channel_id=1, source_target_pairs={{0,16},{4,20},{8,24},{12,28},{16,0},{20,4},{24,8},{28,12},{1,17},{... | collective-permute-start | bytes 196616 | tf_op jit(solution)/shard_map/ppermute | solution.py:448
  52.6 6.7 %collective-permute-start.11 = (bf16[2,16,1024]{2,1,0:T(8,128)(2,1)S(1)}, bf16[2,16,1024]{2,1,0:T(8,128)(2,1)S(1)}, u32[]{:S(2)}, u32[]{:S(2)}) collective-permute-start(bf16[2,16,1024]{2,1,0:T(8,128)(2,1)S(1)} %part.1.refs_0_), channel_id=1, source_target_pairs={{0,8},{4,12},{8,0},{12,4},{16,24},{20,28},{24,16},{28,20},{1,9},{5... | collective-permute-start | bytes 196616 | tf_op jit(solution)/shard_map/ppermute | solution.py:448
  54.6 8.5 %collective-permute-start.17 = (bf16[8,16,1024]{2,1,0:T(8,128)(2,1)S(1)}, bf16[8,16,1024]{2,1,0:T(8,128)(2,1)S(1)}, u32[]{:S(2)}, u32[]{:S(2)}) collective-permute-start(bf16[8,16,1024]{2,1,0:T(8,128)(2,1)S(1)} %collective-permute-done.16.refs_0_), channel_id=1, source_target_pairs={{0,1},{1,0},{2,3},{3,2},{4,5},{5,4},{6,7},{7,6},{8,9},{9,8},{10,11... | collective-permute-start | bytes 786440 | tf_op jit(solution)/shard_map/ppermute | solution.py:492
  58.7 2.1 %copy-start.1 = (bf16[272,512]{1,0:T(8,128)(2,1)S(1)}, bf16[272,512]{1,0:T(8,128)(2,1)}, u32[]{:S(2)}) copy-start(bf16[272,512]{1,0:T(8,128)(2,1)} %constant.6.clone.refs_1_) | copy-start | bytes 835588
  58.7 2.1 %copy-start.2 = (bf16[256,512]{1,0:T(8,128)(2,1)S(1)}, bf16[256,512]{1,0:T(8,128)(2,1)}, u32[]{:S(2)}) copy-start(bf16[256,512]{1,0:T(8,128)(2,1)} %constant.7.clone.refs_2_) | copy-start | bytes 786436
  59.3 8.8 %collective-permute-start.20 = (bf16[8,16,1024]{2,1,0:T(8,128)(2,1)S(1)}, bf16[8,16,1024]{2,1,0:T(8,128)(2,1)S(1)}, u32[]{:S(2)}, u32[]{:S(2)}) collective-permute-start(bf16[8,16,1024]{2,1,0:T(8,128)(2,1)S(1)} %gather.3.refs_0_), channel_id=1, source_target_pairs={{0,4},{4,0},{8,12},{12,8},{16,20},{20,16},{24,28},{28,24},{1,5},{5... | collective-permute-start | bytes 786440 | tf_op jit(solution)/shard_map/ppermute | solution.py:452
  60.6 8.5 %collective-permute-start.15 = (bf16[8,16,1024]{2,1,0:T(8,128)(2,1)S(1)}, bf16[8,16,1024]{2,1,0:T(8,128)(2,1)S(1)}, u32[]{:S(2)}, u32[]{:S(2)}) collective-permute-start(bf16[8,16,1024]{2,1,0:T(8,128)(2,1)S(1)} %gather.3.refs_0_), channel_id=1, source_target_pairs={{0,1},{1,0},{2,3},{3,2},{4,5},{5,4},{6,7},{7,6},{8,9},{9,8},{10,11... | collective-permute-start | bytes 786440 | tf_op jit(solution)/shard_map/ppermute | solution.py:492
  61.5 11.8 %collective-permute-start.18 = (bf16[8,32,512]{2,1,0:T(8,128)(2,1)S(1)}, bf16[8,32,512]{2,1,0:T(8,128)(2,1)S(1)}, u32[]{:S(2)}, u32[]{:S(2)}) collective-permute-start(bf16[8,32,512]{2,1,0:T(8,128)(2,1)S(1)} %get-tuple-element.58), channel_id=1, source_target_pairs={{0,2},{1,3},{2,0},{3,1},{4,6},{5,7},{6,4},{7,5},{8,10},{9,11},{10,... | collective-permute-start | bytes 786440 | tf_op jit(solution)/shard_map/ppermute | solution.py:495
  68.1 7.0 %collective-permute-start.21 = (bf16[8,16,1024]{2,1,0:T(8,128)(2,1)S(1)}, bf16[8,16,1024]{2,1,0:T(8,128)(2,1)S(1)}, u32[]{:S(2)}, u32[]{:S(2)}) collective-permute-start(bf16[8,16,1024]{2,1,0:T(8,128)(2,1)S(1)} %collective-permute-done.20.refs_0_.refs_5_), channel_id=1, source_target_pairs={{0,1},{1,0},{2,3},{3,2},{4,5},{5,4},{6,7},{7,6},{8,9},{9,8},{10,11... | collective-permute-start | bytes 786440 | tf_op jit(solution)/shard_map/ppermute | solution.py:492
  68.1 11.1 %collective-permute-start.22 = (bf16[8,32,512]{2,1,0:T(8,128)(2,1)S(1)}, bf16[8,32,512]{2,1,0:T(8,128)(2,1)S(1)}, u32[]{:S(2)}, u32[]{:S(2)}) collective-permute-start(bf16[8,32,512]{2,1,0:T(8,128)(2,1)S(1)} %get-tuple-element.57.refs_4_), channel_id=1, source_target_pairs={{0,2},{1,3},{2,0},{3,1},{4,6},{5,7},{6,4},{7,5},{8,10},{9,11},{10,... | collective-permute-start | bytes 786440 | tf_op jit(solution)/shard_map/ppermute | solution.py:495
  73.9 8.6 %collective-permute-start.19 = (bf16[8,32,512]{2,1,0:T(8,128)(2,1)S(1)}, bf16[8,32,512]{2,1,0:T(8,128)(2,1)S(1)}, u32[]{:S(2)}, u32[]{:S(2)}) collective-permute-start(bf16[8,32,512]{2,1,0:T(8,128)(2,1)S(1)} %get-tuple-element.60), channel_id=1, source_target_pairs={{0,2},{1,3},{2,0},{3,1},{4,6},{5,7},{6,4},{7,5},{8,10},{9,11},{10,... | collective-permute-start | bytes 786440 | tf_op jit(solution)/shard_map/ppermute | solution.py:495
  79.3 1.6 %copy-start.3 = (bf16[512,512]{1,0:T(8,128)(2,1)S(1)}, bf16[512,512]{1,0:T(8,128)(2,1)}, u32[]{:S(2)}) copy-start(bf16[512,512]{1,0:T(8,128)(2,1)} %constant.8.clone.refs_4_) | copy-start | bytes 1572868
  79.9 8.2 %collective-permute-start.23 = (bf16[8,32,512]{2,1,0:T(8,128)(2,1)S(1)}, bf16[8,32,512]{2,1,0:T(8,128)(2,1)S(1)}, u32[]{:S(2)}, u32[]{:S(2)}) collective-permute-start(bf16[8,32,512]{2,1,0:T(8,128)(2,1)S(1)} %get-tuple-element.62), channel_id=1, source_target_pairs={{0,2},{1,3},{2,0},{3,1},{4,6},{5,7},{6,4},{7,5},{8,10},{9,11},{10,... | collective-permute-start | bytes 786440 | tf_op jit(solution)/shard_map/ppermute | solution.py:495

commit v5 on v4

--- a/solution.py
+++ b/solution.py
@@ -16,17 +16,18 @@
 CHUNKS = 2
 LANES = 128
 AFTER = {
-    "own_first": ("turned0", "turned1"),
-    "lags2": ("far0",),
-    "lags3": ("far1", "sums2", "theirs_b"),
-    "lags1": ("other1",),
-    "end0": ("far1",),
-    "bins1": ("other1",),
-    "bins2": ("leave1",),
-    "lags0": ("mine_a",),
-    "part": ("mine_a", "turned0"),
-    "gather": ("sums0",),
-    "meet_a": ("turned0",),
+    "halve": ("pieces_a",),
+    "own_first": ("turned0",),
+    "gather_a": ("turned1",),
+    "lags3": ("far2", "sums1"),
+    "gather": ("leave0", "mine_a_near", "other0", "own_b", "theirs_a"),
+    "bins3": ("leave1", "sums1", "sums2", "theirs_b", "theirs_b_near"),
+    "lags1": ("far0", "other2"),
+    "end0": ("leave1", "leave2", "sums1", "theirs_b"),
+    "bins1": ("mine_b", "other0", "theirs_b"),
+    "part": ("pieces_a",),
+    "lags0": ("mine_a", "other0", "other1", "sums0", "turned1"),
+    "lags2": ("leave0",),
 }
 F32 = jnp.float32
 BF16 = jnp.bfloat16
@@ -37,7 +38,7 @@
 HBM = pl.BlockSpec(memory_space=pltpu.HBM)
 
 
-def call(kernel, ins, in_specs, outs, scratch, limit, name, after=()):
+def call(kernel, ins, in_specs, outs, scratch, limit, name, after=(), aliases=None):
     count = len(ins)
 
     def body(*refs):
@@ -49,6 +50,7 @@
         out_specs=[VMEM] * len(outs),
         out_shape=[jax.ShapeDtypeStruct(shape, dtype) for shape, dtype in outs],
         scratch_shapes=scratch,
+        input_output_aliases=aliases or {},
         compiler_params=pltpu.CompilerParams(vmem_limit_bytes=limit * MIB),
         cost_estimate=pl.CostEstimate(flops=0, bytes_accessed=16, transcendentals=0),
         name=name,
@@ -75,6 +77,11 @@
     return chunk * per_chunk + (x ^ half) * 4 * quarter + (z ^ part) * quarter + i
 
 
+def source_row(blocks, r, count):
+    per_chunk = count // CHUNKS
+    return r // per_chunk * per_chunk + source_at(blocks, r % per_chunk, per_chunk)
+
+
 def amplitude(values):
     freqs = values.shape[-1] // 2
     real, imag = values[:, :freqs], values[:, freqs:]
@@ -92,6 +99,18 @@
     divisor = jnp.dot(triple, band, preferred_element_type=F32) * share + EPSILON
     near = pl.reciprocal(divisor, approx=True)
     return near * (2.0 - divisor * near)
+
+
+def rim_kernel(spec_ref, first_ref, last_ref):
+    windows, chans, _ = spec_ref.shape
+    for w in range(windows):
+        first_ref[w] = spec_ref[w, :16].astype(F32)[:1].astype(BF16)
+        last_ref[w] = spec_ref[w, chans - 16 :].astype(F32)[15:].astype(BF16)
+
+
+def rim(spectra):
+    windows, _, width = spectra.shape
+    return call(rim_kernel, (spectra,), [VMEM], [((windows, 1, width), BF16)] * 2, [], 8, "rim")
 
 
 def whiten_kernel(spec_ref, white_ref, band, part_ref, raw_ref, buf, tri, inv, sems):
@@ -228,10 +247,10 @@
                     out[w, q * share : (q + 1) * share, lanes] = body.astype(BF16)
 
 
-def halve(parts, white, edge, chans):
+def halve(parts, white, edge, chans, after):
     _, windows, width = edge.shape
     shape = (windows, 2 * chans // parts, width)
-    return call(halve_kernel, (white, edge), [VMEM] * 2, [(shape, BF16)] * 2, [], 8, "halve")
+    return call(halve_kernel, (white, edge), [VMEM] * 2, [(shape, BF16)] * 2, [], 8, "halve", after)
 
 
 def turn_kernel(white_ref, out_ref, held):
@@ -327,30 +346,35 @@
     tile = LANES
     pairs = rows // 2
     for p in range(pairs):
-        whole, crossed = [], []
+        pieces = []
         for s in (2 * p, 2 * p + 1):
             for ref in (own_ref, other_ref):
                 v = ref[s].astype(F32)
-                whole += [v[:, :freqs], v[:, freqs:]]
-                crossed += [-v[:, freqs:], v[:, :freqs]]
-        for k, pieces in enumerate((whole, crossed)):
-            stack = jnp.concatenate(pieces, axis=0)
-            for j in range(freqs // tile):
-                turned = stack[:, j * tile : (j + 1) * tile].T
-                at = j * tile * 2 * rows + k * pairs + p
-                vt[pl.ds(at, tile, stride=2 * rows), :] = turned
-                vt[pl.ds(at + rows, tile, stride=2 * rows), :] = pltpu.roll(turned, tile // 2, 1)
-
-    first = lax.broadcasted_iota(jnp.int32, (rows, lanes), 1) < lanes // 2
+                pieces += [v[:, :freqs], v[:, freqs:]]
+        stack = jnp.concatenate(pieces, axis=0)
+        for j in range(freqs // tile):
+            turned = stack[:, j * tile : (j + 1) * tile].T
+            at = j * tile * rows + p
+            vt[pl.ds(at, tile, stride=rows), :] = turned
+            vt[pl.ds(at + pairs, tile, stride=rows), :] = pltpu.roll(turned, tile // 2, 1)
+
+    left = lax.broadcasted_iota(jnp.int32, (rows, lanes), 1) < lanes // 2
+    top = lax.broadcasted_iota(jnp.int32, (rows, lanes), 0) < pairs
     unroll = 256
 
     def step(i, carry):
         for k in range(unroll):
             f = i * unroll + k
-            lhs = vt[pl.ds(pl.multiple_of(f * 2 * rows, 8), 2 * rows), : 2 * depth].astype(BF16)
-            x = jnp.concatenate([low_ref[f], high_ref[f]], axis=0)
-            sums = jnp.dot(lhs, x, preferred_element_type=F32)
-            st[pl.ds(pl.multiple_of(f * rows, 8), rows), :] = jnp.where(first, sums[:rows], sums[rows:])
+            at = pl.multiple_of(f * rows, 8)
+            lhs = vt[pl.ds(at, rows), : 2 * depth].astype(BF16)
+            a, b = low_ref[f], high_ref[f]
+            straight = jnp.concatenate([a, b], axis=0)
+            crossed = jnp.concatenate([a[windows:], -a[:windows], b[windows:], -b[:windows]], axis=0)
+            sums = jnp.dot(lhs, jnp.concatenate([straight, crossed], axis=1), preferred_element_type=F32)
+            real, imag = sums[:, :lanes], sums[:, lanes:]
+            even = jnp.where(top, real, pltpu.roll(imag, pairs, 0))
+            odd = jnp.where(top, pltpu.roll(real, pairs, 0), imag)
+            st[pl.ds(at, rows), :] = jnp.where(left, even, odd)
         return carry
 
     lax.fori_loop(0, freqs // unroll, step, 0)
@@ -364,7 +388,7 @@
         (own, other, *turned),
         [VMEM] * 4,
         [((held, LANES), F32)],
-        [pltpu.VMEM((2 * held, LANES), F32)],
+        [pltpu.VMEM((held, LANES), F32)],
         10,
         "bins",
         after,
@@ -401,42 +425,45 @@
     return call(lags_kernel, (sums, *tables), [VMEM] * 3, [(shape, BF16)] * 2, [], 10, "lags", after)
 
 
-def unfold_kernel(blocks, pairs, *refs):
-    ins, mix_ref, earlier, (out_ref, held) = refs[: 2 * pairs], refs[2 * pairs], refs[2 * pairs + 1 : -2], refs[-2:]
-    rows, chans, lags = ins[0].shape
-    per_chunk = pairs * rows
-    pitch = per_chunk + 8
-    for pair in range(pairs):
+def unfold_kernel(blocks, starts, sources, *refs):
+    ins, mix_ref, outs = refs[: 2 * len(starts)], refs[2 * len(starts)], refs[2 * len(starts) + 1 :]
+    held = outs[-1]
+    chans, lags = ins[0].shape[1:]
+    pitch = sources + 8
+    for k, start in enumerate(starts):
+        rows = ins[2 * k].shape[0]
         total = jnp.zeros((rows * chans, lags), F32)
-        for ref in ins[2 * pair : 2 * pair + 2]:
+        for ref in ins[2 * k : 2 * k + 2]:
             flat = ref[...].reshape(rows * chans, lags)
             total = total + jnp.dot(flat, mix_ref[...], preferred_element_type=F32)
         for r in range(rows):
-            at = source_at(blocks, pair * rows + r, per_chunk)
+            at = source_row(blocks, start + r, sources)
             for j in range(lags // LANES):
                 lanes = slice(j * LANES, (j + 1) * LANES)
                 held[j, pl.ds(at, chans, stride=pitch), :] = total[r * chans : (r + 1) * chans, lanes]
-    first = out_ref.shape[1] - per_chunk
-    for c in range(chans):
-        if earlier:
-            out_ref[c, :first, :] = earlier[0][c]
-        for j in range(lags // LANES):
-            lanes = slice(j * LANES, (j + 1) * LANES)
-            out_ref[c, first:, lanes] = held[j, c * pitch : c * pitch + per_chunk, :].astype(BF16)
-
-
-def unfold(blocks, ins, mix, earlier, after):
-    rows, chans, lags = ins[0].shape
-    per_chunk = len(ins) // 2 * rows
+    if len(outs) == 3:
+        out_ref = outs[1]
+        for c in range(chans):
+            for j in range(lags // LANES):
+                lanes = slice(j * LANES, (j + 1) * LANES)
+                out_ref[c, :, lanes] = held[j, c * pitch : c * pitch + sources, :].astype(BF16)
+
+
+def unfold(blocks, starts, sources, ins, mix, earlier, after):
+    chans, lags = ins[0].shape[1:]
+    held = ((lags // LANES, chans * (sources + 8), LANES), F32)
+    outs = [((chans, sources, lags), BF16), held] if earlier else [held]
+    count = len(ins) + 1
     return call(
-        functools.partial(unfold_kernel, blocks, len(ins) // 2),
+        functools.partial(unfold_kernel, blocks, starts, sources),
         (*ins, mix, *earlier),
-        [VMEM] * (len(ins) + 1 + len(earlier)),
-        [((chans, per_chunk * (1 + len(earlier)), lags), BF16)],
-        [pltpu.VMEM((lags // LANES, chans * (per_chunk + 8), LANES), F32)],
+        [VMEM] * (count + len(earlier)),
+        outs,
+        [],
         16,
         "unfold",
         after,
+        {count: 1} if earlier else None,
     )[0]
 
 
@@ -481,8 +508,9 @@
     freqs = width // 2
     forward = [(i, (i + 1) % blocks) for i in range(blocks)]
     backward = [(b, a) for a, b in forward]
-    low = lax.ppermute(spectra[:, chans - 1 :, :], "chan", forward)
-    high = lax.ppermute(spectra[:, :1, :], "chan", backward)
+    first, last = rim(spectra)
+    low = lax.ppermute(last, "chan", forward)
+    high = lax.ppermute(first, "chan", backward)
     white, band, edge_sums, raw = whiten(spectra)
     *picks, edge = edges(blocks, chans, valid, sources, low, high, white, band, edge_sums, raw)
     tables = lag_tables(freqs, windows)
@@ -494,9 +522,7 @@
     def far(array):
         return lax.ppermute(array, "win", xor_pairs(parts, 2))
 
-    keep, send = halve(parts, white, edge, chans)
-    turned = [turn(keep), turn(near(send))]
-    made = {"turned0": turned[0], "turned1": turned[1]}
+    made = {}
     ends = []
 
     def after(name):
@@ -507,7 +533,7 @@
         made[name + "_near"] = near(rows)
 
     def put(i, name):
-        made[f"sums{i}"] = bins(made[name], made[name + "_near"], turned, after(f"bins{i}"))
+        made[f"sums{i}"] = bins(made[name], made[name + "_near"], (made["turned0"], made["turned1"]), after(f"bins{i}"))
 
     def transform(i):
         sums = made[f"sums{i}"]
@@ -516,16 +542,19 @@
         made[f"far{i}"] = far(leave)
         ends.extend([stay, made[f"far{i}"]])
 
-    def end(chunk, earlier):
-        return unfold(blocks, ends[4 * chunk : 4 * chunk + 4], mix, earlier, after(f"end{chunk}"))
+    def turn_halves():
+        keep, send = halve(parts, white, edge, chans, after("halve"))
+        made["turned0"], made["turned1"] = turn(keep), turn(near(send))
 
     if blocks == 8:
-        pieces_a = meet_x(picks[0], picks[1], after("meet_a"))
+        pieces_a = meet_x(picks[0], picks[1], ())
         pieces_b = meet_x(picks[2], picks[3], ())
+        made["pieces_a"] = pieces_a[0]
+        turn_halves()
         sent = own_first([pieces_a[0]] + over_z(pieces_a[1:]), pieces_b[1:], after("own_first"))
         came = over_z(sent)
         rows = pieces_b[0].shape[0]
-        swap("mine_a", gather((sent[0], *came), rows))
+        swap("mine_a", gather((sent[0], *came), rows, after("gather_a")))
         swap("theirs_a", over_x(made["mine_a"]))
         made["own_b"] = own_b = part(came, pieces_b[0], after("part"))
         others = over_z([own_b] * 3)
@@ -535,6 +564,7 @@
         swap("mine_b", gather((own_b, *others), rows, after("gather")))
         swap("theirs_b", over_x(made["mine_b"]))
     else:
+        turn_halves()
         for name, pick in zip(("mine_a", "theirs_a", "mine_b", "theirs_b"), picks):
             swap(name, lax.psum(pick, "chan"))
         put(0, "mine_a")
@@ -542,7 +572,10 @@
     for i, name in ((1, "theirs_a"), (2, "mine_b"), (3, "theirs_b")):
         put(i, name)
         transform(i)
-    return end(1, (end(0, ()),))
+    count = sources.shape[0]
+    starts = [k * count // 4 for k in range(4)]
+    held = unfold(blocks, starts[:3], count, ends[:6], mix, (), after("end0"))
+    return unfold(blocks, starts[3:], count, ends[6:], mix, (held,), after("end1"))
 
 
 def solution(mesh):

time: 90.5 us -> 88.9 us (0.982)
  waiting for transfers between devices: 24 us -> 28.8 us
  Pallas kernels: 33.7 us -> 29.4 us
  local copies, waits for them, and re-layouts: 3.35 us -> 2.22 us
    pallas_call x21 -> x22, Pallas kernels: 33.7 us -> 29.4 us  [call(): pl.pallas_call(body, in_specs=[*in_specs] + [ANY] * len(after), out_specs...]
    ppermute x2, waiting for transfers between devices: 5.63 us -> 9.6 us  [meet_x(): return add_parts(keep, lax.ppermute(send, 'chan', xor_pairs(8, 1)), after)]
    ppermute x2, starting transfers between devices: 2.08 us -> 0.42 us  [meet_x(): return add_parts(keep, lax.ppermute(send, 'chan', xor_pairs(8, 1)), after)]
    ppermute x9, starting transfers between devices: 12.5 us -> 14.1 us  [over_z(): lax.ppermute(array, 'chan', xor_pairs(8, 2 * p))]
    ppermute x9, waiting for transfers between devices: 11 us -> 9.43 us  [over_z(): lax.ppermute(array, 'chan', xor_pairs(8, 2 * p))]
    ppermute x4, waiting for transfers between devices: 6.31 us -> 7.54 us  [far(): return lax.ppermute(array, 'win', xor_pairs(parts, 2))]
    ppermute x2, waiting for transfers between devices: 1.06 us -> 2.22 us  [over_x(): return lax.ppermute(array, 'chan', xor_pairs(8, 1))]
    slice x1 -> x0, local copies, waits for them, and re-layouts: 1.13 us -> none  [on_device(): high = lax.ppermute(spectra[:, :1, :], 'chan', backward)]
  transfers between devices with their start and end apart: 24 -> 24, of which waited for: 10 -> 9; matrix products, arithmetic and copies ran while one was open for 0% -> 0% of each run, Pallas kernels for 33% -> 28%
where the time goes in v5:
time: 88.9 us; the launch traced here: 88.8 us
  Pallas kernels  29.4 us (33%)
  waiting for transfers between devices  28.8 us (32%)
  starting transfers between devices  28.1 us (32%)
  local copies, waits for them, and re-layouts  2.22 us (2%)
    pallas_call x22, Pallas kernels, call(): pl.pallas_call(body, in_specs=[*in_specs] + [ANY] * len(after), out_specs...  29.4 us
    ppermute x9, starting transfers between devices, over_z(): lax.ppermute(array, 'chan', xor_pairs(8, 2 * p))  14.1 us
    ppermute x2, waiting for transfers between devices, meet_x(): return add_parts(keep, lax.ppermute(send, 'chan', xor_pairs(8, 1)), after)  9.6 us
    ppermute x9, waiting for transfers between devices, over_z(): lax.ppermute(array, 'chan', xor_pairs(8, 2 * p))  9.43 us
    ppermute x4, waiting for transfers between devices, far(): return lax.ppermute(array, 'win', xor_pairs(parts, 2))  7.54 us
    ppermute x4, starting transfers between devices, far(): return lax.ppermute(array, 'win', xor_pairs(parts, 2))  5.21 us
    ppermute x1, starting transfers between devices, on_device(): high = lax.ppermute(first, 'chan', backward)  3.12 us
    ppermute x1, starting transfers between devices, on_device(): low = lax.ppermute(last, 'chan', forward)  2.99 us
  transfers between devices with their start and end apart: 24, of which 9 were waited for; matrix products, arithmetic and copies ran while one was open for 0% of the time, Pallas kernels for 28%

profile of v5, /device:TPU:0, one launch (start us, length us, event | category | flops | bytes accessed | tf_op | source)
XLA Modules:
  0.0 88.8 jit_solution(8865072781999460694)
XLA Ops:
  0.0 2.2 %copy-done = bf16[16,128,1024]{2,1,0:T(8,128)(2,1)S(1)} copy-done((bf16[16,128,1024]{2,1,0:T(8,128)(2,1)S(1)}, bf16[16,128,1024]{2,1,0:T(8,128)(2,1)}, u32[]{:S(2)}) %copy-start) | copy-done | bytes 4194328
  2.2 0.1 rim.1
  2.2 3.0 %collective-permute-start = (bf16[16,1,1024]{2,1,0:T(2,128)(2,1)S(1)}, bf16[16,1,1024]{2,1,0:T(2,128)(2,1)S(1)}, u32[]{:S(2)}, u32[]{:S(2)}) collective-permute-start(bf16[16,1,1024]{2,1,0:T(2,128)(2,1)S(1)} %get-tuple-element.38), channel_id=1, source_target_pairs={{0,4},{4,8},{8,12},{12,16},{16,20},{20,24},{24,28},{28,0},{1,5},{5... | collective-permute-start | bytes 98312 | tf_op jit(solution)/shard_map/ppermute | solution.py:512
  5.2 3.1 %collective-permute-start.1 = (bf16[16,1,1024]{2,1,0:T(2,128)(2,1)S(1)}, bf16[16,1,1024]{2,1,0:T(2,128)(2,1)S(1)}, u32[]{:S(2)}, u32[]{:S(2)}) collective-permute-start(bf16[16,1,1024]{2,1,0:T(2,128)(2,1)S(1)} %get-tuple-element.39), channel_id=1, source_target_pairs={{4,0},{8,4},{12,8},{16,12},{20,16},{24,20},{28,24},{0,28},{5,1},{9... | collective-permute-start | bytes 98312 | tf_op jit(solution)/shard_map/ppermute | solution.py:513
  8.4 4.9 %whiten.1 = (f32[8,2176,128]{2,1,0:T(8,128)S(1)}, bf16[512,512]{1,0:T(8,128)(2,1)S(1)}, f32[2,16,512]{2,1,0:T(8,128)S(1)}, f32[2,16,1024]{2,1,0:T(8,128)S(1)}) custom-call(bf16[16,128,1024]{2,1,0:T(8,128)(2,1)S(1)} %copy-done.1), custom_call_target="tpu_custom_call" | custom-call | bytes 16 | tf_op jit(solution)/shard_map/whiten/pallas_call | solution.py:47
  13.3 0.0 collective-permute-done.refs_2_
  13.3 0.0 collective-permute-done.1.refs_3_
  13.3 1.7 %edges.1 = (bf16[8,16,1024]{2,1,0:T(8,128)(2,1)S(1)}, bf16[8,16,1024]{2,1,0:T(8,128)(2,1)S(1)}, bf16[8,16,1024]{2,1,0:T(8,128)(2,1)S(1)}, bf16[8,16,1024]{2,1,0:T(8,128)(2,1)S(1)}, f32[2,16,1024]{2,1,0:T(8,128)S(1)}) custom-call(s32[32]{0:T(128)S(1)} %copy-done.5, s32[16]{0:T(128)S(1)} %copy-done.6, bf16[16,1,1024]{2,1,0:T(2,128)(2,1)S(1)} %collective-permute-done.refs_2_, ...), custom_call_target="tpu_custom_call" | custom-call | bytes 16 | tf_op jit(solution)/shard_map/edges/pallas_call | solution.py:47
  15.1 0.1 collective-permute-start.2
  15.1 7.8 %collective-permute-done.2.refs_1_ = bf16[8,16,1024]{2,1,0:T(8,128)(2,1)S(1)} collective-permute-done((bf16[8,16,1024]{2,1,0:T(8,128)(2,1)S(1)}, bf16[8,16,1024]{2,1,0:T(8,128)(2,1)S(1)}, u32[]{:S(2)}, u32[]{:S(2)}) %collective-permute-start.2) | collective-permute-done | bytes 262176 | tf_op jit(solution)/shard_map/ppermute | solution.py:471
  22.9 0.6 halve.1
  23.6 0.1 collective-permute-start.13
  23.6 0.4 collective-permute-start.6
  24.0 0.5 collective-permute-start.3
  24.5 2.6 %collective-permute-start.4 = (bf16[2,16,1024]{2,1,0:T(8,128)(2,1)S(1)}, bf16[2,16,1024]{2,1,0:T(8,128)(2,1)S(1)}, u32[]{:S(2)}, u32[]{:S(2)}) collective-permute-start(bf16[2,16,1024]{2,1,0:T(8,128)(2,1)S(1)} %get-tuple-element.48), channel_id=1, source_target_pairs={{0,16},{4,20},{8,24},{12,28},{16,0},{20,4},{24,8},{28,12},{1,17},{... | collective-permute-start | bytes 196616 | tf_op jit(solution)/shard_map/ppermute | solution.py:475
  27.1 1.3 %collective-permute-start.5 = (bf16[2,16,1024]{2,1,0:T(8,128)(2,1)S(1)}, bf16[2,16,1024]{2,1,0:T(8,128)(2,1)S(1)}, u32[]{:S(2)}, u32[]{:S(2)}) collective-permute-start(bf16[2,16,1024]{2,1,0:T(8,128)(2,1)S(1)} %get-tuple-element.49), channel_id=1, source_target_pairs={{0,24},{4,28},{8,16},{12,20},{16,8},{20,12},{24,0},{28,4},{1,25},{... | collective-permute-start | bytes 196616 | tf_op jit(solution)/shard_map/ppermute | solution.py:475
  28.4 2.1 %turn.2.refs_7_.refs_2_ = bf16[512,32,128]{2,1,0:T(8,128)(2,1)S(1)} custom-call(bf16[16,64,1024]{2,1,0:T(8,128)(2,1)S(1)} %get-tuple-element.56.refs_0_), custom_call_target="tpu_custom_call" | custom-call | bytes 16 | tf_op jit(solution)/shard_map/turn/pallas_call | solution.py:47
  30.5 1.8 %collective-permute-done.6.refs_1_ = bf16[8,16,1024]{2,1,0:T(8,128)(2,1)S(1)} collective-permute-done((bf16[8,16,1024]{2,1,0:T(8,128)(2,1)S(1)}, bf16[8,16,1024]{2,1,0:T(8,128)(2,1)S(1)}, u32[]{:S(2)}, u32[]{:S(2)}) %collective-permute-start.6) | collective-permute-done | bytes 262176 | tf_op jit(solution)/shard_map/ppermute | solution.py:471
  32.4 0.0 collective-permute-done.3.refs_1_
  32.4 0.0 collective-permute-done.4.refs_2_
  32.4 0.8 collective-permute-done.5.refs_3_
  33.3 1.2 %collective-permute-start.7 = (bf16[4,16,1024]{2,1,0:T(8,128)(2,1)S(1)}, bf16[4,16,1024]{2,1,0:T(8,128)(2,1)S(1)}, u32[]{:S(2)}, u32[]{:S(2)}) collective-permute-start(bf16[4,16,1024]{2,1,0:T(8,128)(2,1)S(1)} %get-tuple-element.57.refs_0_), channel_id=1, source_target_pairs={{0,8},{4,12},{8,0},{12,4},{16,24},{20,28},{24,16},{28,20},{1,9},{5... | collective-permute-start | bytes 393224 | tf_op jit(solution)/shard_map/ppermute | solution.py:475
  34.5 1.5 %collective-permute-start.8 = (bf16[4,16,1024]{2,1,0:T(8,128)(2,1)S(1)}, bf16[4,16,1024]{2,1,0:T(8,128)(2,1)S(1)}, u32[]{:S(2)}, u32[]{:S(2)}) collective-permute-start(bf16[4,16,1024]{2,1,0:T(8,128)(2,1)S(1)} %get-tuple-element.58), channel_id=1, source_target_pairs={{0,16},{4,20},{8,24},{12,28},{16,0},{20,4},{24,8},{28,12},{1,17},{... | collective-permute-start | bytes 393224 | tf_op jit(solution)/shard_map/ppermute | solution.py:475
  35.9 1.8 %collective-permute-start.9 = (bf16[4,16,1024]{2,1,0:T(8,128)(2,1)S(1)}, bf16[4,16,1024]{2,1,0:T(8,128)(2,1)S(1)}, u32[]{:S(2)}, u32[]{:S(2)}) collective-permute-start(bf16[4,16,1024]{2,1,0:T(8,128)(2,1)S(1)} %get-tuple-element.59), channel_id=1, source_target_pairs={{0,24},{4,28},{8,16},{12,20},{16,8},{20,12},{24,0},{28,4},{1,25},{... | collective-permute-start | bytes 393224 | tf_op jit(solution)/shard_map/ppermute | solution.py:475
  37.8 0.0 collective-permute-done.13.refs_0_
  37.8 2.1 %turn.3.refs_4_.refs_3_.refs_7_ = bf16[512,32,128]{2,1,0:T(8,128)(2,1)S(1)} custom-call(bf16[16,64,1024]{2,1,0:T(8,128)(2,1)S(1)} %collective-permute-done.13.refs_0_), custom_call_target="tpu_custom_call" | custom-call | bytes 16 | tf_op jit(solution)/shard_map/turn/pallas_call | solution.py:47
  39.9 0.0 collective-permute-done.7.refs_0_.refs_1_
  39.9 6.3 %collective-permute-done.8.refs_1_.refs_2_ = bf16[4,16,1024]{2,1,0:T(8,128)(2,1)S(1)} collective-permute-done((bf16[4,16,1024]{2,1,0:T(8,128)(2,1)S(1)}, bf16[4,16,1024]{2,1,0:T(8,128)(2,1)S(1)}, u32[]{:S(2)}, u32[]{:S(2)}) %collective-permute-start.8) | collective-permute-done | bytes 131104 | tf_op jit(solution)/shard_map/ppermute | solution.py:475
  46.2 0.0 collective-permute-done.9.refs_2_.refs_3_
  46.2 0.1 collective-permute-start.14
  46.3 0.8 collective-permute-start.15
  47.1 0.0 copy-start.2
  47.1 0.0 copy-start.3
  47.1 2.8 %collective-permute-start.10 = (bf16[2,16,1024]{2,1,0:T(8,128)(2,1)S(1)}, bf16[2,16,1024]{2,1,0:T(8,128)(2,1)S(1)}, u32[]{:S(2)}, u32[]{:S(2)}) collective-permute-start(bf16[2,16,1024]{2,1,0:T(8,128)(2,1)S(1)} %part.1.refs_0_.refs_7_), channel_id=1, source_target_pairs={{0,8},{4,12},{8,0},{12,4},{16,24},{20,28},{24,16},{28,20},{1,9},{5... | collective-permute-start | bytes 196616 | tf_op jit(solution)/shard_map/ppermute | solution.py:475
  50.0 2.4 %collective-permute-start.12 = (bf16[2,16,1024]{2,1,0:T(8,128)(2,1)S(1)}, bf16[2,16,1024]{2,1,0:T(8,128)(2,1)S(1)}, u32[]{:S(2)}, u32[]{:S(2)}) collective-permute-start(bf16[2,16,1024]{2,1,0:T(8,128)(2,1)S(1)} %part.1.refs_0_.refs_7_), channel_id=1, source_target_pairs={{0,24},{4,28},{8,16},{12,20},{16,8},{20,12},{24,0},{28,4},{1,25},{... | collective-permute-start | bytes 196616 | tf_op jit(solution)/shard_map/ppermute | solution.py:475
  52.4 3.0 %bins.4.refs_0_.refs_6_ = f32[4096,128]{1,0:T(8,128)S(1)} custom-call(bf16[8,16,1024]{2,1,0:T(8,128)(2,1)S(1)} %gather.2.refs_0_.refs_3_, bf16[8,16,1024]{2,1,0:T(8,128)(2,1)S(1)} %collective-permute-done.14.refs_1_.refs_5_, bf16[512,32,128]{2,1,0:T(8,128)(2,1)S(1)} %turn.2.refs_7_.refs_2_, bf16[512,32,128]{2,1,0:T(8,128)(2,1)S(1)} %turn.3.refs_4_.refs_3_.refs_7_), custom_call_target="tpu_custom_call" | custom-call | bytes 16 | tf_op jit(solution)/shard_map/bins/pallas_call | solution.py:47
  55.4 2.3 %collective-permute-done.11.refs_5_.refs_2_ = bf16[2,16,1024]{2,1,0:T(8,128)(2,1)S(1)} collective-permute-done((bf16[2,16,1024]{2,1,0:T(8,128)(2,1)S(1)}, bf16[2,16,1024]{2,1,0:T(8,128)(2,1)S(1)}, u32[]{:S(2)}, u32[]{:S(2)}) %collective-permute-start.11) | collective-permute-done | bytes 65568 | tf_op jit(solution)/shard_map/ppermute | solution.py:475
  57.7 0.6 lags.4
  58.4 0.0 collective-permute-done.12.refs_3_.refs_4_
  58.4 0.1 collective-permute-start.20
  58.5 1.1 %collective-permute-start.16 = (bf16[8,16,1024]{2,1,0:T(8,128)(2,1)S(1)}, bf16[8,16,1024]{2,1,0:T(8,128)(2,1)S(1)}, u32[]{:S(2)}, u32[]{:S(2)}) collective-permute-start(bf16[8,16,1024]{2,1,0:T(8,128)(2,1)S(1)} %gather.3.refs_4_.refs_0_), channel_id=1, source_target_pairs={{0,4},{4,0},{8,12},{12,8},{16,20},{20,16},{24,28},{28,24},{1,5},{5... | collective-permute-start | bytes 786440 | tf_op jit(solution)/shard_map/ppermute | solution.py:479
  59.6 0.2 collective-permute-start.18
  59.8 1.5 %collective-permute-start.19 = (bf16[8,32,512]{2,1,0:T(8,128)(2,1)S(1)}, bf16[8,32,512]{2,1,0:T(8,128)(2,1)S(1)}, u32[]{:S(2)}, u32[]{:S(2)}) collective-permute-start(bf16[8,32,512]{2,1,0:T(8,128)(2,1)S(1)} %get-tuple-element.62.refs_4_.refs_3_), channel_id=1, source_target_pairs={{0,2},{1,3},{2,0},{3,1},{4,6},{5,7},{6,4},{7,5},{8,10},{9,11},{10,... | collective-permute-start | bytes 786440 | tf_op jit(solution)/shard_map/ppermute | solution.py:523
  61.3 0.0 collective-permute-done.20.refs_1_
  61.3 3.0 %bins.6.refs_6_.refs_0_ = f32[4096,128]{1,0:T(8,128)S(1)} custom-call(bf16[8,16,1024]{2,1,0:T(8,128)(2,1)S(1)} %gather.3.refs_4_.refs_0_, bf16[8,16,1024]{2,1,0:T(8,128)(2,1)S(1)} %collective-permute-done.20.refs_1_, bf16[512,32,128]{2,1,0:T(8,128)(2,1)S(1)} %turn.2.refs_7_.refs_2_, bf16[512,32,128]{2,1,0:T(8,128)(2,1)S(1)} %turn.3.refs_4_.refs_3_.refs_7_), custom_call_target="tpu_custom_call" | custom-call | bytes 16 | tf_op jit(solution)/shard_map/bins/pallas_call | solution.py:47
  64.4 0.6 lags.6
  65.0 2.2 %collective-permute-done.16.refs_6_.refs_0_.refs_7_.refs_10_ = bf16[8,16,1024]{2,1,0:T(8,128)(2,1)S(1)} collective-permute-done((bf16[8,16,1024]{2,1,0:T(8,128)(2,1)S(1)}, bf16[8,16,1024]{2,1,0:T(8,128)(2,1)S(1)}, u32[]{:S(2)}, u32[]{:S(2)}) %collective-permute-start.16) | collective-permute-done | bytes 262176 | tf_op jit(solution)/shard_map/ppermute | solution.py:479
  67.2 0.0 collective-permute-start.17
  67.2 1.5 %collective-permute-start.21 = (bf16[8,32,512]{2,1,0:T(8,128)(2,1)S(1)}, bf16[8,32,512]{2,1,0:T(8,128)(2,1)S(1)}, u32[]{:S(2)}, u32[]{:S(2)}) collective-permute-start(bf16[8,32,512]{2,1,0:T(8,128)(2,1)S(1)} %get-tuple-element.64.refs_8_), channel_id=1, source_target_pairs={{0,2},{1,3},{2,0},{3,1},{4,6},{5,7},{6,4},{7,5},{8,10},{9,11},{10,... | collective-permute-start | bytes 786440 | tf_op jit(solution)/shard_map/ppermute | solution.py:523
  68.8 0.0 collective-permute-done.18.refs_1_
  68.8 3.2 %bins.5.refs_0_.refs_5_.refs_4_.refs_9_ = f32[4096,128]{1,0:T(8,128)S(1)} custom-call(bf16[8,16,1024]{2,1,0:T(8,128)(2,1)S(1)} %collective-permute-done.15.refs_8_.refs_0_, bf16[8,16,1024]{2,1,0:T(8,128)(2,1)S(1)} %collective-permute-done.18.refs_1_, bf16[512,32,128]{2,1,0:T(8,128)(2,1)S(1)} %turn.2.refs_7_.refs_2_, ...), custom_call_target="tpu_custom_call" | custom-call | bytes 16 | tf_op jit(solution)/shard_map/bins/pallas_call | solution.py:47
  72.0 0.0 collective-permute-done.19.refs_3_.refs_1_
  72.0 0.6 lags.5
  72.6 0.6 collective-permute-start.23
  73.2 0.0 collective-permute-done.17.refs_1_.refs_8_
  73.2 3.0 %bins.7.refs_0_ = f32[4096,128]{1,0:T(8,128)S(1)} custom-call(bf16[8,16,1024]{2,1,0:T(8,128)(2,1)S(1)} %collective-permute-done.16.refs_6_.refs_0_.refs_7_.refs_10_, bf16[8,16,1024]{2,1,0:T(8,128)(2,1)S(1)} %collective-permute-done.17.refs_1_.refs_8_, bf16[512,32,128]{2,1,0:T(8,128)(2,1)S(1)} %turn.2.refs_7_.refs_2_, ...), custom_call_target="tpu_custom_call" | custom-call | bytes 16 | tf_op jit(solution)/shard_map/bins/pallas_call | solution.py:47
  76.2 0.0 copy-start.4
  76.2 0.1 collective-permute-done.21.refs_3_.refs_5_
  76.3 0.6 lags.7
  77.0 1.6 %collective-permute-start.22 = (bf16[8,32,512]{2,1,0:T(8,128)(2,1)S(1)}, bf16[8,32,512]{2,1,0:T(8,128)(2,1)S(1)}, u32[]{:S(2)}, u32[]{:S(2)}) collective-permute-start(bf16[8,32,512]{2,1,0:T(8,128)(2,1)S(1)} %get-tuple-element.66), channel_id=1, source_target_pairs={{0,2},{1,3},{2,0},{3,1},{4,6},{5,7},{6,4},{7,5},{8,10},{9,11},{10,... | collective-permute-start | bytes 786440 | tf_op jit(solution)/shard_map/ppermute | solution.py:523
  78.6 3.4 %collective-permute-done.23.refs_3_ = bf16[8,32,512]{2,1,0:T(8,128)(2,1)S(1)} collective-permute-done((bf16[8,32,512]{2,1,0:T(8,128)(2,1)S(1)}, bf16[8,32,512]{2,1,0:T(8,128)(2,1)S(1)}, u32[]{:S(2)}, u32[]{:S(2)}) %collective-permute-start.23) | collective-permute-done | bytes 262176 | tf_op jit(solution)/shard_map/ppermute | solution.py:523
  82.0 1.2 %unfold.2.refs_3_ = f32[4,1280,128]{2,1,0:T(8,128)S(1)} custom-call(bf16[8,32,512]{2,1,0:T(8,128)(2,1)S(1)} %get-tuple-element.67.refs_0_, bf16[8,32,512]{2,1,0:T(8,128)(2,1)S(1)} %collective-permute-done.19.refs_3_.refs_1_, bf16[8,32,512]{2,1,0:T(8,128)(2,1)S(1)} %get-tuple-element.68.refs_2_, bf16[8,32,512]{2,1,0:T(8,128)(2,1)S(1)} %collective-permute-done.23.refs_3_, ...), custom_call_target="tpu_custom_call" | custom-call | bytes 16 | tf_op jit(solution)/shard_map/unfold/pallas_call | solution.py:47
  83.1 4.1 %collective-permute-done.22.refs_1_ = bf16[8,32,512]{2,1,0:T(8,128)(2,1)S(1)} collective-permute-done((bf16[8,32,512]{2,1,0:T(8,128)(2,1)S(1)}, bf16[8,32,512]{2,1,0:T(8,128)(2,1)S(1)}, u32[]{:S(2)}, u32[]{:S(2)}) %collective-permute-start.22) | collective-permute-done | bytes 262176 | tf_op jit(solution)/shard_map/ppermute | solution.py:523
  87.2 1.6 %unfold.3 = (bf16[32,32,512]{2,1,0:T(8,128)(2,1)}, f32[4,1280,128]{2,1,0:T(8,128)S(1)}) custom-call(bf16[8,32,512]{2,1,0:T(8,128)(2,1)S(1)} %get-tuple-element.65.refs_0_, bf16[8,32,512]{2,1,0:T(8,128)(2,1)S(1)} %collective-permute-done.22.refs_1_, bf16[512,512]{1,0:T(8,128)(2,1)S(1)} %copy-done.4, ...), custom_call_target="tpu_custom_call", output_to_operand_aliasing={{1}: (3, {})} | custom-call | bytes 16 | tf_op jit(solution)/shard_map/unfold/pallas_call | solution.py:47
  (20 shorter events, 0.2 us)
Async XLA Ops:
  0.0 2.2 %copy-start = (bf16[16,128,1024]{2,1,0:T(8,128)(2,1)S(1)}, bf16[16,128,1024]{2,1,0:T(8,128)(2,1)}, u32[]{:S(2)}) copy-start(bf16[16,128,1024]{2,1,0:T(8,128)(2,1)} %refs_0_.4) | copy-start | bytes 12582916
  2.2 6.2 %copy-start.1 = (bf16[16,128,1024]{2,1,0:T(8,128)(2,1)S(1)}, bf16[16,128,1024]{2,1,0:T(8,128)(2,1)}, u32[]{:S(2)}) copy-start(bf16[16,128,1024]{2,1,0:T(8,128)(2,1)} %refs_0_.4) | copy-start | bytes 12582916
  2.2 11.1 %collective-permute-start = (bf16[16,1,1024]{2,1,0:T(2,128)(2,1)S(1)}, bf16[16,1,1024]{2,1,0:T(2,128)(2,1)S(1)}, u32[]{:S(2)}, u32[]{:S(2)}) collective-permute-start(bf16[16,1,1024]{2,1,0:T(2,128)(2,1)S(1)} %get-tuple-element.38), channel_id=1, source_target_pairs={{0,4},{4,8},{8,12},{12,16},{16,20},{20,24},{24,28},{28,0},{1,5},{5... | collective-permute-start | bytes 98312 | tf_op jit(solution)/shard_map/ppermute | solution.py:512
  5.2 8.1 %copy-start.5 = (s32[32]{0:T(128)S(1)}, s32[32]{0:T(128)}, u32[]{:S(2)}) copy-start(s32[32]{0:T(128)} %refs_0_.5) | copy-start | bytes 388
  5.2 8.1 %copy-start.6 = (s32[16]{0:T(128)S(1)}, s32[16]{0:T(128)}, u32[]{:S(2)}) copy-start(s32[16]{0:T(128)} %refs_1_.5) | copy-start | bytes 196
  5.2 8.1 %collective-permute-start.1 = (bf16[16,1,1024]{2,1,0:T(2,128)(2,1)S(1)}, bf16[16,1,1024]{2,1,0:T(2,128)(2,1)S(1)}, u32[]{:S(2)}, u32[]{:S(2)}) collective-permute-start(bf16[16,1,1024]{2,1,0:T(2,128)(2,1)S(1)} %get-tuple-element.39), channel_id=1, source_target_pairs={{4,0},{8,4},{12,8},{16,12},{20,16},{24,20},{28,24},{0,28},{5,1},{9... | collective-permute-start | bytes 98312 | tf_op jit(solution)/shard_map/ppermute | solution.py:513
  15.1 7.8 %collective-permute-start.2 = (bf16[8,16,1024]{2,1,0:T(8,128)(2,1)S(1)}, bf16[8,16,1024]{2,1,0:T(8,128)(2,1)S(1)}, u32[]{:S(2)}, u32[]{:S(2)}) collective-permute-start(bf16[8,16,1024]{2,1,0:T(8,128)(2,1)S(1)} %get-tuple-element.45), channel_id=1, source_target_pairs={{0,4},{4,0},{8,12},{12,8},{16,20},{20,16},{24,28},{28,24},{1,5},{5... | collective-permute-start | bytes 786440 | tf_op jit(solution)/shard_map/ppermute | solution.py:471
  23.6 14.2 %collective-permute-start.13 = (bf16[16,64,1024]{2,1,0:T(8,128)(2,1)S(1)}, bf16[16,64,1024]{2,1,0:T(8,128)(2,1)S(1)}, u32[]{:S(2)}, u32[]{:S(2)}) collective-permute-start(bf16[16,64,1024]{2,1,0:T(8,128)(2,1)S(1)} %get-tuple-element.61), channel_id=1, source_target_pairs={{0,1},{1,0},{2,3},{3,2},{4,5},{5,4},{6,7},{7,6},{8,9},{9,8},{10,11... | collective-permute-start | bytes 6291464 | tf_op jit(solution)/shard_map/ppermute | solution.py:520
  23.6 8.7 %collective-permute-start.6 = (bf16[8,16,1024]{2,1,0:T(8,128)(2,1)S(1)}, bf16[8,16,1024]{2,1,0:T(8,128)(2,1)S(1)}, u32[]{:S(2)}, u32[]{:S(2)}) collective-permute-start(bf16[8,16,1024]{2,1,0:T(8,128)(2,1)S(1)} %get-tuple-element.51), channel_id=1, source_target_pairs={{0,4},{4,0},{8,12},{12,8},{16,20},{20,16},{24,28},{28,24},{1,5},{5... | collective-permute-start | bytes 786440 | tf_op jit(solution)/shard_map/ppermute | solution.py:471
  24.0 8.4 %collective-permute-start.3 = (bf16[2,16,1024]{2,1,0:T(8,128)(2,1)S(1)}, bf16[2,16,1024]{2,1,0:T(8,128)(2,1)S(1)}, u32[]{:S(2)}, u32[]{:S(2)}) collective-permute-start(bf16[2,16,1024]{2,1,0:T(8,128)(2,1)S(1)} %get-tuple-element.47), channel_id=1, source_target_pairs={{0,8},{4,12},{8,0},{12,4},{16,24},{20,28},{24,16},{28,20},{1,9},{5... | collective-permute-start | bytes 196616 | tf_op jit(solution)/shard_map/ppermute | solution.py:475
  24.5 7.9 %collective-permute-start.4 = (bf16[2,16,1024]{2,1,0:T(8,128)(2,1)S(1)}, bf16[2,16,1024]{2,1,0:T(8,128)(2,1)S(1)}, u32[]{:S(2)}, u32[]{:S(2)}) collective-permute-start(bf16[2,16,1024]{2,1,0:T(8,128)(2,1)S(1)} %get-tuple-element.48), channel_id=1, source_target_pairs={{0,16},{4,20},{8,24},{12,28},{16,0},{20,4},{24,8},{28,12},{1,17},{... | collective-permute-start | bytes 196616 | tf_op jit(solution)/shard_map/ppermute | solution.py:475
  27.1 6.2 %collective-permute-start.5 = (bf16[2,16,1024]{2,1,0:T(8,128)(2,1)S(1)}, bf16[2,16,1024]{2,1,0:T(8,128)(2,1)S(1)}, u32[]{:S(2)}, u32[]{:S(2)}) collective-permute-start(bf16[2,16,1024]{2,1,0:T(8,128)(2,1)S(1)} %get-tuple-element.49), channel_id=1, source_target_pairs={{0,24},{4,28},{8,16},{12,20},{16,8},{20,12},{24,0},{28,4},{1,25},{... | collective-permute-start | bytes 196616 | tf_op jit(solution)/shard_map/ppermute | solution.py:475
  33.3 6.6 %collective-permute-start.7 = (bf16[4,16,1024]{2,1,0:T(8,128)(2,1)S(1)}, bf16[4,16,1024]{2,1,0:T(8,128)(2,1)S(1)}, u32[]{:S(2)}, u32[]{:S(2)}) collective-permute-start(bf16[4,16,1024]{2,1,0:T(8,128)(2,1)S(1)} %get-tuple-element.57.refs_0_), channel_id=1, source_target_pairs={{0,8},{4,12},{8,0},{12,4},{16,24},{20,28},{24,16},{28,20},{1,9},{5... | collective-permute-start | bytes 393224 | tf_op jit(solution)/shard_map/ppermute | solution.py:475
  34.5 11.7 %collective-permute-start.8 = (bf16[4,16,1024]{2,1,0:T(8,128)(2,1)S(1)}, bf16[4,16,1024]{2,1,0:T(8,128)(2,1)S(1)}, u32[]{:S(2)}, u32[]{:S(2)}) collective-permute-start(bf16[4,16,1024]{2,1,0:T(8,128)(2,1)S(1)} %get-tuple-element.58), channel_id=1, source_target_pairs={{0,16},{4,20},{8,24},{12,28},{16,0},{20,4},{24,8},{28,12},{1,17},{... | collective-permute-start | bytes 393224 | tf_op jit(solution)/shard_map/ppermute | solution.py:475
  35.9 10.2 %collective-permute-start.9 = (bf16[4,16,1024]{2,1,0:T(8,128)(2,1)S(1)}, bf16[4,16,1024]{2,1,0:T(8,128)(2,1)S(1)}, u32[]{:S(2)}, u32[]{:S(2)}) collective-permute-start(bf16[4,16,1024]{2,1,0:T(8,128)(2,1)S(1)} %get-tuple-element.59), channel_id=1, source_target_pairs={{0,24},{4,28},{8,16},{12,20},{16,8},{20,12},{24,0},{28,4},{1,25},{... | collective-permute-start | bytes 393224 | tf_op jit(solution)/shard_map/ppermute | solution.py:475
  46.2 6.2 %collective-permute-start.14 = (bf16[8,16,1024]{2,1,0:T(8,128)(2,1)S(1)}, bf16[8,16,1024]{2,1,0:T(8,128)(2,1)S(1)}, u32[]{:S(2)}, u32[]{:S(2)}) collective-permute-start(bf16[8,16,1024]{2,1,0:T(8,128)(2,1)S(1)} %gather.2.refs_0_.refs_3_), channel_id=1, source_target_pairs={{0,1},{1,0},{2,3},{3,2},{4,5},{5,4},{6,7},{7,6},{8,9},{9,8},{10,11... | collective-permute-start | bytes 786440 | tf_op jit(solution)/shard_map/ppermute | solution.py:520
  46.3 12.1 %collective-permute-start.15 = (bf16[8,16,1024]{2,1,0:T(8,128)(2,1)S(1)}, bf16[8,16,1024]{2,1,0:T(8,128)(2,1)S(1)}, u32[]{:S(2)}, u32[]{:S(2)}) collective-permute-start(bf16[8,16,1024]{2,1,0:T(8,128)(2,1)S(1)} %gather.2.refs_0_.refs_3_), channel_id=1, source_target_pairs={{0,4},{4,0},{8,12},{12,8},{16,20},{20,16},{24,28},{28,24},{1,5},{5... | collective-permute-start | bytes 786440 | tf_op jit(solution)/shard_map/ppermute | solution.py:479
  47.1 10.6 %copy-start.2 = (bf16[272,512]{1,0:T(8,128)(2,1)S(1)}, bf16[272,512]{1,0:T(8,128)(2,1)}, u32[]{:S(2)}) copy-start(bf16[272,512]{1,0:T(8,128)(2,1)} %constant.6.clone.refs_1_) | copy-start | bytes 835588
  47.1 10.6 %copy-start.3 = (bf16[256,512]{1,0:T(8,128)(2,1)S(1)}, bf16[256,512]{1,0:T(8,128)(2,1)}, u32[]{:S(2)}) copy-start(bf16[256,512]{1,0:T(8,128)(2,1)} %constant.7.clone.refs_2_) | copy-start | bytes 786436
  47.1 8.3 %collective-permute-start.10 = (bf16[2,16,1024]{2,1,0:T(8,128)(2,1)S(1)}, bf16[2,16,1024]{2,1,0:T(8,128)(2,1)S(1)}, u32[]{:S(2)}, u32[]{:S(2)}) collective-permute-start(bf16[2,16,1024]{2,1,0:T(8,128)(2,1)S(1)} %part.1.refs_0_.refs_7_), channel_id=1, source_target_pairs={{0,8},{4,12},{8,0},{12,4},{16,24},{20,28},{24,16},{28,20},{1,9},{5... | collective-permute-start | bytes 196616 | tf_op jit(solution)/shard_map/ppermute | solution.py:475
  49.9 7.8 %collective-permute-start.11 = (bf16[2,16,1024]{2,1,0:T(8,128)(2,1)S(1)}, bf16[2,16,1024]{2,1,0:T(8,128)(2,1)S(1)}, u32[]{:S(2)}, u32[]{:S(2)}) collective-permute-start(bf16[2,16,1024]{2,1,0:T(8,128)(2,1)S(1)} %part.1.refs_0_.refs_7_), channel_id=1, source_target_pairs={{0,16},{4,20},{8,24},{12,28},{16,0},{20,4},{24,8},{28,12},{1,17},{... | collective-permute-start | bytes 196616 | tf_op jit(solution)/shard_map/ppermute | solution.py:475
  50.0 8.4 %collective-permute-start.12 = (bf16[2,16,1024]{2,1,0:T(8,128)(2,1)S(1)}, bf16[2,16,1024]{2,1,0:T(8,128)(2,1)S(1)}, u32[]{:S(2)}, u32[]{:S(2)}) collective-permute-start(bf16[2,16,1024]{2,1,0:T(8,128)(2,1)S(1)} %part.1.refs_0_.refs_7_), channel_id=1, source_target_pairs={{0,24},{4,28},{8,16},{12,20},{16,8},{20,12},{24,0},{28,4},{1,25},{... | collective-permute-start | bytes 196616 | tf_op jit(solution)/shard_map/ppermute | solution.py:475
  58.4 2.9 %collective-permute-start.20 = (bf16[8,16,1024]{2,1,0:T(8,128)(2,1)S(1)}, bf16[8,16,1024]{2,1,0:T(8,128)(2,1)S(1)}, u32[]{:S(2)}, u32[]{:S(2)}) collective-permute-start(bf16[8,16,1024]{2,1,0:T(8,128)(2,1)S(1)} %gather.3.refs_4_.refs_0_), channel_id=1, source_target_pairs={{0,1},{1,0},{2,3},{3,2},{4,5},{5,4},{6,7},{7,6},{8,9},{9,8},{10,11... | collective-permute-start | bytes 786440 | tf_op jit(solution)/shard_map/ppermute | solution.py:520
  58.5 8.7 %collective-permute-start.16 = (bf16[8,16,1024]{2,1,0:T(8,128)(2,1)S(1)}, bf16[8,16,1024]{2,1,0:T(8,128)(2,1)S(1)}, u32[]{:S(2)}, u32[]{:S(2)}) collective-permute-start(bf16[8,16,1024]{2,1,0:T(8,128)(2,1)S(1)} %gather.3.refs_4_.refs_0_), channel_id=1, source_target_pairs={{0,4},{4,0},{8,12},{12,8},{16,20},{20,16},{24,28},{28,24},{1,5},{5... | collective-permute-start | bytes 786440 | tf_op jit(solution)/shard_map/ppermute | solution.py:479
  59.6 9.1 %collective-permute-start.18 = (bf16[8,16,1024]{2,1,0:T(8,128)(2,1)S(1)}, bf16[8,16,1024]{2,1,0:T(8,128)(2,1)S(1)}, u32[]{:S(2)}, u32[]{:S(2)}) collective-permute-start(bf16[8,16,1024]{2,1,0:T(8,128)(2,1)S(1)} %collective-permute-done.15.refs_8_.refs_0_), channel_id=1, source_target_pairs={{0,1},{1,0},{2,3},{3,2},{4,5},{5,4},{6,7},{7,6},{8,9},{9,8},{10,11... | collective-permute-start | bytes 786440 | tf_op jit(solution)/shard_map/ppermute | solution.py:520
  59.8 12.2 %collective-permute-start.19 = (bf16[8,32,512]{2,1,0:T(8,128)(2,1)S(1)}, bf16[8,32,512]{2,1,0:T(8,128)(2,1)S(1)}, u32[]{:S(2)}, u32[]{:S(2)}) collective-permute-start(bf16[8,32,512]{2,1,0:T(8,128)(2,1)S(1)} %get-tuple-element.62.refs_4_.refs_3_), channel_id=1, source_target_pairs={{0,2},{1,3},{2,0},{3,1},{4,6},{5,7},{6,4},{7,5},{8,10},{9,11},{10,... | collective-permute-start | bytes 786440 | tf_op jit(solution)/shard_map/ppermute | solution.py:523
  67.2 6.0 %collective-permute-start.17 = (bf16[8,16,1024]{2,1,0:T(8,128)(2,1)S(1)}, bf16[8,16,1024]{2,1,0:T(8,128)(2,1)S(1)}, u32[]{:S(2)}, u32[]{:S(2)}) collective-permute-start(bf16[8,16,1024]{2,1,0:T(8,128)(2,1)S(1)} %collective-permute-done.16.refs_6_.refs_0_.refs_7_.refs_10_), channel_id=1, source_target_pairs={{0,1},{1,0},{2,3},{3,2},{4,5},{5,4},{6,7},{7,6},{8,9},{9,8},{10,11... | collective-permute-start | bytes 786440 | tf_op jit(solution)/shard_map/ppermute | solution.py:520
  67.2 9.1 %collective-permute-start.21 = (bf16[8,32,512]{2,1,0:T(8,128)(2,1)S(1)}, bf16[8,32,512]{2,1,0:T(8,128)(2,1)S(1)}, u32[]{:S(2)}, u32[]{:S(2)}) collective-permute-start(bf16[8,32,512]{2,1,0:T(8,128)(2,1)S(1)} %get-tuple-element.64.refs_8_), channel_id=1, source_target_pairs={{0,2},{1,3},{2,0},{3,1},{4,6},{5,7},{6,4},{7,5},{8,10},{9,11},{10,... | collective-permute-start | bytes 786440 | tf_op jit(solution)/shard_map/ppermute | solution.py:523
  72.6 9.3 %collective-permute-start.23 = (bf16[8,32,512]{2,1,0:T(8,128)(2,1)S(1)}, bf16[8,32,512]{2,1,0:T(8,128)(2,1)S(1)}, u32[]{:S(2)}, u32[]{:S(2)}) collective-permute-start(bf16[8,32,512]{2,1,0:T(8,128)(2,1)S(1)} %get-tuple-element.63.refs_4_.refs_7_), channel_id=1, source_target_pairs={{0,2},{1,3},{2,0},{3,1},{4,6},{5,7},{6,4},{7,5},{8,10},{9,11},{10,... | collective-permute-start | bytes 786440 | tf_op jit(solution)/shard_map/ppermute | solution.py:523
  76.2 5.7 %copy-start.4 = (bf16[512,512]{1,0:T(8,128)(2,1)S(1)}, bf16[512,512]{1,0:T(8,128)(2,1)}, u32[]{:S(2)}) copy-start(bf16[512,512]{1,0:T(8,128)(2,1)} %constant.8.clone.refs_6_.refs_2_) | copy-start | bytes 1572868
  77.0 10.2 %collective-permute-start.22 = (bf16[8,32,512]{2,1,0:T(8,128)(2,1)S(1)}, bf16[8,32,512]{2,1,0:T(8,128)(2,1)S(1)}, u32[]{:S(2)}, u32[]{:S(2)}) collective-permute-start(bf16[8,32,512]{2,1,0:T(8,128)(2,1)S(1)} %get-tuple-element.66), channel_id=1, source_target_pairs={{0,2},{1,3},{2,0},{3,1},{4,6},{5,7},{6,4},{7,5},{8,10},{9,11},{10,... | collective-permute-start | bytes 786440 | tf_op jit(solution)/shard_map/ppermute | solution.py:523

commit v6 on v5

--- a/solution.py
+++ b/solution.py
@@ -164,7 +164,7 @@
         (spectra,),
         [HBM],
         [
-            ((width // LANES, windows * (chans + 8), LANES), F32),
+            ((width // LANES, (windows + 1) * (chans + 8), LANES), F32),
             ((freqs, freqs), BF16),
             ((2, windows, freqs), F32),
             ((2, windows, width), F32),
@@ -228,8 +228,8 @@
 def halve_kernel(white_ref, edge_ref, keep_ref, send_ref):
     windows, chans, width = keep_ref.shape
     share = chans // 2
-    blocks = white_ref.shape[1] // windows // share
-    pitch = white_ref.shape[1] // windows
+    pitch = white_ref.shape[1] // (windows + 1)
+    blocks = pitch // share
     me = lax.axis_index("win")
     row = lax.broadcasted_iota(jnp.int32, (8, LANES), 0)
 
@@ -451,7 +451,7 @@
 
 def unfold(blocks, starts, sources, ins, mix, earlier, after):
     chans, lags = ins[0].shape[1:]
-    held = ((lags // LANES, chans * (sources + 8), LANES), F32)
+    held = ((lags // LANES, (chans + 1) * (sources + 8), LANES), F32)
     outs = [((chans, sources, lags), BF16), held] if earlier else [held]
     count = len(ins) + 1
     return call(

time: 88.9 us -> 88.9 us (level)
  no operation moved by 1% of the time
where the time goes in v6:
time: 88.9 us; the launch traced here: 88.8 us
  Pallas kernels  29.3 us (33%)
  waiting for transfers between devices  28.8 us (32%)
  starting transfers between devices  28.1 us (32%)
  local copies, waits for them, and re-layouts  2.22 us (2%)
    pallas_call x22, Pallas kernels, call(): pl.pallas_call(body, in_specs=[*in_specs] + [ANY] * len(after), out_specs...  29.3 us
    ppermute x9, starting transfers between devices, over_z(): lax.ppermute(array, 'chan', xor_pairs(8, 2 * p))  14.1 us
    ppermute x2, waiting for transfers between devices, meet_x(): return add_parts(keep, lax.ppermute(send, 'chan', xor_pairs(8, 1)), after)  9.61 us
    ppermute x9, waiting for transfers between devices, over_z(): lax.ppermute(array, 'chan', xor_pairs(8, 2 * p))  9.43 us
    ppermute x4, waiting for transfers between devices, far(): return lax.ppermute(array, 'win', xor_pairs(parts, 2))  7.54 us
    ppermute x4, starting transfers between devices, far(): return lax.ppermute(array, 'win', xor_pairs(parts, 2))  5.19 us
    ppermute x1, starting transfers between devices, on_device(): high = lax.ppermute(first, 'chan', backward)  3.12 us
    ppermute x1, starting transfers between devices, on_device(): low = lax.ppermute(last, 'chan', forward)  2.99 us
  transfers between devices with their start and end apart: 24, of which 9 were waited for; matrix products, arithmetic and copies ran while one was open for 0% of the time, Pallas kernels for 28%

profile of v6, /device:TPU:0, one launch (start us, length us, event | category | flops | bytes accessed | tf_op | source)
XLA Modules:
  0.0 88.8 jit_solution(10522698435646996557)
XLA Ops:
  0.0 2.2 %copy-done = bf16[16,128,1024]{2,1,0:T(8,128)(2,1)S(1)} copy-done((bf16[16,128,1024]{2,1,0:T(8,128)(2,1)S(1)}, bf16[16,128,1024]{2,1,0:T(8,128)(2,1)}, u32[]{:S(2)}) %copy-start) | copy-done | bytes 4194328
  2.2 0.1 rim.1
  2.2 3.0 %collective-permute-start = (bf16[16,1,1024]{2,1,0:T(2,128)(2,1)S(1)}, bf16[16,1,1024]{2,1,0:T(2,128)(2,1)S(1)}, u32[]{:S(2)}, u32[]{:S(2)}) collective-permute-start(bf16[16,1,1024]{2,1,0:T(2,128)(2,1)S(1)} %get-tuple-element.38), channel_id=1, source_target_pairs={{0,4},{4,8},{8,12},{12,16},{16,20},{20,24},{24,28},{28,0},{1,5},{5... | collective-permute-start | bytes 98312 | tf_op jit(solution)/shard_map/ppermute | solution.py:512
  5.2 3.1 %collective-permute-start.1 = (bf16[16,1,1024]{2,1,0:T(2,128)(2,1)S(1)}, bf16[16,1,1024]{2,1,0:T(2,128)(2,1)S(1)}, u32[]{:S(2)}, u32[]{:S(2)}) collective-permute-start(bf16[16,1,1024]{2,1,0:T(2,128)(2,1)S(1)} %get-tuple-element.39), channel_id=1, source_target_pairs={{4,0},{8,4},{12,8},{16,12},{20,16},{24,20},{28,24},{0,28},{5,1},{9... | collective-permute-start | bytes 98312 | tf_op jit(solution)/shard_map/ppermute | solution.py:513
  8.4 4.9 %whiten.1 = (f32[8,2312,128]{2,1,0:T(8,128)S(1)}, bf16[512,512]{1,0:T(8,128)(2,1)S(1)}, f32[2,16,512]{2,1,0:T(8,128)S(1)}, f32[2,16,1024]{2,1,0:T(8,128)S(1)}) custom-call(bf16[16,128,1024]{2,1,0:T(8,128)(2,1)S(1)} %copy-done.1), custom_call_target="tpu_custom_call" | custom-call | bytes 16 | tf_op jit(solution)/shard_map/whiten/pallas_call | solution.py:47
  13.3 0.0 collective-permute-done.refs_2_
  13.3 0.0 collective-permute-done.1.refs_3_
  13.3 1.7 %edges.1 = (bf16[8,16,1024]{2,1,0:T(8,128)(2,1)S(1)}, bf16[8,16,1024]{2,1,0:T(8,128)(2,1)S(1)}, bf16[8,16,1024]{2,1,0:T(8,128)(2,1)S(1)}, bf16[8,16,1024]{2,1,0:T(8,128)(2,1)S(1)}, f32[2,16,1024]{2,1,0:T(8,128)S(1)}) custom-call(s32[32]{0:T(128)S(1)} %copy-done.5, s32[16]{0:T(128)S(1)} %copy-done.6, bf16[16,1,1024]{2,1,0:T(2,128)(2,1)S(1)} %collective-permute-done.refs_2_, ...), custom_call_target="tpu_custom_call" | custom-call | bytes 16 | tf_op jit(solution)/shard_map/edges/pallas_call | solution.py:47
  15.0 0.1 collective-permute-start.2
  15.1 7.8 %collective-permute-done.2.refs_1_ = bf16[8,16,1024]{2,1,0:T(8,128)(2,1)S(1)} collective-permute-done((bf16[8,16,1024]{2,1,0:T(8,128)(2,1)S(1)}, bf16[8,16,1024]{2,1,0:T(8,128)(2,1)S(1)}, u32[]{:S(2)}, u32[]{:S(2)}) %collective-permute-start.2) | collective-permute-done | bytes 262176 | tf_op jit(solution)/shard_map/ppermute | solution.py:471
  22.9 0.6 halve.1
  23.6 0.1 collective-permute-start.13
  23.6 0.4 collective-permute-start.6
  24.0 0.5 collective-permute-start.3
  24.5 2.6 %collective-permute-start.4 = (bf16[2,16,1024]{2,1,0:T(8,128)(2,1)S(1)}, bf16[2,16,1024]{2,1,0:T(8,128)(2,1)S(1)}, u32[]{:S(2)}, u32[]{:S(2)}) collective-permute-start(bf16[2,16,1024]{2,1,0:T(8,128)(2,1)S(1)} %get-tuple-element.48), channel_id=1, source_target_pairs={{0,16},{4,20},{8,24},{12,28},{16,0},{20,4},{24,8},{28,12},{1,17},{... | collective-permute-start | bytes 196616 | tf_op jit(solution)/shard_map/ppermute | solution.py:475
  27.1 1.3 %collective-permute-start.5 = (bf16[2,16,1024]{2,1,0:T(8,128)(2,1)S(1)}, bf16[2,16,1024]{2,1,0:T(8,128)(2,1)S(1)}, u32[]{:S(2)}, u32[]{:S(2)}) collective-permute-start(bf16[2,16,1024]{2,1,0:T(8,128)(2,1)S(1)} %get-tuple-element.49), channel_id=1, source_target_pairs={{0,24},{4,28},{8,16},{12,20},{16,8},{20,12},{24,0},{28,4},{1,25},{... | collective-permute-start | bytes 196616 | tf_op jit(solution)/shard_map/ppermute | solution.py:475
  28.4 2.1 %turn.2.refs_7_.refs_2_ = bf16[512,32,128]{2,1,0:T(8,128)(2,1)S(1)} custom-call(bf16[16,64,1024]{2,1,0:T(8,128)(2,1)S(1)} %get-tuple-element.56.refs_0_), custom_call_target="tpu_custom_call" | custom-call | bytes 16 | tf_op jit(solution)/shard_map/turn/pallas_call | solution.py:47
  30.5 1.8 %collective-permute-done.6.refs_1_ = bf16[8,16,1024]{2,1,0:T(8,128)(2,1)S(1)} collective-permute-done((bf16[8,16,1024]{2,1,0:T(8,128)(2,1)S(1)}, bf16[8,16,1024]{2,1,0:T(8,128)(2,1)S(1)}, u32[]{:S(2)}, u32[]{:S(2)}) %collective-permute-start.6) | collective-permute-done | bytes 262176 | tf_op jit(solution)/shard_map/ppermute | solution.py:471
  32.4 0.0 collective-permute-done.3.refs_1_
  32.4 0.0 collective-permute-done.4.refs_2_
  32.4 0.8 collective-permute-done.5.refs_3_
  33.3 1.2 %collective-permute-start.7 = (bf16[4,16,1024]{2,1,0:T(8,128)(2,1)S(1)}, bf16[4,16,1024]{2,1,0:T(8,128)(2,1)S(1)}, u32[]{:S(2)}, u32[]{:S(2)}) collective-permute-start(bf16[4,16,1024]{2,1,0:T(8,128)(2,1)S(1)} %get-tuple-element.57.refs_0_), channel_id=1, source_target_pairs={{0,8},{4,12},{8,0},{12,4},{16,24},{20,28},{24,16},{28,20},{1,9},{5... | collective-permute-start | bytes 393224 | tf_op jit(solution)/shard_map/ppermute | solution.py:475
  34.5 1.5 %collective-permute-start.8 = (bf16[4,16,1024]{2,1,0:T(8,128)(2,1)S(1)}, bf16[4,16,1024]{2,1,0:T(8,128)(2,1)S(1)}, u32[]{:S(2)}, u32[]{:S(2)}) collective-permute-start(bf16[4,16,1024]{2,1,0:T(8,128)(2,1)S(1)} %get-tuple-element.58), channel_id=1, source_target_pairs={{0,16},{4,20},{8,24},{12,28},{16,0},{20,4},{24,8},{28,12},{1,17},{... | collective-permute-start | bytes 393224 | tf_op jit(solution)/shard_map/ppermute | solution.py:475
  35.9 1.8 %collective-permute-start.9 = (bf16[4,16,1024]{2,1,0:T(8,128)(2,1)S(1)}, bf16[4,16,1024]{2,1,0:T(8,128)(2,1)S(1)}, u32[]{:S(2)}, u32[]{:S(2)}) collective-permute-start(bf16[4,16,1024]{2,1,0:T(8,128)(2,1)S(1)} %get-tuple-element.59), channel_id=1, source_target_pairs={{0,24},{4,28},{8,16},{12,20},{16,8},{20,12},{24,0},{28,4},{1,25},{... | collective-permute-start | bytes 393224 | tf_op jit(solution)/shard_map/ppermute | solution.py:475
  37.8 0.0 collective-permute-done.13.refs_0_
  37.8 2.1 %turn.3.refs_4_.refs_3_.refs_7_ = bf16[512,32,128]{2,1,0:T(8,128)(2,1)S(1)} custom-call(bf16[16,64,1024]{2,1,0:T(8,128)(2,1)S(1)} %collective-permute-done.13.refs_0_), custom_call_target="tpu_custom_call" | custom-call | bytes 16 | tf_op jit(solution)/shard_map/turn/pallas_call | solution.py:47
  39.9 0.0 collective-permute-done.7.refs_0_.refs_1_
  39.9 6.3 %collective-permute-done.8.refs_1_.refs_2_ = bf16[4,16,1024]{2,1,0:T(8,128)(2,1)S(1)} collective-permute-done((bf16[4,16,1024]{2,1,0:T(8,128)(2,1)S(1)}, bf16[4,16,1024]{2,1,0:T(8,128)(2,1)S(1)}, u32[]{:S(2)}, u32[]{:S(2)}) %collective-permute-start.8) | collective-permute-done | bytes 131104 | tf_op jit(solution)/shard_map/ppermute | solution.py:475
  46.2 0.0 collective-permute-done.9.refs_2_.refs_3_
  46.2 0.1 collective-permute-start.14
  46.3 0.8 collective-permute-start.15
  47.1 0.0 copy-start.2
  47.1 0.0 copy-start.3
  47.1 2.8 %collective-permute-start.10 = (bf16[2,16,1024]{2,1,0:T(8,128)(2,1)S(1)}, bf16[2,16,1024]{2,1,0:T(8,128)(2,1)S(1)}, u32[]{:S(2)}, u32[]{:S(2)}) collective-permute-start(bf16[2,16,1024]{2,1,0:T(8,128)(2,1)S(1)} %part.1.refs_0_.refs_7_), channel_id=1, source_target_pairs={{0,8},{4,12},{8,0},{12,4},{16,24},{20,28},{24,16},{28,20},{1,9},{5... | collective-permute-start | bytes 196616 | tf_op jit(solution)/shard_map/ppermute | solution.py:475
  49.9 0.0 collective-permute-start.11
  50.0 2.4 %collective-permute-start.12 = (bf16[2,16,1024]{2,1,0:T(8,128)(2,1)S(1)}, bf16[2,16,1024]{2,1,0:T(8,128)(2,1)S(1)}, u32[]{:S(2)}, u32[]{:S(2)}) collective-permute-start(bf16[2,16,1024]{2,1,0:T(8,128)(2,1)S(1)} %part.1.refs_0_.refs_7_), channel_id=1, source_target_pairs={{0,24},{4,28},{8,16},{12,20},{16,8},{20,12},{24,0},{28,4},{1,25},{... | collective-permute-start | bytes 196616 | tf_op jit(solution)/shard_map/ppermute | solution.py:475
  52.4 0.0 collective-permute-done.14.refs_1_.refs_5_
  52.4 3.0 %bins.4.refs_0_.refs_6_ = f32[4096,128]{1,0:T(8,128)S(1)} custom-call(bf16[8,16,1024]{2,1,0:T(8,128)(2,1)S(1)} %gather.2.refs_0_.refs_3_, bf16[8,16,1024]{2,1,0:T(8,128)(2,1)S(1)} %collective-permute-done.14.refs_1_.refs_5_, bf16[512,32,128]{2,1,0:T(8,128)(2,1)S(1)} %turn.2.refs_7_.refs_2_, bf16[512,32,128]{2,1,0:T(8,128)(2,1)S(1)} %turn.3.refs_4_.refs_3_.refs_7_), custom_call_target="tpu_custom_call" | custom-call | bytes 16 | tf_op jit(solution)/shard_map/bins/pallas_call | solution.py:47
  55.4 0.0 collective-permute-done.10.refs_4_.refs_1_.refs_6_.refs_5_
  55.4 2.3 %collective-permute-done.11.refs_5_.refs_2_ = bf16[2,16,1024]{2,1,0:T(8,128)(2,1)S(1)} collective-permute-done((bf16[2,16,1024]{2,1,0:T(8,128)(2,1)S(1)}, bf16[2,16,1024]{2,1,0:T(8,128)(2,1)S(1)}, u32[]{:S(2)}, u32[]{:S(2)}) %collective-permute-start.11) | collective-permute-done | bytes 65568 | tf_op jit(solution)/shard_map/ppermute | solution.py:475
  57.7 0.6 lags.4
  58.4 0.0 collective-permute-done.12.refs_3_.refs_4_
  58.4 0.1 collective-permute-start.20
  58.5 1.1 %collective-permute-start.16 = (bf16[8,16,1024]{2,1,0:T(8,128)(2,1)S(1)}, bf16[8,16,1024]{2,1,0:T(8,128)(2,1)S(1)}, u32[]{:S(2)}, u32[]{:S(2)}) collective-permute-start(bf16[8,16,1024]{2,1,0:T(8,128)(2,1)S(1)} %gather.3.refs_4_.refs_0_), channel_id=1, source_target_pairs={{0,4},{4,0},{8,12},{12,8},{16,20},{20,16},{24,28},{28,24},{1,5},{5... | collective-permute-start | bytes 786440 | tf_op jit(solution)/shard_map/ppermute | solution.py:479
  59.6 0.2 collective-permute-start.18
  59.8 1.5 %collective-permute-start.19 = (bf16[8,32,512]{2,1,0:T(8,128)(2,1)S(1)}, bf16[8,32,512]{2,1,0:T(8,128)(2,1)S(1)}, u32[]{:S(2)}, u32[]{:S(2)}) collective-permute-start(bf16[8,32,512]{2,1,0:T(8,128)(2,1)S(1)} %get-tuple-element.62.refs_4_.refs_3_), channel_id=1, source_target_pairs={{0,2},{1,3},{2,0},{3,1},{4,6},{5,7},{6,4},{7,5},{8,10},{9,11},{10,... | collective-permute-start | bytes 786440 | tf_op jit(solution)/shard_map/ppermute | solution.py:523
  61.3 3.0 %bins.6.refs_6_.refs_0_ = f32[4096,128]{1,0:T(8,128)S(1)} custom-call(bf16[8,16,1024]{2,1,0:T(8,128)(2,1)S(1)} %gather.3.refs_4_.refs_0_, bf16[8,16,1024]{2,1,0:T(8,128)(2,1)S(1)} %collective-permute-done.20.refs_1_, bf16[512,32,128]{2,1,0:T(8,128)(2,1)S(1)} %turn.2.refs_7_.refs_2_, bf16[512,32,128]{2,1,0:T(8,128)(2,1)S(1)} %turn.3.refs_4_.refs_3_.refs_7_), custom_call_target="tpu_custom_call" | custom-call | bytes 16 | tf_op jit(solution)/shard_map/bins/pallas_call | solution.py:47
  64.4 0.6 lags.6
  65.0 2.2 %collective-permute-done.16.refs_6_.refs_0_.refs_7_.refs_10_ = bf16[8,16,1024]{2,1,0:T(8,128)(2,1)S(1)} collective-permute-done((bf16[8,16,1024]{2,1,0:T(8,128)(2,1)S(1)}, bf16[8,16,1024]{2,1,0:T(8,128)(2,1)S(1)}, u32[]{:S(2)}, u32[]{:S(2)}) %collective-permute-start.16) | collective-permute-done | bytes 262176 | tf_op jit(solution)/shard_map/ppermute | solution.py:479
  67.2 0.0 collective-permute-start.17
  67.2 1.5 %collective-permute-start.21 = (bf16[8,32,512]{2,1,0:T(8,128)(2,1)S(1)}, bf16[8,32,512]{2,1,0:T(8,128)(2,1)S(1)}, u32[]{:S(2)}, u32[]{:S(2)}) collective-permute-start(bf16[8,32,512]{2,1,0:T(8,128)(2,1)S(1)} %get-tuple-element.64.refs_8_), channel_id=1, source_target_pairs={{0,2},{1,3},{2,0},{3,1},{4,6},{5,7},{6,4},{7,5},{8,10},{9,11},{10,... | collective-permute-start | bytes 786440 | tf_op jit(solution)/shard_map/ppermute | solution.py:523
  68.8 0.0 collective-permute-done.18.refs_1_
  68.8 3.2 %bins.5.refs_0_.refs_5_.refs_4_.refs_9_ = f32[4096,128]{1,0:T(8,128)S(1)} custom-call(bf16[8,16,1024]{2,1,0:T(8,128)(2,1)S(1)} %collective-permute-done.15.refs_8_.refs_0_, bf16[8,16,1024]{2,1,0:T(8,128)(2,1)S(1)} %collective-permute-done.18.refs_1_, bf16[512,32,128]{2,1,0:T(8,128)(2,1)S(1)} %turn.2.refs_7_.refs_2_, ...), custom_call_target="tpu_custom_call" | custom-call | bytes 16 | tf_op jit(solution)/shard_map/bins/pallas_call | solution.py:47
  72.0 0.6 lags.5
  72.6 0.6 collective-permute-start.23
  73.2 3.0 %bins.7.refs_0_ = f32[4096,128]{1,0:T(8,128)S(1)} custom-call(bf16[8,16,1024]{2,1,0:T(8,128)(2,1)S(1)} %collective-permute-done.16.refs_6_.refs_0_.refs_7_.refs_10_, bf16[8,16,1024]{2,1,0:T(8,128)(2,1)S(1)} %collective-permute-done.17.refs_1_.refs_8_, bf16[512,32,128]{2,1,0:T(8,128)(2,1)S(1)} %turn.2.refs_7_.refs_2_, ...), custom_call_target="tpu_custom_call" | custom-call | bytes 16 | tf_op jit(solution)/shard_map/bins/pallas_call | solution.py:47
  76.2 0.0 copy-start.4
  76.2 0.1 collective-permute-done.21.refs_3_.refs_5_
  76.3 0.6 lags.7
  77.0 1.6 %collective-permute-start.22 = (bf16[8,32,512]{2,1,0:T(8,128)(2,1)S(1)}, bf16[8,32,512]{2,1,0:T(8,128)(2,1)S(1)}, u32[]{:S(2)}, u32[]{:S(2)}) collective-permute-start(bf16[8,32,512]{2,1,0:T(8,128)(2,1)S(1)} %get-tuple-element.66), channel_id=1, source_target_pairs={{0,2},{1,3},{2,0},{3,1},{4,6},{5,7},{6,4},{7,5},{8,10},{9,11},{10,... | collective-permute-start | bytes 786440 | tf_op jit(solution)/shard_map/ppermute | solution.py:523
  78.6 3.4 %collective-permute-done.23.refs_3_ = bf16[8,32,512]{2,1,0:T(8,128)(2,1)S(1)} collective-permute-done((bf16[8,32,512]{2,1,0:T(8,128)(2,1)S(1)}, bf16[8,32,512]{2,1,0:T(8,128)(2,1)S(1)}, u32[]{:S(2)}, u32[]{:S(2)}) %collective-permute-start.23) | collective-permute-done | bytes 262176 | tf_op jit(solution)/shard_map/ppermute | solution.py:523
  82.0 1.2 %unfold.2.refs_3_ = f32[4,1320,128]{2,1,0:T(8,128)S(1)} custom-call(bf16[8,32,512]{2,1,0:T(8,128)(2,1)S(1)} %get-tuple-element.67.refs_0_, bf16[8,32,512]{2,1,0:T(8,128)(2,1)S(1)} %collective-permute-done.19.refs_3_.refs_1_, bf16[8,32,512]{2,1,0:T(8,128)(2,1)S(1)} %get-tuple-element.68.refs_2_, bf16[8,32,512]{2,1,0:T(8,128)(2,1)S(1)} %collective-permute-done.23.refs_3_, ...), custom_call_target="tpu_custom_call" | custom-call | bytes 16 | tf_op jit(solution)/shard_map/unfold/pallas_call | solution.py:47
  83.1 4.1 %collective-permute-done.22.refs_1_ = bf16[8,32,512]{2,1,0:T(8,128)(2,1)S(1)} collective-permute-done((bf16[8,32,512]{2,1,0:T(8,128)(2,1)S(1)}, bf16[8,32,512]{2,1,0:T(8,128)(2,1)S(1)}, u32[]{:S(2)}, u32[]{:S(2)}) %collective-permute-start.22) | collective-permute-done | bytes 262176 | tf_op jit(solution)/shard_map/ppermute | solution.py:523
  87.2 1.6 %unfold.3 = (bf16[32,32,512]{2,1,0:T(8,128)(2,1)}, f32[4,1320,128]{2,1,0:T(8,128)S(1)}) custom-call(bf16[8,32,512]{2,1,0:T(8,128)(2,1)S(1)} %get-tuple-element.65.refs_0_, bf16[8,32,512]{2,1,0:T(8,128)(2,1)S(1)} %collective-permute-done.22.refs_1_, bf16[512,512]{1,0:T(8,128)(2,1)S(1)} %copy-done.4, ...), custom_call_target="tpu_custom_call", output_to_operand_aliasing={{1}: (3, {})} | custom-call | bytes 16 | tf_op jit(solution)/shard_map/unfold/pallas_call | solution.py:47
  (20 shorter events, 0.2 us)
Async XLA Ops:
  0.0 2.2 %copy-start = (bf16[16,128,1024]{2,1,0:T(8,128)(2,1)S(1)}, bf16[16,128,1024]{2,1,0:T(8,128)(2,1)}, u32[]{:S(2)}) copy-start(bf16[16,128,1024]{2,1,0:T(8,128)(2,1)} %refs_0_.4) | copy-start | bytes 12582916
  2.2 6.2 %copy-start.1 = (bf16[16,128,1024]{2,1,0:T(8,128)(2,1)S(1)}, bf16[16,128,1024]{2,1,0:T(8,128)(2,1)}, u32[]{:S(2)}) copy-start(bf16[16,128,1024]{2,1,0:T(8,128)(2,1)} %refs_0_.4) | copy-start | bytes 12582916
  2.2 11.0 %collective-permute-start = (bf16[16,1,1024]{2,1,0:T(2,128)(2,1)S(1)}, bf16[16,1,1024]{2,1,0:T(2,128)(2,1)S(1)}, u32[]{:S(2)}, u32[]{:S(2)}) collective-permute-start(bf16[16,1,1024]{2,1,0:T(2,128)(2,1)S(1)} %get-tuple-element.38), channel_id=1, source_target_pairs={{0,4},{4,8},{8,12},{12,16},{16,20},{20,24},{24,28},{28,0},{1,5},{5... | collective-permute-start | bytes 98312 | tf_op jit(solution)/shard_map/ppermute | solution.py:512
  5.2 8.1 %copy-start.5 = (s32[32]{0:T(128)S(1)}, s32[32]{0:T(128)}, u32[]{:S(2)}) copy-start(s32[32]{0:T(128)} %refs_0_.5) | copy-start | bytes 388
  5.2 8.1 %copy-start.6 = (s32[16]{0:T(128)S(1)}, s32[16]{0:T(128)}, u32[]{:S(2)}) copy-start(s32[16]{0:T(128)} %refs_1_.5) | copy-start | bytes 196
  5.2 8.1 %collective-permute-start.1 = (bf16[16,1,1024]{2,1,0:T(2,128)(2,1)S(1)}, bf16[16,1,1024]{2,1,0:T(2,128)(2,1)S(1)}, u32[]{:S(2)}, u32[]{:S(2)}) collective-permute-start(bf16[16,1,1024]{2,1,0:T(2,128)(2,1)S(1)} %get-tuple-element.39), channel_id=1, source_target_pairs={{4,0},{8,4},{12,8},{16,12},{20,16},{24,20},{28,24},{0,28},{5,1},{9... | collective-permute-start | bytes 98312 | tf_op jit(solution)/shard_map/ppermute | solution.py:513
  15.0 7.8 %collective-permute-start.2 = (bf16[8,16,1024]{2,1,0:T(8,128)(2,1)S(1)}, bf16[8,16,1024]{2,1,0:T(8,128)(2,1)S(1)}, u32[]{:S(2)}, u32[]{:S(2)}) collective-permute-start(bf16[8,16,1024]{2,1,0:T(8,128)(2,1)S(1)} %get-tuple-element.45), channel_id=1, source_target_pairs={{0,4},{4,0},{8,12},{12,8},{16,20},{20,16},{24,28},{28,24},{1,5},{5... | collective-permute-start | bytes 786440 | tf_op jit(solution)/shard_map/ppermute | solution.py:471
  23.6 14.2 %collective-permute-start.13 = (bf16[16,64,1024]{2,1,0:T(8,128)(2,1)S(1)}, bf16[16,64,1024]{2,1,0:T(8,128)(2,1)S(1)}, u32[]{:S(2)}, u32[]{:S(2)}) collective-permute-start(bf16[16,64,1024]{2,1,0:T(8,128)(2,1)S(1)} %get-tuple-element.61), channel_id=1, source_target_pairs={{0,1},{1,0},{2,3},{3,2},{4,5},{5,4},{6,7},{7,6},{8,9},{9,8},{10,11... | collective-permute-start | bytes 6291464 | tf_op jit(solution)/shard_map/ppermute | solution.py:520
  23.6 8.7 %collective-permute-start.6 = (bf16[8,16,1024]{2,1,0:T(8,128)(2,1)S(1)}, bf16[8,16,1024]{2,1,0:T(8,128)(2,1)S(1)}, u32[]{:S(2)}, u32[]{:S(2)}) collective-permute-start(bf16[8,16,1024]{2,1,0:T(8,128)(2,1)S(1)} %get-tuple-element.51), channel_id=1, source_target_pairs={{0,4},{4,0},{8,12},{12,8},{16,20},{20,16},{24,28},{28,24},{1,5},{5... | collective-permute-start | bytes 786440 | tf_op jit(solution)/shard_map/ppermute | solution.py:471
  24.0 8.4 %collective-permute-start.3 = (bf16[2,16,1024]{2,1,0:T(8,128)(2,1)S(1)}, bf16[2,16,1024]{2,1,0:T(8,128)(2,1)S(1)}, u32[]{:S(2)}, u32[]{:S(2)}) collective-permute-start(bf16[2,16,1024]{2,1,0:T(8,128)(2,1)S(1)} %get-tuple-element.47), channel_id=1, source_target_pairs={{0,8},{4,12},{8,0},{12,4},{16,24},{20,28},{24,16},{28,20},{1,9},{5... | collective-permute-start | bytes 196616 | tf_op jit(solution)/shard_map/ppermute | solution.py:475
  24.5 7.9 %collective-permute-start.4 = (bf16[2,16,1024]{2,1,0:T(8,128)(2,1)S(1)}, bf16[2,16,1024]{2,1,0:T(8,128)(2,1)S(1)}, u32[]{:S(2)}, u32[]{:S(2)}) collective-permute-start(bf16[2,16,1024]{2,1,0:T(8,128)(2,1)S(1)} %get-tuple-element.48), channel_id=1, source_target_pairs={{0,16},{4,20},{8,24},{12,28},{16,0},{20,4},{24,8},{28,12},{1,17},{... | collective-permute-start | bytes 196616 | tf_op jit(solution)/shard_map/ppermute | solution.py:475
  27.1 6.2 %collective-permute-start.5 = (bf16[2,16,1024]{2,1,0:T(8,128)(2,1)S(1)}, bf16[2,16,1024]{2,1,0:T(8,128)(2,1)S(1)}, u32[]{:S(2)}, u32[]{:S(2)}) collective-permute-start(bf16[2,16,1024]{2,1,0:T(8,128)(2,1)S(1)} %get-tuple-element.49), channel_id=1, source_target_pairs={{0,24},{4,28},{8,16},{12,20},{16,8},{20,12},{24,0},{28,4},{1,25},{... | collective-permute-start | bytes 196616 | tf_op jit(solution)/shard_map/ppermute | solution.py:475
  33.3 6.6 %collective-permute-start.7 = (bf16[4,16,1024]{2,1,0:T(8,128)(2,1)S(1)}, bf16[4,16,1024]{2,1,0:T(8,128)(2,1)S(1)}, u32[]{:S(2)}, u32[]{:S(2)}) collective-permute-start(bf16[4,16,1024]{2,1,0:T(8,128)(2,1)S(1)} %get-tuple-element.57.refs_0_), channel_id=1, source_target_pairs={{0,8},{4,12},{8,0},{12,4},{16,24},{20,28},{24,16},{28,20},{1,9},{5... | collective-permute-start | bytes 393224 | tf_op jit(solution)/shard_map/ppermute | solution.py:475
  34.5 11.7 %collective-permute-start.8 = (bf16[4,16,1024]{2,1,0:T(8,128)(2,1)S(1)}, bf16[4,16,1024]{2,1,0:T(8,128)(2,1)S(1)}, u32[]{:S(2)}, u32[]{:S(2)}) collective-permute-start(bf16[4,16,1024]{2,1,0:T(8,128)(2,1)S(1)} %get-tuple-element.58), channel_id=1, source_target_pairs={{0,16},{4,20},{8,24},{12,28},{16,0},{20,4},{24,8},{28,12},{1,17},{... | collective-permute-start | bytes 393224 | tf_op jit(solution)/shard_map/ppermute | solution.py:475
  35.9 10.2 %collective-permute-start.9 = (bf16[4,16,1024]{2,1,0:T(8,128)(2,1)S(1)}, bf16[4,16,1024]{2,1,0:T(8,128)(2,1)S(1)}, u32[]{:S(2)}, u32[]{:S(2)}) collective-permute-start(bf16[4,16,1024]{2,1,0:T(8,128)(2,1)S(1)} %get-tuple-element.59), channel_id=1, source_target_pairs={{0,24},{4,28},{8,16},{12,20},{16,8},{20,12},{24,0},{28,4},{1,25},{... | collective-permute-start | bytes 393224 | tf_op jit(solution)/shard_map/ppermute | solution.py:475
  46.2 6.2 %collective-permute-start.14 = (bf16[8,16,1024]{2,1,0:T(8,128)(2,1)S(1)}, bf16[8,16,1024]{2,1,0:T(8,128)(2,1)S(1)}, u32[]{:S(2)}, u32[]{:S(2)}) collective-permute-start(bf16[8,16,1024]{2,1,0:T(8,128)(2,1)S(1)} %gather.2.refs_0_.refs_3_), channel_id=1, source_target_pairs={{0,1},{1,0},{2,3},{3,2},{4,5},{5,4},{6,7},{7,6},{8,9},{9,8},{10,11... | collective-permute-start | bytes 786440 | tf_op jit(solution)/shard_map/ppermute | solution.py:520
  46.3 12.1 %collective-permute-start.15 = (bf16[8,16,1024]{2,1,0:T(8,128)(2,1)S(1)}, bf16[8,16,1024]{2,1,0:T(8,128)(2,1)S(1)}, u32[]{:S(2)}, u32[]{:S(2)}) collective-permute-start(bf16[8,16,1024]{2,1,0:T(8,128)(2,1)S(1)} %gather.2.refs_0_.refs_3_), channel_id=1, source_target_pairs={{0,4},{4,0},{8,12},{12,8},{16,20},{20,16},{24,28},{28,24},{1,5},{5... | collective-permute-start | bytes 786440 | tf_op jit(solution)/shard_map/ppermute | solution.py:479
  47.1 10.6 %copy-start.2 = (bf16[272,512]{1,0:T(8,128)(2,1)S(1)}, bf16[272,512]{1,0:T(8,128)(2,1)}, u32[]{:S(2)}) copy-start(bf16[272,512]{1,0:T(8,128)(2,1)} %constant.6.clone.refs_1_) | copy-start | bytes 835588
  47.1 10.6 %copy-start.3 = (bf16[256,512]{1,0:T(8,128)(2,1)S(1)}, bf16[256,512]{1,0:T(8,128)(2,1)}, u32[]{:S(2)}) copy-start(bf16[256,512]{1,0:T(8,128)(2,1)} %constant.7.clone.refs_2_) | copy-start | bytes 786436
  47.1 8.3 %collective-permute-start.10 = (bf16[2,16,1024]{2,1,0:T(8,128)(2,1)S(1)}, bf16[2,16,1024]{2,1,0:T(8,128)(2,1)S(1)}, u32[]{:S(2)}, u32[]{:S(2)}) collective-permute-start(bf16[2,16,1024]{2,1,0:T(8,128)(2,1)S(1)} %part.1.refs_0_.refs_7_), channel_id=1, source_target_pairs={{0,8},{4,12},{8,0},{12,4},{16,24},{20,28},{24,16},{28,20},{1,9},{5... | collective-permute-start | bytes 196616 | tf_op jit(solution)/shard_map/ppermute | solution.py:475
  49.9 7.8 %collective-permute-start.11 = (bf16[2,16,1024]{2,1,0:T(8,128)(2,1)S(1)}, bf16[2,16,1024]{2,1,0:T(8,128)(2,1)S(1)}, u32[]{:S(2)}, u32[]{:S(2)}) collective-permute-start(bf16[2,16,1024]{2,1,0:T(8,128)(2,1)S(1)} %part.1.refs_0_.refs_7_), channel_id=1, source_target_pairs={{0,16},{4,20},{8,24},{12,28},{16,0},{20,4},{24,8},{28,12},{1,17},{... | collective-permute-start | bytes 196616 | tf_op jit(solution)/shard_map/ppermute | solution.py:475
  50.0 8.4 %collective-permute-start.12 = (bf16[2,16,1024]{2,1,0:T(8,128)(2,1)S(1)}, bf16[2,16,1024]{2,1,0:T(8,128)(2,1)S(1)}, u32[]{:S(2)}, u32[]{:S(2)}) collective-permute-start(bf16[2,16,1024]{2,1,0:T(8,128)(2,1)S(1)} %part.1.refs_0_.refs_7_), channel_id=1, source_target_pairs={{0,24},{4,28},{8,16},{12,20},{16,8},{20,12},{24,0},{28,4},{1,25},{... | collective-permute-start | bytes 196616 | tf_op jit(solution)/shard_map/ppermute | solution.py:475
  58.4 2.9 %collective-permute-start.20 = (bf16[8,16,1024]{2,1,0:T(8,128)(2,1)S(1)}, bf16[8,16,1024]{2,1,0:T(8,128)(2,1)S(1)}, u32[]{:S(2)}, u32[]{:S(2)}) collective-permute-start(bf16[8,16,1024]{2,1,0:T(8,128)(2,1)S(1)} %gather.3.refs_4_.refs_0_), channel_id=1, source_target_pairs={{0,1},{1,0},{2,3},{3,2},{4,5},{5,4},{6,7},{7,6},{8,9},{9,8},{10,11... | collective-permute-start | bytes 786440 | tf_op jit(solution)/shard_map/ppermute | solution.py:520
  58.5 8.7 %collective-permute-start.16 = (bf16[8,16,1024]{2,1,0:T(8,128)(2,1)S(1)}, bf16[8,16,1024]{2,1,0:T(8,128)(2,1)S(1)}, u32[]{:S(2)}, u32[]{:S(2)}) collective-permute-start(bf16[8,16,1024]{2,1,0:T(8,128)(2,1)S(1)} %gather.3.refs_4_.refs_0_), channel_id=1, source_target_pairs={{0,4},{4,0},{8,12},{12,8},{16,20},{20,16},{24,28},{28,24},{1,5},{5... | collective-permute-start | bytes 786440 | tf_op jit(solution)/shard_map/ppermute | solution.py:479
  59.6 9.1 %collective-permute-start.18 = (bf16[8,16,1024]{2,1,0:T(8,128)(2,1)S(1)}, bf16[8,16,1024]{2,1,0:T(8,128)(2,1)S(1)}, u32[]{:S(2)}, u32[]{:S(2)}) collective-permute-start(bf16[8,16,1024]{2,1,0:T(8,128)(2,1)S(1)} %collective-permute-done.15.refs_8_.refs_0_), channel_id=1, source_target_pairs={{0,1},{1,0},{2,3},{3,2},{4,5},{5,4},{6,7},{7,6},{8,9},{9,8},{10,11... | collective-permute-start | bytes 786440 | tf_op jit(solution)/shard_map/ppermute | solution.py:520
  59.8 12.2 %collective-permute-start.19 = (bf16[8,32,512]{2,1,0:T(8,128)(2,1)S(1)}, bf16[8,32,512]{2,1,0:T(8,128)(2,1)S(1)}, u32[]{:S(2)}, u32[]{:S(2)}) collective-permute-start(bf16[8,32,512]{2,1,0:T(8,128)(2,1)S(1)} %get-tuple-element.62.refs_4_.refs_3_), channel_id=1, source_target_pairs={{0,2},{1,3},{2,0},{3,1},{4,6},{5,7},{6,4},{7,5},{8,10},{9,11},{10,... | collective-permute-start | bytes 786440 | tf_op jit(solution)/shard_map/ppermute | solution.py:523
  67.2 6.0 %collective-permute-start.17 = (bf16[8,16,1024]{2,1,0:T(8,128)(2,1)S(1)}, bf16[8,16,1024]{2,1,0:T(8,128)(2,1)S(1)}, u32[]{:S(2)}, u32[]{:S(2)}) collective-permute-start(bf16[8,16,1024]{2,1,0:T(8,128)(2,1)S(1)} %collective-permute-done.16.refs_6_.refs_0_.refs_7_.refs_10_), channel_id=1, source_target_pairs={{0,1},{1,0},{2,3},{3,2},{4,5},{5,4},{6,7},{7,6},{8,9},{9,8},{10,11... | collective-permute-start | bytes 786440 | tf_op jit(solution)/shard_map/ppermute | solution.py:520
  67.2 9.1 %collective-permute-start.21 = (bf16[8,32,512]{2,1,0:T(8,128)(2,1)S(1)}, bf16[8,32,512]{2,1,0:T(8,128)(2,1)S(1)}, u32[]{:S(2)}, u32[]{:S(2)}) collective-permute-start(bf16[8,32,512]{2,1,0:T(8,128)(2,1)S(1)} %get-tuple-element.64.refs_8_), channel_id=1, source_target_pairs={{0,2},{1,3},{2,0},{3,1},{4,6},{5,7},{6,4},{7,5},{8,10},{9,11},{10,... | collective-permute-start | bytes 786440 | tf_op jit(solution)/shard_map/ppermute | solution.py:523
  72.6 9.3 %collective-permute-start.23 = (bf16[8,32,512]{2,1,0:T(8,128)(2,1)S(1)}, bf16[8,32,512]{2,1,0:T(8,128)(2,1)S(1)}, u32[]{:S(2)}, u32[]{:S(2)}) collective-permute-start(bf16[8,32,512]{2,1,0:T(8,128)(2,1)S(1)} %get-tuple-element.63.refs_4_.refs_7_), channel_id=1, source_target_pairs={{0,2},{1,3},{2,0},{3,1},{4,6},{5,7},{6,4},{7,5},{8,10},{9,11},{10,... | collective-permute-start | bytes 786440 | tf_op jit(solution)/shard_map/ppermute | solution.py:523
  76.2 5.7 %copy-start.4 = (bf16[512,512]{1,0:T(8,128)(2,1)S(1)}, bf16[512,512]{1,0:T(8,128)(2,1)}, u32[]{:S(2)}) copy-start(bf16[512,512]{1,0:T(8,128)(2,1)} %constant.8.clone.refs_6_.refs_2_) | copy-start | bytes 1572868
  77.0 10.2 %collective-permute-start.22 = (bf16[8,32,512]{2,1,0:T(8,128)(2,1)S(1)}, bf16[8,32,512]{2,1,0:T(8,128)(2,1)S(1)}, u32[]{:S(2)}, u32[]{:S(2)}) collective-permute-start(bf16[8,32,512]{2,1,0:T(8,128)(2,1)S(1)} %get-tuple-element.66), channel_id=1, source_target_pairs={{0,2},{1,3},{2,0},{3,1},{4,6},{5,7},{6,4},{7,5},{8,10},{9,11},{10,... | collective-permute-start | bytes 786440 | tf_op jit(solution)/shard_map/ppermute | solution.py:523
